TPU v7x, 256 devices: a whole 4x4x8 slice. The times are simulated.
256 devices in a mesh: rows: 64 (over z, y, core), cols: 4 (over x).
Axes of the slice: x: 4, y: 4, z: 8, core: 2. Of those that a mesh axis runs over, the one named last changes fastest.
Arguments:
- tile_blocks: bfloat16 [2048, 8, 256, 256], P(('rows', 'cols')), may hold values from 0.049804688 to 1
- tile_cols: int32 [2048, 8], P(('rows', 'cols')), may hold values from 0 to 2047, as said below
- tile_count: int32 [2048], P(('rows', 'cols')), may hold values from 1 to 8
- start_mass: float32 [524288], P(('rows', 'cols')), may hold values from 0.5 to 64
- probe_block: bfloat16 [32, 524288], P(None, ('rows', 'cols')), may hold values from -6 to 6
Outputs:
- basis: float32 [32, 524288], P(None, ('rows', 'cols'))
Inputs may be any that keep to these rules, and one draw needn't show every extreme that they name: `tile_cols`: slot 0 names the block row itself; every other slot names a block within 8 blocks of its row, cyclically over 2048.
All inputs are finite; a program needn't handle non-finite values.
Results may differ from a plain program's by a relative error of at most 0.00035.
The roundings to bfloat16 on the way count: a program that leaves them out, or rounds other values in their place, can miss the bound.
Values may be sent and summed in bfloat16 or wider, within the bound.
No kernel may reach another device: no remote copies, remote signals or barrier semaphores. Data moves between devices by JAX's collectives and lax.ppermute only.
A program may use at most 64 MiB of HBM per device.

v0:
```python
import functools
import math

import jax
import jax.numpy as jnp
from jax import lax
from jax.experimental import pallas as pl
from jax.experimental.pallas import tpu as pltpu
from jax.sharding import PartitionSpec as P

RING = ("rows", "cols")
F32 = jnp.float32
BF16 = jnp.bfloat16
HIGHEST = lax.Precision.HIGHEST
LAST_DIMS = (((1,), (1,)), ((), ()))
SMEM = pl.BlockSpec(memory_space=pltpu.SMEM)
VMEM = pl.BlockSpec(memory_space=pltpu.VMEM)
ANY = pl.BlockSpec(memory_space=pl.ANY)


def swap(shard, axis, partner):
    count = lax.axis_size(axis)
    return lax.ppermute(shard, axis, [(i, partner(i) % count) for i in range(count)])


def ring_pairs(shard_odd, shard_even):
    got_odd = swap(shard_odd, RING, lambda i: i + 1 if i % 2 else i - 1)
    got_even = swap(shard_even, RING, lambda i: i - 1 if i % 2 else i + 1)
    return got_odd, got_even


def all_sum(part):
    part = part + swap(part, "rows", lambda i: i ^ 1)
    part = part + sum(swap(part, "cols", lambda i, d=d: i ^ d) for d in (2, 1, 3))
    part = part + sum(swap(part, "rows", lambda i, d=d: i ^ d) for d in (4, 2, 6))
    part = part + swap(part, "rows", lambda i: i ^ 8)
    return part + sum(
        swap(part, "rows", lambda i, d=d: i + 8 * d if (i // 8) % 2 else i - 8 * d) for d in (3, 2, 1)
    )


def push(target_ref, tiles_ref, parts, window, outs):
    blocks, slots = tiles_ref.shape[:2]
    height = parts[0].shape[0]
    window[...] = jnp.zeros_like(window)
    rows = jnp.concatenate(parts, axis=0) if len(parts) > 1 else parts[0]
    owner = lax.broadcasted_iota(jnp.int32, rows.shape, 0) % blocks
    for block in range(blocks):
        left = jnp.where(owner == block, rows, 0.0).astype(BF16)
        for slot in range(slots):
            product = jnp.dot(left, tiles_ref[block, slot], preferred_element_type=F32)
            if len(parts) > 1:
                product = product[:height] + product[height:]
            window[target_ref[block * slots + slot]] += product
    for channel in range(height // blocks):
        rows = slice(channel * blocks, (channel + 1) * blocks)
        landed = jnp.sum(window[0 : 3 * blocks, rows, :], axis=1)
        for part, out in zip((0, 1, 2), outs):
            out[rows, :] = landed[part * blocks : (part + 1) * blocks]


def two_parts(value):
    high = value.astype(BF16).astype(F32)
    return high, value - high


def load_kernel(target_ref, count_ref, tiles_hbm, start_ref, tiles_ref, inverse_ref, odd_ref, own_ref, even_ref, window, sems):
    blocks, slots, width = tiles_ref.shape[:3]
    copies = [pltpu.make_async_copy(tiles_hbm.at[b], tiles_ref.at[b], sems.at[b]) for b in range(blocks)]
    for copy in copies:
        copy.start()
    ones = jnp.ones((8, width), BF16)
    sums = []
    for block in range(blocks):
        copies[block].wait()
        total = jnp.zeros((8, width), F32)
        for slot in range(slots):
            part = lax.dot_general(ones, tiles_ref[block, slot], LAST_DIMS, preferred_element_type=F32)
            total = total + jnp.where(slot < count_ref[block], part, 0.0)
        sums.append(total[0:1])
    inverse = 1.0 / jnp.concatenate(sums, axis=0)
    inverse_ref[...] = inverse
    push(target_ref, tiles_ref, (start_ref[...] * inverse,), window, (odd_ref, own_ref, even_ref))


def second_kernel(target_ref, tiles_ref, inverse_ref, odd, own, even, to_odd, kept, to_even, value_ref, window):
    raw = 0.85 * (own[...] + odd[...] + even[...]) + 0.15
    value_ref[...] = raw
    inverse = inverse_ref[...]
    rows = jnp.concatenate([raw * inverse, inverse], axis=0)
    push(target_ref, tiles_ref, two_parts(rows), window, (to_odd, kept, to_even))


def chain_kernel(channels, target_ref, tiles_ref, inverse_ref, odd, own, even, to_odd, kept, to_even, value_ref, window):
    value = own[...] + odd[...] + even[...]
    value_ref[...] = value
    inverse = inverse_ref[...]
    rows = jnp.concatenate([value[8 * c : 8 * c + 8] * inverse for c in range(channels)], axis=0)
    push(target_ref, tiles_ref, two_parts(rows), window, (to_odd, kept, to_even))


def sums_kernel(raw_ref, second_ref, third_ref, odd, own, even, out_ref):
    raw = raw_ref[...]
    second = second_ref[0:8]
    ones_1 = second_ref[8:16]
    third = third_ref[0:8]
    ones_2 = third_ref[8:16]
    fourth = own[...] + odd[...] + even[...]
    wanted = (
        raw * raw,
        second * second, second,
        third * third, third * ones_1, third, ones_1 * ones_1, ones_1,
        fourth * fourth, fourth * ones_2, fourth * ones_1, fourth,
        ones_2 * ones_2, ones_2 * ones_1, ones_2, jnp.zeros_like(raw),
    )
    lines = [jnp.sum(term[:, :128] + term[:, 128:], axis=0, keepdims=True) for term in wanted]
    out_ref[...] = jnp.concatenate(lines, axis=0)


def scales_of(sums, zones):
    totals = jnp.sum(sums, axis=1, keepdims=True)
    (r11, c22, c2o, c33, c3p, c3o, pp, po, c44, c4q, c4p, c4o, qq, qp, qo) = (totals[i : i + 1] for i in range(15))
    root = math.sqrt(zones)
    floor = 0.15 * 0.15 * zones
    scale_1 = root / jnp.sqrt(r11)
    a2 = 0.85 * scale_1
    scale_2 = root / jnp.sqrt(a2 * a2 * c22 + 0.3 * a2 * c2o + floor)
    a3 = 0.85 * scale_2 * a2
    p3 = 0.85 * scale_2 * 0.15
    scale_3 = root / jnp.sqrt(
        a3 * a3 * c33 + 2.0 * a3 * (p3 * c3p + 0.15 * c3o) + p3 * p3 * pp + 0.3 * p3 * po + floor
    )
    a4 = 0.85 * scale_3 * a3
    q4 = 0.85 * scale_3 * p3
    p4 = 0.85 * scale_3 * 0.15
    scale_4 = root / jnp.sqrt(
        a4 * a4 * c44 + 2.0 * a4 * (q4 * c4q + p4 * c4p + 0.15 * c4o)
        + q4 * q4 * qq + p4 * p4 * pp + 2.0 * q4 * (p4 * qp + 0.15 * qo) + 0.3 * p4 * po + floor
    )
    return scale_1, scale_2, scale_3, scale_4


def replay_kernel(zones, target_ref, tiles_ref, inverse_ref, sums_ref, raw_ref, to_odd, kept, to_even, scales_ref, window):
    scales = scales_of(sums_ref[...], zones)
    for place, scale in enumerate(scales):
        scales_ref[place : place + 1, :] = jnp.broadcast_to(scale, (1, 128))
    rows = (raw_ref[...] * scales[0]) * inverse_ref[...]
    push(target_ref, tiles_ref, (rows,), window, (to_odd, kept, to_even))


def again_kernel(place, target_ref, tiles_ref, inverse_ref, scales_ref, odd, own, even, to_odd, kept, to_even, window):
    raw = 0.85 * (own[...] + odd[...] + even[...]) + 0.15
    rows = (raw * scales_ref[place : place + 1, 0:1]) * inverse_ref[...]
    push(target_ref, tiles_ref, (rows,), window, (to_odd, kept, to_even))


def transposed_kernel(target_ref, tiles_ref, inverse_ref, scales_ref, odd, own, even, probe_ref, to_odd, kept, to_even, root_ref, window):
    blocks, slots, width = tiles_ref.shape[:3]
    raw = 0.85 * (own[...] + odd[...] + even[...]) + 0.15
    root = jnp.sqrt(raw * scales_ref[3:4, 0:1])
    root_ref[...] = root
    gain = root * inverse_ref[...]
    window[...] = jnp.zeros_like(window)
    for block in range(blocks):
        probe = probe_ref[:, block * width : (block + 1) * width].astype(F32)
        left = (probe * gain[block : block + 1]).astype(BF16)
        for slot in range(slots):
            product = jnp.dot(left, tiles_ref[block, slot], preferred_element_type=F32)
            window[target_ref[block * slots + slot]] += product
    to_odd[...] = window[0:blocks]
    kept[...] = window[blocks : 2 * blocks]
    to_even[...] = window[2 * blocks : 3 * blocks]


def forward_kernel(target_ref, tiles_ref, inverse_ref, root_odd, root_own, root_even, probe_odd, probe_own, probe_even, out_ref, window):
    blocks, slots, width = tiles_ref.shape[:3]
    for part, (root_ref, probe_ref) in enumerate(((root_odd, probe_odd), (root_own, probe_own), (root_even, probe_even))):
        inverse_root = 1.0 / root_ref[...]
        for block in range(blocks):
            probe = probe_ref[:, block * width : (block + 1) * width].astype(F32)
            window[part * blocks + block] = (probe * inverse_root[block : block + 1]).astype(BF16)
    window[3 * blocks] = jnp.zeros(window.shape[1:], BF16)
    gain = root_own[...] * inverse_ref[...]
    for block in range(blocks):
        total = jnp.zeros(window.shape[1:], F32)
        for slot in range(slots):
            left = window[target_ref[block * slots + slot]]
            total += lax.dot_general(left, tiles_ref[block, slot], LAST_DIMS, preferred_element_type=F32)
        out_ref[block] = total * gain[block : block + 1]


def embed_kernel(forward_ref, odd, own, even, root_ref, out_ref, gram_ref):
    blocks, chans, width = forward_ref.shape
    inverse_root = 1.0 / root_ref[...]
    gram = jnp.zeros((chans, chans), F32)
    for block in range(blocks):
        landed = own[block] + odd[block] + even[block]
        embedded = 0.5 * (forward_ref[block] + landed * inverse_root[block : block + 1])
        out_ref[:, block * width : (block + 1) * width] = embedded
        gram += lax.dot_general(embedded, embedded, LAST_DIMS, precision=HIGHEST, preferred_element_type=F32)
    gram_ref[...] = gram


def basis_kernel(gram_ref, embedded_ref, out_ref):
    size = gram_ref.shape[0]
    row = lax.broadcasted_iota(jnp.int32, (size, size), 0)
    col = lax.broadcasted_iota(jnp.int32, (size, size), 1)
    identity = jnp.where(row == col, 1.0, 0.0)
    work = jnp.concatenate([gram_ref[...], identity], axis=1)
    line = lax.broadcasted_iota(jnp.int32, (size, 1), 0)
    for step in range(size):
        pivot_row = work[step : step + 1, :]
        factor = work[:, step : step + 1] * (1.0 / pivot_row[:, step : step + 1])
        work = work - jnp.where(line > step, factor, 0.0) * pivot_row
    pivots = jnp.sum(work[:, :size] * identity, axis=1, keepdims=True)
    inverse = work[:, size:] * (1.0 / jnp.sqrt(pivots))
    out_ref[...] = jnp.dot(inverse, embedded_ref[...], precision=HIGHEST, preferred_element_type=F32)


def call(kernel, name, outs, operands, specs, scratch, limit=24):
    return pl.pallas_call(
        kernel,
        out_shape=outs,
        in_specs=specs,
        out_specs=[VMEM] * len(outs),
        scratch_shapes=scratch,
        compiler_params=pltpu.CompilerParams(vmem_limit_bytes=limit << 20),
        name=name,
    )(*operands)


def per_device(tile_blocks, tile_cols, tile_count, start_mass, probe_block):
    blocks, slots, width = tile_blocks.shape[:3]
    chans = probe_block.shape[0]
    total_blocks = blocks * lax.axis_size(RING)
    zones = total_blocks * width
    place = lax.axis_index(RING)
    live = jnp.arange(slots)[None, :] < tile_count[:, None]
    place_in_window = (tile_cols - place * blocks + blocks) % total_blocks
    before = place_in_window < blocks
    after = place_in_window >= 2 * blocks
    flipped = jnp.where(before, place_in_window + 2 * blocks, jnp.where(after, place_in_window - 2 * blocks, place_in_window))
    target = jnp.where(place % 2 == 1, flipped, place_in_window)
    target = jnp.where(live, target, 3 * blocks).reshape(-1).astype(jnp.int32)

    def rows(channels=1):
        return jax.ShapeDtypeStruct((channels * blocks, width), F32)

    def window(channels, kind=F32):
        return pltpu.VMEM((3 * blocks + 1, channels, width), kind)

    tiles, inverse, to_odd, own, to_even = call(
        load_kernel, "load",
        [pltpu.VMEM(tile_blocks.shape, BF16), rows(), rows(), rows(), rows()],
        (target, tile_count, tile_blocks, start_mass.reshape(blocks, width)),
        [SMEM, SMEM, ANY, VMEM],
        [window(blocks), pltpu.SemaphoreType.DMA((blocks,))],
    )
    tiles = pltpu.with_memory_space_constraint(tiles, pltpu.VMEM)
    odd, even = ring_pairs(to_odd, to_even)

    def step(kernel, name, channels_out, operands, extra, scratch=None):
        specs = [SMEM] + [VMEM] * (2 + len(operands))
        outs = [rows(channels_out)] * 3 + extra
        scratch = [window(channels_out * blocks)] if scratch is None else scratch
        return call(kernel, name, outs, (target, tiles, inverse, *operands), specs, scratch)

    to_odd, own, to_even, raw = step(second_kernel, "second", 2, (odd, own, even), [rows()])
    odd, even = ring_pairs(to_odd, to_even)
    to_odd, own, to_even, second = step(functools.partial(chain_kernel, 2), "third", 2, (odd, own, even), [rows(2)])
    odd, even = ring_pairs(to_odd, to_even)
    to_odd, own, to_even, third = step(functools.partial(chain_kernel, 1), "fourth", 1, (odd, own, even), [rows(2)])
    odd, even = ring_pairs(to_odd, to_even)
    (sums,) = call(
        sums_kernel, "sums", [jax.ShapeDtypeStruct((16, 128), F32)], (raw, second, third, odd, own, even), [VMEM] * 6, []
    )
    sums = all_sum(sums)
    to_odd, own, to_even, scales = step(
        functools.partial(replay_kernel, zones), "replay_2", 1, (sums, raw), [jax.ShapeDtypeStruct((8, 128), F32)]
    )
    odd, even = ring_pairs(to_odd, to_even)
    to_odd, own, to_even = step(functools.partial(again_kernel, 1), "replay_3", 1, (scales, odd, own, even), [])
    odd, even = ring_pairs(to_odd, to_even)
    to_odd, own, to_even = step(functools.partial(again_kernel, 2), "replay_4", 1, (scales, odd, own, even), [])
    odd, even = ring_pairs(to_odd, to_even)

    wide = jax.ShapeDtypeStruct((blocks, chans, width), F32)
    probe_odd, probe_even = ring_pairs(probe_block, probe_block)
    to_odd, own, to_even, root = call(
        transposed_kernel, "transposed", [wide, wide, wide, rows()],
        (target, tiles, inverse, scales, odd, own, even, probe_block),
        [SMEM] + [VMEM] * 7, [window(chans)],
    )
    root_odd, root_even = ring_pairs(root, root)
    odd, even = ring_pairs(to_odd, to_even)
    (forward,) = call(
        forward_kernel, "forward", [wide],
        (target, tiles, inverse, root_odd, root, root_even, probe_odd, probe_block, probe_even),
        [SMEM] + [VMEM] * 8, [window(chans, BF16)],
    )
    embedded, gram = call(
        embed_kernel, "embed",
        [jax.ShapeDtypeStruct((chans, blocks * width), F32), jax.ShapeDtypeStruct((chans, chans), F32)],
        (forward, odd, own, even, root), [VMEM] * 5, [],
    )
    gram = all_sum(gram)
    (basis,) = call(
        basis_kernel, "basis", [jax.ShapeDtypeStruct((chans, blocks * width), F32)], (gram, embedded), [VMEM] * 2, []
    )
    return basis


def solution(mesh):
    return jax.shard_map(
        per_device,
        mesh=mesh,
        in_specs=(P(RING, None, None, None), P(RING, None), P(RING), P(RING), P(None, RING)),
        out_specs=P(None, RING),
        check_vma=False,
    )
```

profile of v0, /device:TPU:2, one launch (start us, length us, event | category | flops | bytes accessed | tf_op | source)
XLA Modules:
  0.0 172.8 jit_solution(6036899600059380128)
XLA Ops:
  1.5 3.4 %copy-done = bf16[8,8,256,256]{3,2,1,0:T(8,128)(2,1)S(1)} copy-done((bf16[8,8,256,256]{3,2,1,0:T(8,128)(2,1)S(1)}, bf16[8,8,256,256]{3,2,1,0:T(8,128)(2,1)}, u32[]{:S(2)}) %copy-start) | copy-done | bytes 8388632
  5.6 5.5 %load.1 = (bf16[8,8,256,256]{3,2,1,0:T(8,128)(2,1)S(1)}, f32[8,256]{1,0:T(8,128)S(1)}, f32[8,256]{1,0:T(8,128)S(1)}, f32[8,256]{1,0:T(8,128)S(1)}, f32[8,256]{1,0:T(8,128)S(1)}) custom-call(s32[64]{0:T(128)S(1)} %reshape.7.target_ref, s32[8]{0:T(128)S(1)} %copy-done.2, bf16[8,8,256,256]{3,2,1,0:T(8,128)(2,1)S(1)} %copy-done, f32[8,256]{1,0:T(8,128)S(1)} %reshape.8.start_ref), custom_call_target="tpu_custom_call" | custom-call | tf_op jit(solution)/shard_map/load/pallas_call | solution.py:221
  12.7 9.0 %collective-permute-start.1 = (f32[8,256]{1,0:T(8,128)S(1)}, f32[8,256]{1,0:T(8,128)S(1)}, u32[]{:S(2)}, u32[]{:S(2)}) collective-permute-start(f32[8,256]{1,0:T(8,128)S(1)} %get-tuple-element.42), channel_id=1, source_target_pairs={{0,1},{1,0},{2,3},{3,2},{4,5},{5,4},{6,7},{7,6},{8,9},{9,8},{10,11... | collective-permute-start | bytes 24584 | tf_op jit(solution)/shard_map/ppermute | solution.py:23
  23.3 2.2 %second.1 = (f32[16,256]{1,0:T(8,128)S(1)}, f32[16,256]{1,0:T(8,128)S(1)}, f32[16,256]{1,0:T(8,128)S(1)}, f32[8,256]{1,0:T(8,128)S(1)}) custom-call(s32[64]{0:T(128)S(1)} %reshape.7.target_ref, bf16[8,8,256,256]{3,2,1,0:T(8,128)(2,1)S(1)} %get-tuple-element.38.tiles_ref, f32[8,256]{1,0:T(8,128)S(1)} %get-tuple-element.39.inverse_ref, ...), custom_call_target="tpu_custom_call" | custom-call | tf_op jit(solution)/shard_map/second/pallas_call | solution.py:221
  25.6 6.9 %collective-permute-start.3 = (f32[16,256]{1,0:T(8,128)S(1)}, f32[16,256]{1,0:T(8,128)S(1)}, u32[]{:S(2)}, u32[]{:S(2)}) collective-permute-start(f32[16,256]{1,0:T(8,128)S(1)} %get-tuple-element.46), channel_id=1, source_target_pairs={{0,1},{1,0},{2,3},{3,2},{4,5},{5,4},{6,7},{7,6},{8,9},{9,8},{10,11... | collective-permute-start | bytes 49160 | tf_op jit(solution)/shard_map/ppermute | solution.py:23
  34.2 2.2 %third.1 = (f32[16,256]{1,0:T(8,128)S(1)}, f32[16,256]{1,0:T(8,128)S(1)}, f32[16,256]{1,0:T(8,128)S(1)}, f32[16,256]{1,0:T(8,128)S(1)}) custom-call(s32[64]{0:T(128)S(1)} %reshape.7.target_ref, bf16[8,8,256,256]{3,2,1,0:T(8,128)(2,1)S(1)} %get-tuple-element.38.tiles_ref, f32[8,256]{1,0:T(8,128)S(1)} %get-tuple-element.39.inverse_ref, ...), custom_call_target="tpu_custom_call" | custom-call | tf_op jit(solution)/shard_map/third/pallas_call | solution.py:221
  36.5 6.9 %collective-permute-start.5 = (f32[16,256]{1,0:T(8,128)S(1)}, f32[16,256]{1,0:T(8,128)S(1)}, u32[]{:S(2)}, u32[]{:S(2)}) collective-permute-start(f32[16,256]{1,0:T(8,128)S(1)} %get-tuple-element.50), channel_id=1, source_target_pairs={{0,1},{1,0},{2,3},{3,2},{4,5},{5,4},{6,7},{7,6},{8,9},{9,8},{10,11... | collective-permute-start | bytes 49160 | tf_op jit(solution)/shard_map/ppermute | solution.py:23
  47.0 6.9 %collective-permute-start.7 = (f32[8,256]{1,0:T(8,128)S(1)}, f32[8,256]{1,0:T(8,128)S(1)}, u32[]{:S(2)}, u32[]{:S(2)}) collective-permute-start(f32[8,256]{1,0:T(8,128)S(1)} %get-tuple-element.54), channel_id=1, source_target_pairs={{0,1},{1,0},{2,3},{3,2},{4,5},{5,4},{6,7},{7,6},{8,9},{9,8},{10,11... | collective-permute-start | bytes 24584 | tf_op jit(solution)/shard_map/ppermute | solution.py:23
  58.8 2.1 %collective-permute-start.9 = (f32[16,128]{1,0:T(8,128)S(1)}, f32[16,128]{1,0:T(8,128)S(1)}, u32[]{:S(2)}, u32[]{:S(2)}) collective-permute-start(f32[16,128]{1,0:T(8,128)S(1)} %add.91), channel_id=1, source_target_pairs={{0,2},{1,3},{2,0},{3,1},{4,6},{5,7},{6,4},{7,5},{8,10},{9,11},{10,... | collective-permute-start | bytes 24584 | tf_op jit(solution)/shard_map/ppermute | solution.py:23
  60.9 3.1 %collective-permute-done.9 = f32[16,128]{1,0:T(8,128)S(1)} collective-permute-done((f32[16,128]{1,0:T(8,128)S(1)}, f32[16,128]{1,0:T(8,128)S(1)}, u32[]{:S(2)}, u32[]{:S(2)}) %collective-permute-start.9) | collective-permute-done | bytes 8224 | tf_op jit(solution)/shard_map/ppermute | solution.py:23
  64.1 4.6 %collective-permute-start.12 = (f32[16,128]{1,0:T(8,128)S(1)}, f32[16,128]{1,0:T(8,128)S(1)}, u32[]{:S(2)}, u32[]{:S(2)}) collective-permute-start(f32[16,128]{1,0:T(8,128)S(1)} %add_add_fusion.5), channel_id=1, source_target_pairs={{0,16},{4,20},{8,24},{12,28},{16,0},{20,4},{24,8},{28,12},{32,48},... | collective-permute-start | bytes 24584 | tf_op jit(solution)/shard_map/ppermute | solution.py:23
  70.4 3.6 %collective-permute-done.15 = f32[16,128]{1,0:T(8,128)S(1)} collective-permute-done((f32[16,128]{1,0:T(8,128)S(1)}, f32[16,128]{1,0:T(8,128)S(1)}, u32[]{:S(2)}, u32[]{:S(2)}) %collective-permute-start.15) | collective-permute-done | bytes 8224 | tf_op jit(solution)/shard_map/ppermute | solution.py:23
  74.1 4.8 %collective-permute-start.18 = (f32[16,128]{1,0:T(8,128)S(1)}, f32[16,128]{1,0:T(8,128)S(1)}, u32[]{:S(2)}, u32[]{:S(2)}) collective-permute-start(f32[16,128]{1,0:T(8,128)S(1)} %add.98), channel_id=1, source_target_pairs={{0,224},{4,228},{8,232},{12,236},{16,240},{20,244},{24,248},{28,25... | collective-permute-start | bytes 24584 | tf_op jit(solution)/shard_map/ppermute | solution.py:23
  78.9 2.4 %collective-permute-start.16 = (f32[16,128]{1,0:T(8,128)S(1)}, f32[16,128]{1,0:T(8,128)S(1)}, u32[]{:S(2)}, u32[]{:S(2)}) collective-permute-start(f32[16,128]{1,0:T(8,128)S(1)} %add.98), channel_id=1, source_target_pairs={{0,160},{4,164},{8,168},{12,172},{16,176},{20,180},{24,184},{28,18... | collective-permute-start | bytes 24584 | tf_op jit(solution)/shard_map/ppermute | solution.py:23
  81.2 2.2 %collective-permute-done.17 = f32[16,128]{1,0:T(8,128)S(1)} collective-permute-done((f32[16,128]{1,0:T(8,128)S(1)}, f32[16,128]{1,0:T(8,128)S(1)}, u32[]{:S(2)}, u32[]{:S(2)}) %collective-permute-start.17) | collective-permute-done | bytes 8224 | tf_op jit(solution)/shard_map/ppermute | solution.py:23
  83.4 2.1 %collective-permute-done.16 = f32[16,128]{1,0:T(8,128)S(1)} collective-permute-done((f32[16,128]{1,0:T(8,128)S(1)}, f32[16,128]{1,0:T(8,128)S(1)}, u32[]{:S(2)}, u32[]{:S(2)}) %collective-permute-start.16) | collective-permute-done | bytes 8224 | tf_op jit(solution)/shard_map/ppermute | solution.py:23
  87.6 3.5 %collective-permute-done.19.odd = f32[8,256]{1,0:T(8,128)S(1)} collective-permute-done((f32[8,256]{1,0:T(8,128)S(1)}, f32[8,256]{1,0:T(8,128)S(1)}, u32[]{:S(2)}, u32[]{:S(2)}) %collective-permute-start.19) | collective-permute-done | bytes 8224 | tf_op jit(solution)/shard_map/ppermute | solution.py:23
  95.1 4.0 %collective-permute-start.22 = (f32[8,256]{1,0:T(8,128)S(1)}, f32[8,256]{1,0:T(8,128)S(1)}, u32[]{:S(2)}, u32[]{:S(2)}) collective-permute-start(f32[8,256]{1,0:T(8,128)S(1)} %get-tuple-element.61), channel_id=1, source_target_pairs={{0,1},{1,0},{2,3},{3,2},{4,5},{5,4},{6,7},{7,6},{8,9},{9,8},{10,11... | collective-permute-start | bytes 24584 | tf_op jit(solution)/shard_map/ppermute | solution.py:23
  102.6 6.9 %collective-permute-start.24 = (f32[8,256]{1,0:T(8,128)S(1)}, f32[8,256]{1,0:T(8,128)S(1)}, u32[]{:S(2)}, u32[]{:S(2)}) collective-permute-start(f32[8,256]{1,0:T(8,128)S(1)} %get-tuple-element.64), channel_id=1, source_target_pairs={{0,1},{1,0},{2,3},{3,2},{4,5},{5,4},{6,7},{7,6},{8,9},{9,8},{10,11... | collective-permute-start | bytes 24584 | tf_op jit(solution)/shard_map/ppermute | solution.py:23
  111.1 2.2 %transposed.1 = (f32[8,32,256]{2,1,0:T(8,128)S(1)}, f32[8,32,256]{2,1,0:T(8,128)S(1)}, f32[8,32,256]{2,1,0:T(8,128)S(1)}, f32[8,256]{1,0:T(8,128)S(1)}) custom-call(s32[64]{0:T(128)S(1)} %reshape.7.target_ref, bf16[8,8,256,256]{3,2,1,0:T(8,128)(2,1)S(1)} %get-tuple-element.38.tiles_ref, f32[8,256]{1,0:T(8,128)S(1)} %get-tuple-element.39.inverse_ref, ...), custom_call_target="tpu_custom_call" | custom-call | tf_op jit(solution)/shard_map/transposed/pallas_call | solution.py:221
  113.7 7.2 %collective-permute-start.30 = (f32[8,32,256]{2,1,0:T(8,128)S(1)}, f32[8,32,256]{2,1,0:T(8,128)S(1)}, u32[]{:S(2)}, u32[]{:S(2)}) collective-permute-start(f32[8,32,256]{2,1,0:T(8,128)S(1)} %get-tuple-element.68), channel_id=1, source_target_pairs={{0,1},{1,0},{2,3},{3,2},{4,5},{5,4},{6,7},{7,6},{8,9},{9,8},{10,11... | collective-permute-start | bytes 786440 | tf_op jit(solution)/shard_map/ppermute | solution.py:23
  120.8 5.7 %collective-permute-start.28 = (bf16[32,2048]{1,0:T(8,128)(2,1)S(1)}, bf16[32,2048]{1,0:T(8,128)(2,1)S(1)}, u32[]{:S(2)}, u32[]{:S(2)}) collective-permute-start(bf16[32,2048]{1,0:T(8,128)(2,1)S(1)} %copy-done.1), channel_id=1, source_target_pairs={{0,1},{1,0},{2,3},{3,2},{4,5},{5,4},{6,7},{7,6},{8,9},{9,8},{10,11... | collective-permute-start | bytes 393224 | tf_op jit(solution)/shard_map/ppermute | solution.py:23
  126.6 3.6 %collective-permute-done.26.root_even = f32[8,256]{1,0:T(8,128)S(1)} collective-permute-done((f32[8,256]{1,0:T(8,128)S(1)}, f32[8,256]{1,0:T(8,128)S(1)}, u32[]{:S(2)}, u32[]{:S(2)}) %collective-permute-start.26) | collective-permute-done | bytes 8224 | tf_op jit(solution)/shard_map/ppermute | solution.py:23
  130.2 3.6 %collective-permute-done.25.root_odd = f32[8,256]{1,0:T(8,128)S(1)} collective-permute-done((f32[8,256]{1,0:T(8,128)S(1)}, f32[8,256]{1,0:T(8,128)S(1)}, u32[]{:S(2)}, u32[]{:S(2)}) %collective-permute-start.25) | collective-permute-done | bytes 8224 | tf_op jit(solution)/shard_map/ppermute | solution.py:23
  133.9 3.1 %forward.1.forward_ref = f32[8,32,256]{2,1,0:T(8,128)S(1)} custom-call(s32[64]{0:T(128)S(1)} %reshape.7.target_ref, bf16[8,8,256,256]{3,2,1,0:T(8,128)(2,1)S(1)} %get-tuple-element.38.tiles_ref, f32[8,256]{1,0:T(8,128)S(1)} %get-tuple-element.39.inverse_ref, f32[8,256]{1,0:T(8,128)S(1)} %collective-permute-done.25.root_odd, ...), custom_call_target="tpu_custom_call" | custom-call | tf_op jit(solution)/shard_map/forward/pallas_call | solution.py:221
  138.6 6.3 %collective-permute-start.33 = (f32[32,32]{1,0:T(8,128)S(1)}, f32[32,32]{1,0:T(8,128)S(1)}, u32[]{:S(2)}, u32[]{:S(2)}) collective-permute-start(f32[32,32]{1,0:T(8,128)S(1)} %add.102), channel_id=1, source_target_pairs={{0,1},{1,0},{2,3},{3,2},{4,5},{5,4},{6,7},{7,6},{8,9},{9,8},{10,11... | collective-permute-start | bytes 12296 | tf_op jit(solution)/shard_map/ppermute | solution.py:23
  146.9 3.3 %collective-permute-done.32 = f32[32,32]{1,0:T(8,128)S(1)} collective-permute-done((f32[32,32]{1,0:T(8,128)S(1)}, f32[32,32]{1,0:T(8,128)S(1)}, u32[]{:S(2)}, u32[]{:S(2)}) %collective-permute-start.32) | collective-permute-done | bytes 4128 | tf_op jit(solution)/shard_map/ppermute | solution.py:23
  150.3 4.6 %collective-permute-start.35 = (f32[32,32]{1,0:T(8,128)S(1)}, f32[32,32]{1,0:T(8,128)S(1)}, u32[]{:S(2)}, u32[]{:S(2)}) collective-permute-start(f32[32,32]{1,0:T(8,128)S(1)} %add_add_fusion.2), channel_id=1, source_target_pairs={{0,16},{4,20},{8,24},{12,28},{16,0},{20,4},{24,8},{28,12},{32,48},... | collective-permute-start | bytes 12296 | tf_op jit(solution)/shard_map/ppermute | solution.py:23
  156.8 3.7 %collective-permute-done.38 = f32[32,32]{1,0:T(8,128)S(1)} collective-permute-done((f32[32,32]{1,0:T(8,128)S(1)}, f32[32,32]{1,0:T(8,128)S(1)}, u32[]{:S(2)}, u32[]{:S(2)}) %collective-permute-start.38) | collective-permute-done | bytes 4128 | tf_op jit(solution)/shard_map/ppermute | solution.py:23
  162.2 3.9 %collective-permute-start.39 = (f32[32,32]{1,0:T(8,128)S(1)}, f32[32,32]{1,0:T(8,128)S(1)}, u32[]{:S(2)}, u32[]{:S(2)}) collective-permute-start(f32[32,32]{1,0:T(8,128)S(1)} %add.109), channel_id=1, source_target_pairs={{0,160},{4,164},{8,168},{12,172},{16,176},{20,180},{24,184},{28,18... | collective-permute-start | bytes 12296 | tf_op jit(solution)/shard_map/ppermute | solution.py:23
  166.9 2.1 %collective-permute-done.39 = f32[32,32]{1,0:T(8,128)S(1)} collective-permute-done((f32[32,32]{1,0:T(8,128)S(1)}, f32[32,32]{1,0:T(8,128)S(1)}, u32[]{:S(2)}, u32[]{:S(2)}) %collective-permute-start.39) | collective-permute-done | bytes 4128 | tf_op jit(solution)/shard_map/ppermute | solution.py:23
  169.0 3.8 %basis.1 = f32[32,2048]{1,0:T(8,128)} custom-call(f32[32,32]{1,0:T(8,128)S(1)} %add_add_fusion.gram_ref, f32[32,2048]{1,0:T(8,128)S(1)} %get-tuple-element.70.embedded_ref), custom_call_target="tpu_custom_call" | custom-call | tf_op jit(solution)/shard_map/basis/pallas_call | solution.py:221
  (83 shorter events, 37.2 us)
Async XLA Ops:
  11.1 10.6 %collective-permute-start = (f32[8,256]{1,0:T(8,128)S(1)}, f32[8,256]{1,0:T(8,128)S(1)}, u32[]{:S(2)}, u32[]{:S(2)}) collective-permute-start(f32[8,256]{1,0:T(8,128)S(1)} %get-tuple-element.40), channel_id=1, source_target_pairs={{0,255},{1,2},{2,1},{3,4},{4,3},{5,6},{6,5},{7,8},{8,7},{9,10},{10... | collective-permute-start | bytes 24584 | tf_op jit(solution)/shard_map/ppermute | solution.py:23
  12.7 10.6 %collective-permute-start.1 = (f32[8,256]{1,0:T(8,128)S(1)}, f32[8,256]{1,0:T(8,128)S(1)}, u32[]{:S(2)}, u32[]{:S(2)}) collective-permute-start(f32[8,256]{1,0:T(8,128)S(1)} %get-tuple-element.42), channel_id=1, source_target_pairs={{0,1},{1,0},{2,3},{3,2},{4,5},{5,4},{6,7},{7,6},{8,9},{9,8},{10,11... | collective-permute-start | bytes 24584 | tf_op jit(solution)/shard_map/ppermute | solution.py:23
  25.5 7.0 %collective-permute-start.2 = (f32[16,256]{1,0:T(8,128)S(1)}, f32[16,256]{1,0:T(8,128)S(1)}, u32[]{:S(2)}, u32[]{:S(2)}) collective-permute-start(f32[16,256]{1,0:T(8,128)S(1)} %get-tuple-element.44), channel_id=1, source_target_pairs={{0,255},{1,2},{2,1},{3,4},{4,3},{5,6},{6,5},{7,8},{8,7},{9,10},{10... | collective-permute-start | bytes 49160 | tf_op jit(solution)/shard_map/ppermute | solution.py:23
  25.6 8.6 %collective-permute-start.3 = (f32[16,256]{1,0:T(8,128)S(1)}, f32[16,256]{1,0:T(8,128)S(1)}, u32[]{:S(2)}, u32[]{:S(2)}) collective-permute-start(f32[16,256]{1,0:T(8,128)S(1)} %get-tuple-element.46), channel_id=1, source_target_pairs={{0,1},{1,0},{2,3},{3,2},{4,5},{5,4},{6,7},{7,6},{8,9},{9,8},{10,11... | collective-permute-start | bytes 49160 | tf_op jit(solution)/shard_map/ppermute | solution.py:23
  36.4 7.0 %collective-permute-start.4 = (f32[16,256]{1,0:T(8,128)S(1)}, f32[16,256]{1,0:T(8,128)S(1)}, u32[]{:S(2)}, u32[]{:S(2)}) collective-permute-start(f32[16,256]{1,0:T(8,128)S(1)} %get-tuple-element.48), channel_id=1, source_target_pairs={{0,255},{1,2},{2,1},{3,4},{4,3},{5,6},{6,5},{7,8},{8,7},{9,10},{10... | collective-permute-start | bytes 49160 | tf_op jit(solution)/shard_map/ppermute | solution.py:23
  36.5 8.6 %collective-permute-start.5 = (f32[16,256]{1,0:T(8,128)S(1)}, f32[16,256]{1,0:T(8,128)S(1)}, u32[]{:S(2)}, u32[]{:S(2)}) collective-permute-start(f32[16,256]{1,0:T(8,128)S(1)} %get-tuple-element.50), channel_id=1, source_target_pairs={{0,1},{1,0},{2,3},{3,2},{4,5},{5,4},{6,7},{7,6},{8,9},{9,8},{10,11... | collective-permute-start | bytes 49160 | tf_op jit(solution)/shard_map/ppermute | solution.py:23
  46.9 7.0 %collective-permute-start.6 = (f32[8,256]{1,0:T(8,128)S(1)}, f32[8,256]{1,0:T(8,128)S(1)}, u32[]{:S(2)}, u32[]{:S(2)}) collective-permute-start(f32[8,256]{1,0:T(8,128)S(1)} %get-tuple-element.52), channel_id=1, source_target_pairs={{0,255},{1,2},{2,1},{3,4},{4,3},{5,6},{6,5},{7,8},{8,7},{9,10},{10... | collective-permute-start | bytes 24584 | tf_op jit(solution)/shard_map/ppermute | solution.py:23
  47.0 8.5 %collective-permute-start.7 = (f32[8,256]{1,0:T(8,128)S(1)}, f32[8,256]{1,0:T(8,128)S(1)}, u32[]{:S(2)}, u32[]{:S(2)}) collective-permute-start(f32[8,256]{1,0:T(8,128)S(1)} %get-tuple-element.54), channel_id=1, source_target_pairs={{0,1},{1,0},{2,3},{3,2},{4,5},{5,4},{6,7},{7,6},{8,9},{9,8},{10,11... | collective-permute-start | bytes 24584 | tf_op jit(solution)/shard_map/ppermute | solution.py:23
  58.8 5.2 %collective-permute-start.9 = (f32[16,128]{1,0:T(8,128)S(1)}, f32[16,128]{1,0:T(8,128)S(1)}, u32[]{:S(2)}, u32[]{:S(2)}) collective-permute-start(f32[16,128]{1,0:T(8,128)S(1)} %add.91), channel_id=1, source_target_pairs={{0,2},{1,3},{2,0},{3,1},{4,6},{5,7},{6,4},{7,5},{8,10},{9,11},{10,... | collective-permute-start | bytes 24584 | tf_op jit(solution)/shard_map/ppermute | solution.py:23
  64.0 4.9 %collective-permute-start.14 = (f32[16,128]{1,0:T(8,128)S(1)}, f32[16,128]{1,0:T(8,128)S(1)}, u32[]{:S(2)}, u32[]{:S(2)}) collective-permute-start(f32[16,128]{1,0:T(8,128)S(1)} %add_add_fusion.5), channel_id=1, source_target_pairs={{0,24},{4,28},{8,16},{12,20},{16,8},{20,12},{24,0},{28,4},{32,56},... | collective-permute-start | bytes 24584 | tf_op jit(solution)/shard_map/ppermute | solution.py:23
  64.0 4.9 %collective-permute-start.13 = (f32[16,128]{1,0:T(8,128)S(1)}, f32[16,128]{1,0:T(8,128)S(1)}, u32[]{:S(2)}, u32[]{:S(2)}) collective-permute-start(f32[16,128]{1,0:T(8,128)S(1)} %add_add_fusion.5), channel_id=1, source_target_pairs={{0,8},{4,12},{8,0},{12,4},{16,24},{20,28},{24,16},{28,20},{32,40},... | collective-permute-start | bytes 24584 | tf_op jit(solution)/shard_map/ppermute | solution.py:23
  64.1 6.3 %collective-permute-start.12 = (f32[16,128]{1,0:T(8,128)S(1)}, f32[16,128]{1,0:T(8,128)S(1)}, u32[]{:S(2)}, u32[]{:S(2)}) collective-permute-start(f32[16,128]{1,0:T(8,128)S(1)} %add_add_fusion.5), channel_id=1, source_target_pairs={{0,16},{4,20},{8,24},{12,28},{16,0},{20,4},{24,8},{28,12},{32,48},... | collective-permute-start | bytes 24584 | tf_op jit(solution)/shard_map/ppermute | solution.py:23
  74.1 7.2 %collective-permute-start.18 = (f32[16,128]{1,0:T(8,128)S(1)}, f32[16,128]{1,0:T(8,128)S(1)}, u32[]{:S(2)}, u32[]{:S(2)}) collective-permute-start(f32[16,128]{1,0:T(8,128)S(1)} %add.98), channel_id=1, source_target_pairs={{0,224},{4,228},{8,232},{12,236},{16,240},{20,244},{24,248},{28,25... | collective-permute-start | bytes 24584 | tf_op jit(solution)/shard_map/ppermute | solution.py:23
  78.9 4.5 %collective-permute-start.17 = (f32[16,128]{1,0:T(8,128)S(1)}, f32[16,128]{1,0:T(8,128)S(1)}, u32[]{:S(2)}, u32[]{:S(2)}) collective-permute-start(f32[16,128]{1,0:T(8,128)S(1)} %add.98), channel_id=1, source_target_pairs={{0,192},{4,196},{8,200},{12,204},{16,208},{20,212},{24,216},{28,22... | collective-permute-start | bytes 24584 | tf_op jit(solution)/shard_map/ppermute | solution.py:23
  78.9 6.7 %collective-permute-start.16 = (f32[16,128]{1,0:T(8,128)S(1)}, f32[16,128]{1,0:T(8,128)S(1)}, u32[]{:S(2)}, u32[]{:S(2)}) collective-permute-start(f32[16,128]{1,0:T(8,128)S(1)} %add.98), channel_id=1, source_target_pairs={{0,160},{4,164},{8,168},{12,172},{16,176},{20,180},{24,184},{28,18... | collective-permute-start | bytes 24584 | tf_op jit(solution)/shard_map/ppermute | solution.py:23
  93.1 6.0 %collective-permute-start.21 = (f32[8,256]{1,0:T(8,128)S(1)}, f32[8,256]{1,0:T(8,128)S(1)}, u32[]{:S(2)}, u32[]{:S(2)}) collective-permute-start(f32[8,256]{1,0:T(8,128)S(1)} %get-tuple-element.59), channel_id=1, source_target_pairs={{0,255},{1,2},{2,1},{3,4},{4,3},{5,6},{6,5},{7,8},{8,7},{9,10},{10... | collective-permute-start | bytes 24584 | tf_op jit(solution)/shard_map/ppermute | solution.py:23
  95.1 5.6 %collective-permute-start.22 = (f32[8,256]{1,0:T(8,128)S(1)}, f32[8,256]{1,0:T(8,128)S(1)}, u32[]{:S(2)}, u32[]{:S(2)}) collective-permute-start(f32[8,256]{1,0:T(8,128)S(1)} %get-tuple-element.61), channel_id=1, source_target_pairs={{0,1},{1,0},{2,3},{3,2},{4,5},{5,4},{6,7},{7,6},{8,9},{9,8},{10,11... | collective-permute-start | bytes 24584 | tf_op jit(solution)/shard_map/ppermute | solution.py:23
  102.5 7.0 %collective-permute-start.23 = (f32[8,256]{1,0:T(8,128)S(1)}, f32[8,256]{1,0:T(8,128)S(1)}, u32[]{:S(2)}, u32[]{:S(2)}) collective-permute-start(f32[8,256]{1,0:T(8,128)S(1)} %get-tuple-element.62), channel_id=1, source_target_pairs={{0,255},{1,2},{2,1},{3,4},{4,3},{5,6},{6,5},{7,8},{8,7},{9,10},{10... | collective-permute-start | bytes 24584 | tf_op jit(solution)/shard_map/ppermute | solution.py:23
  102.6 8.5 %collective-permute-start.24 = (f32[8,256]{1,0:T(8,128)S(1)}, f32[8,256]{1,0:T(8,128)S(1)}, u32[]{:S(2)}, u32[]{:S(2)}) collective-permute-start(f32[8,256]{1,0:T(8,128)S(1)} %get-tuple-element.64), channel_id=1, source_target_pairs={{0,1},{1,0},{2,3},{3,2},{4,5},{5,4},{6,7},{7,6},{8,9},{9,8},{10,11... | collective-permute-start | bytes 24584 | tf_op jit(solution)/shard_map/ppermute | solution.py:23
  113.3 23.6 %collective-permute-start.29 = (f32[8,32,256]{2,1,0:T(8,128)S(1)}, f32[8,32,256]{2,1,0:T(8,128)S(1)}, u32[]{:S(2)}, u32[]{:S(2)}) collective-permute-start(f32[8,32,256]{2,1,0:T(8,128)S(1)} %get-tuple-element.66), channel_id=1, source_target_pairs={{0,255},{1,2},{2,1},{3,4},{4,3},{5,6},{6,5},{7,8},{8,7},{9,10},{10... | collective-permute-start | bytes 786440 | tf_op jit(solution)/shard_map/ppermute | solution.py:23
  113.7 23.3 %collective-permute-start.30 = (f32[8,32,256]{2,1,0:T(8,128)S(1)}, f32[8,32,256]{2,1,0:T(8,128)S(1)}, u32[]{:S(2)}, u32[]{:S(2)}) collective-permute-start(f32[8,32,256]{2,1,0:T(8,128)S(1)} %get-tuple-element.68), channel_id=1, source_target_pairs={{0,1},{1,0},{2,3},{3,2},{4,5},{5,4},{6,7},{7,6},{8,9},{9,8},{10,11... | collective-permute-start | bytes 786440 | tf_op jit(solution)/shard_map/ppermute | solution.py:23
  120.8 13.0 %collective-permute-start.27 = (bf16[32,2048]{1,0:T(8,128)(2,1)S(1)}, bf16[32,2048]{1,0:T(8,128)(2,1)S(1)}, u32[]{:S(2)}, u32[]{:S(2)}) collective-permute-start(bf16[32,2048]{1,0:T(8,128)(2,1)S(1)} %copy-done.1), channel_id=1, source_target_pairs={{0,255},{1,2},{2,1},{3,4},{4,3},{5,6},{6,5},{7,8},{8,7},{9,10},{10... | collective-permute-start | bytes 393224 | tf_op jit(solution)/shard_map/ppermute | solution.py:23
  120.8 13.0 %collective-permute-start.28 = (bf16[32,2048]{1,0:T(8,128)(2,1)S(1)}, bf16[32,2048]{1,0:T(8,128)(2,1)S(1)}, u32[]{:S(2)}, u32[]{:S(2)}) collective-permute-start(bf16[32,2048]{1,0:T(8,128)(2,1)S(1)} %copy-done.1), channel_id=1, source_target_pairs={{0,1},{1,0},{2,3},{3,2},{4,5},{5,4},{6,7},{7,6},{8,9},{9,8},{10,11... | collective-permute-start | bytes 393224 | tf_op jit(solution)/shard_map/ppermute | solution.py:23
  138.6 8.3 %collective-permute-start.34 = (f32[32,32]{1,0:T(8,128)S(1)}, f32[32,32]{1,0:T(8,128)S(1)}, u32[]{:S(2)}, u32[]{:S(2)}) collective-permute-start(f32[32,32]{1,0:T(8,128)S(1)} %add.102), channel_id=1, source_target_pairs={{0,3},{1,2},{2,1},{3,0},{4,7},{5,6},{6,5},{7,4},{8,11},{9,10},{10,... | collective-permute-start | bytes 12296 | tf_op jit(solution)/shard_map/ppermute | solution.py:23
  138.6 8.3 %collective-permute-start.33 = (f32[32,32]{1,0:T(8,128)S(1)}, f32[32,32]{1,0:T(8,128)S(1)}, u32[]{:S(2)}, u32[]{:S(2)}) collective-permute-start(f32[32,32]{1,0:T(8,128)S(1)} %add.102), channel_id=1, source_target_pairs={{0,1},{1,0},{2,3},{3,2},{4,5},{5,4},{6,7},{7,6},{8,9},{9,8},{10,11... | collective-permute-start | bytes 12296 | tf_op jit(solution)/shard_map/ppermute | solution.py:23
  144.9 5.2 %collective-permute-start.32 = (f32[32,32]{1,0:T(8,128)S(1)}, f32[32,32]{1,0:T(8,128)S(1)}, u32[]{:S(2)}, u32[]{:S(2)}) collective-permute-start(f32[32,32]{1,0:T(8,128)S(1)} %add.102), channel_id=1, source_target_pairs={{0,2},{1,3},{2,0},{3,1},{4,6},{5,7},{6,4},{7,5},{8,10},{9,11},{10,... | collective-permute-start | bytes 12296 | tf_op jit(solution)/shard_map/ppermute | solution.py:23
  150.2 4.9 %collective-permute-start.37 = (f32[32,32]{1,0:T(8,128)S(1)}, f32[32,32]{1,0:T(8,128)S(1)}, u32[]{:S(2)}, u32[]{:S(2)}) collective-permute-start(f32[32,32]{1,0:T(8,128)S(1)} %add_add_fusion.2), channel_id=1, source_target_pairs={{0,24},{4,28},{8,16},{12,20},{16,8},{20,12},{24,0},{28,4},{32,56},... | collective-permute-start | bytes 12296 | tf_op jit(solution)/shard_map/ppermute | solution.py:23
  150.2 4.9 %collective-permute-start.36 = (f32[32,32]{1,0:T(8,128)S(1)}, f32[32,32]{1,0:T(8,128)S(1)}, u32[]{:S(2)}, u32[]{:S(2)}) collective-permute-start(f32[32,32]{1,0:T(8,128)S(1)} %add_add_fusion.2), channel_id=1, source_target_pairs={{0,8},{4,12},{8,0},{12,4},{16,24},{20,28},{24,16},{28,20},{32,40},... | collective-permute-start | bytes 12296 | tf_op jit(solution)/shard_map/ppermute | solution.py:23
  150.3 6.5 %collective-permute-start.35 = (f32[32,32]{1,0:T(8,128)S(1)}, f32[32,32]{1,0:T(8,128)S(1)}, u32[]{:S(2)}, u32[]{:S(2)}) collective-permute-start(f32[32,32]{1,0:T(8,128)S(1)} %add_add_fusion.2), channel_id=1, source_target_pairs={{0,16},{4,20},{8,24},{12,28},{16,0},{20,4},{24,8},{28,12},{32,48},... | collective-permute-start | bytes 12296 | tf_op jit(solution)/shard_map/ppermute | solution.py:23
  160.5 5.6 %collective-permute-start.41 = (f32[32,32]{1,0:T(8,128)S(1)}, f32[32,32]{1,0:T(8,128)S(1)}, u32[]{:S(2)}, u32[]{:S(2)}) collective-permute-start(f32[32,32]{1,0:T(8,128)S(1)} %add.109), channel_id=1, source_target_pairs={{0,224},{4,228},{8,232},{12,236},{16,240},{20,244},{24,248},{28,25... | collective-permute-start | bytes 12296 | tf_op jit(solution)/shard_map/ppermute | solution.py:23
  162.2 4.6 %collective-permute-start.40 = (f32[32,32]{1,0:T(8,128)S(1)}, f32[32,32]{1,0:T(8,128)S(1)}, u32[]{:S(2)}, u32[]{:S(2)}) collective-permute-start(f32[32,32]{1,0:T(8,128)S(1)} %add.109), channel_id=1, source_target_pairs={{0,192},{4,196},{8,200},{12,204},{16,208},{20,212},{24,216},{28,22... | collective-permute-start | bytes 12296 | tf_op jit(solution)/shard_map/ppermute | solution.py:23
  162.2 6.7 %collective-permute-start.39 = (f32[32,32]{1,0:T(8,128)S(1)}, f32[32,32]{1,0:T(8,128)S(1)}, u32[]{:S(2)}, u32[]{:S(2)}) collective-permute-start(f32[32,32]{1,0:T(8,128)S(1)} %add.109), channel_id=1, source_target_pairs={{0,160},{4,164},{8,168},{12,172},{16,176},{20,180},{24,184},{28,18... | collective-permute-start | bytes 12296 | tf_op jit(solution)/shard_map/ppermute | solution.py:23
  (13 other events, 56.8 us)
where the time goes:
time: 174 us; the launch traced here: 173 us
  starting transfers between devices  92.6 us (53%)
  waiting for transfers between devices  47.7 us (27%)
  Pallas kernels  26.7 us (15%)
  local copies, waits for them, and re-layouts  4.82 us (3%)
    ppermute x42, starting transfers between devices, swap(): lax.ppermute(shard, axis, [(i, partner(i) % count) for i in range(count)])  92.6 us
    ppermute x42, waiting for transfers between devices, swap(): lax.ppermute(shard, axis, [(i, partner(i) % count) for i in range(count)])  47.7 us
    pallas_call x12, Pallas kernels, call(): pl.pallas_call(kernel, out_shape=outs, in_specs=specs, out_specs=[VMEM] *...  26.7 us
    unnamed x6, local copies, waits for them, and re-layouts  4.04 us
  transfers between devices with their start and end apart: 42, of which 24 were waited for; matrix products, arithmetic and copies ran while one was open for 0% of the time, Pallas kernels for 2%

commit v1 on v0

v1 whole, which is shorter than its diff:
```python
import functools
import math

import jax
import jax.numpy as jnp
from jax import lax
from jax.experimental import pallas as pl
from jax.experimental.pallas import tpu as pltpu
from jax.sharding import PartitionSpec as P

RING = ("rows", "cols")
F32 = jnp.float32
BF16 = jnp.bfloat16
HIGHEST = lax.Precision.HIGHEST
LAST_DIMS = (((1,), (1,)), ((), ()))
SMEM = pl.BlockSpec(memory_space=pltpu.SMEM)
VMEM = pl.BlockSpec(memory_space=pltpu.VMEM)
CHUNK = 8
DEAD = 24
HALO_CHUNKS = 128
OWN_CHUNKS = 129
SPARE = 130


def swap(shard, axis, partner):
    count = lax.axis_size(axis)
    return lax.ppermute(shard, axis, [(i, partner(i) % count) for i in range(count)])


def ring_pairs(shard_odd, shard_even):
    got_odd = swap(shard_odd, RING, lambda i: i + 1 if i % 2 else i - 1)
    got_even = swap(shard_even, RING, lambda i: i - 1 if i % 2 else i + 1)
    return got_odd, got_even


def gathered(part, axis, groups):
    spread = jnp.broadcast_to(part[None], (len(groups[0]), *part.shape))
    return lax.all_to_all(spread, axis, 0, 0, tiled=True, axis_index_groups=groups)


def chip_parts(part):
    part = part + swap(part, "rows", lambda i: i ^ 1)
    cols = lax.axis_size("cols")
    devices = lax.axis_size(RING)
    groups = [[i for i in range(devices) if (i // cols) % 2 == core] for core in (0, 1)]
    return gathered(part, RING, groups)


def plane_parts(part):
    part = part + swap(part, "rows", lambda i: i ^ 1)
    part = part + sum(swap(part, "cols", lambda i, d=d: i ^ d) for d in (2, 1, 3))
    groups = [list(range(core, lax.axis_size("rows"), 2)) for core in (0, 1)]
    return gathered(part, "rows", groups)


def two_parts(value):
    high = value.astype(BF16).astype(F32)
    return high, value - high


def spread_blocks(rows, left_ref):
    blocks, height = left_ref.shape[:2]
    if rows.shape[0] < height:
        rows = jnp.concatenate([rows, jnp.zeros((height - rows.shape[0], rows.shape[1]), F32)], axis=0)
    owner = lax.broadcasted_iota(jnp.int32, rows.shape, 0) % blocks
    for block in range(blocks):
        left_ref[block] = jnp.where(owner == block, rows, 0.0).astype(BF16)


def for_tiles(table_ref, own, visit):
    first = 64 if own else 0

    def chunk(number, carry):
        for place in range(CHUNK):
            entry = table_ref[first + number * CHUNK + place]
            visit(entry >> 5, entry & 31)
        return carry

    lax.fori_loop(0, table_ref[OWN_CHUNKS if own else HALO_CHUNKS], chunk, 0)


def push_rows(table_ref, own, tiles_ref, left_ref, window, split):
    height = window.shape[1]
    window[...] = jnp.zeros_like(window)

    def visit(tile, target):
        product = jnp.dot(left_ref[tile >> 3], tiles_ref[tile], preferred_element_type=F32)
        if split:
            product = product[:height] + product[height : 2 * height]
        window[target] += product[:height]

    for_tiles(table_ref, own, visit)


def landed(window, part, out):
    for channel in range(out.shape[0] // 8):
        rows = slice(channel * 8, (channel + 1) * 8)
        out[rows, :] = jnp.sum(window[part * 8 : (part + 1) * 8, rows, :], axis=1)


def load_kernel(cols_hbm, count_hbm, tiles_hbm, start_hbm, tiles_ref, target_ref, inverse_ref, odd_ref, own_ref, even_ref,
                window, start_ref, cols_ref, count_ref, sems, small_sems):
    blocks, slots, width = tiles_hbm.shape[:3]
    small = [
        pltpu.make_async_copy(cols_hbm, cols_ref, small_sems.at[0]),
        pltpu.make_async_copy(count_hbm, count_ref, small_sems.at[1]),
    ]
    small += [
        pltpu.make_async_copy(start_hbm.at[pl.ds(b * width, width)], start_ref.at[b], small_sems.at[2 + b]) for b in range(blocks)
    ]
    copies = [
        pltpu.make_async_copy(tiles_hbm.at[b], tiles_ref.at[pl.ds(b * slots, slots)], sems.at[b]) for b in range(blocks)
    ]
    for copy in small + copies:
        copy.start()
    ones = jnp.ones((16, 128), BF16)
    window[...] = jnp.zeros_like(window)
    line = lax.broadcasted_iota(jnp.int32, (16, width), 0)
    total_blocks = blocks * lax.axis_size("rows") * lax.axis_size("cols")
    place = lax.axis_index("rows") * lax.axis_size("cols") + lax.axis_index("cols")
    swapped = place % 2 == 1
    for copy in small:
        copy.wait()

    def row_sums(block):
        folded = jnp.zeros((width, 128), F32)
        for slot in range(slots):
            tile = tiles_ref[block * slots + slot].astype(F32)
            folded = folded + (tile[:, :128] + tile[:, 128:]) * jnp.where(slot < count_ref[block], 1.0, 0.0)
        total = jnp.zeros((16, width), F32)
        for _ in range(3):
            part = folded.astype(BF16)
            folded = folded - part.astype(F32)
            total = total + lax.dot_general(ones, part, LAST_DIMS, preferred_element_type=F32)
        return total

    def target_of(block, slot):
        target = cols_ref[block, slot] - place * blocks + blocks
        target = jnp.where(target < 0, target + total_blocks, target)
        target = jnp.where(target >= total_blocks, target - total_blocks, target)
        flipped = jnp.where(target >= 2 * blocks, target - 2 * blocks, jnp.where(target < blocks, target + 2 * blocks, target))
        target = jnp.where(swapped, flipped, target)
        return jnp.where(slot < count_ref[block], target, DEAD)

    def push_block(block, total):
        inverse = 1.0 / total
        inverse_ref[block : block + 1, :] = inverse[0:1]
        left = jnp.where(line == block, start_ref[block : block + 1, :] * inverse, 0.0).astype(BF16)
        for slot in range(slots):
            tile = block * slots + slot
            target = target_of(block, slot)
            target_ref[tile] = target
            window[target] += jnp.dot(left, tiles_ref[tile], preferred_element_type=F32)[0:8]

    before = None
    for block in range(blocks):
        copies[block].wait()
        total = row_sums(block)
        if before is not None:
            push_block(block - 1, before)
        before = total
    push_block(blocks - 1, before)
    landed(window, 0, odd_ref)
    landed(window, 1, own_ref)
    landed(window, 2, even_ref)


def table_kernel(target_ref, table_ref):
    for entry in range(128):
        table_ref[entry] = DEAD
    halo_count, own_count = jnp.int32(0), jnp.int32(0)
    for tile in range(target_ref.shape[0]):
        target = target_ref[tile]
        to_own = (target >= 8) & (target < 16)
        to_halo = (target < 8) | ((target >= 16) & (target < DEAD))
        entry = target + tile * 32
        table_ref[jnp.where(to_halo, halo_count, jnp.where(to_own, 64 + own_count, SPARE))] = entry
        halo_count += jnp.where(to_halo, 1, 0)
        own_count += jnp.where(to_own, 1, 0)
    table_ref[HALO_CHUNKS] = (halo_count + CHUNK - 1) >> 3
    table_ref[OWN_CHUNKS] = (own_count + CHUNK - 1) >> 3


def halo_step(rows, split, table_ref, tiles_ref, to_odd, to_even, left_ref, window):
    spread_blocks(jnp.concatenate(two_parts(rows), axis=0) if split else rows, left_ref)
    push_rows(table_ref, False, tiles_ref, left_ref, window, split)
    landed(window, 0, to_odd)
    landed(window, 2, to_even)


def second_kernel(table_ref, tiles_ref, inverse_ref, odd, own, even, to_odd, to_even, left_ref, value_ref, window):
    raw = 0.85 * (own[...] + odd[...] + even[...]) + 0.15
    value_ref[...] = raw
    inverse = inverse_ref[...]
    rows = jnp.concatenate([raw * inverse, inverse], axis=0)
    halo_step(rows, True, table_ref, tiles_ref, to_odd, to_even, left_ref, window)


def chain_kernel(channels, table_ref, tiles_ref, inverse_ref, odd, own, even, to_odd, to_even, left_ref, value_ref, window):
    value = own[...] + odd[...] + even[...]
    value_ref[...] = value
    inverse = inverse_ref[...]
    rows = [value[8 * c : 8 * c + 8] * inverse for c in range(channels)]
    rows = jnp.concatenate(rows, axis=0) if channels > 1 else rows[0]
    halo_step(rows, True, table_ref, tiles_ref, to_odd, to_even, left_ref, window)


def own_kernel(split, table_ref, tiles_ref, left_ref, kept, window):
    push_rows(table_ref, True, tiles_ref, left_ref, window, split)
    landed(window, 1, kept)


def sums_kernel(raw_ref, second_ref, third_ref, odd, own, even, out_ref):
    raw = raw_ref[...]
    second = second_ref[0:8]
    ones_1 = second_ref[8:16]
    third = third_ref[0:8]
    ones_2 = third_ref[8:16]
    fourth = own[...] + odd[...] + even[...]
    wanted = (
        raw * raw,
        second * second, second,
        third * third, third * ones_1, third, ones_1 * ones_1, ones_1,
        fourth * fourth, fourth * ones_2, fourth * ones_1, fourth,
        ones_2 * ones_2, ones_2 * ones_1, ones_2, jnp.zeros_like(raw),
    )
    lines = [jnp.sum(term[:, :128] + term[:, 128:], axis=0, keepdims=True) for term in wanted]
    lines = jnp.sum(jnp.concatenate(lines, axis=0), axis=1, keepdims=True)
    row = lax.broadcasted_iota(jnp.int32, (16, 128), 0)
    lane = lax.broadcasted_iota(jnp.int32, (16, 128), 1)
    out_ref[...] = jnp.sum(jnp.where(row == lane, lines, 0.0), axis=0, keepdims=True)


def scales_of(sums, zones):
    line = jnp.broadcast_to(jnp.sum(sums, axis=0, keepdims=True), (16, 128))
    row = lax.broadcasted_iota(jnp.int32, line.shape, 0)
    lane = lax.broadcasted_iota(jnp.int32, line.shape, 1)
    totals = jnp.sum(jnp.where(row == lane, line, 0.0), axis=1, keepdims=True)
    (r11, c22, c2o, c33, c3p, c3o, pp, po, c44, c4q, c4p, c4o, qq, qp, qo) = (totals[i : i + 1] for i in range(15))
    root = math.sqrt(zones)
    floor = 0.15 * 0.15 * zones
    scale_1 = root / jnp.sqrt(r11)
    a2 = 0.85 * scale_1
    scale_2 = root / jnp.sqrt(a2 * a2 * c22 + 0.3 * a2 * c2o + floor)
    a3 = 0.85 * scale_2 * a2
    p3 = 0.85 * scale_2 * 0.15
    scale_3 = root / jnp.sqrt(
        a3 * a3 * c33 + 2.0 * a3 * (p3 * c3p + 0.15 * c3o) + p3 * p3 * pp + 0.3 * p3 * po + floor
    )
    a4 = 0.85 * scale_3 * a3
    q4 = 0.85 * scale_3 * p3
    p4 = 0.85 * scale_3 * 0.15
    scale_4 = root / jnp.sqrt(
        a4 * a4 * c44 + 2.0 * a4 * (q4 * c4q + p4 * c4p + 0.15 * c4o)
        + q4 * q4 * qq + p4 * p4 * pp + 2.0 * q4 * (p4 * qp + 0.15 * qo) + 0.3 * p4 * po + floor
    )
    return scale_1, scale_2, scale_3, scale_4


def replay_kernel(zones, table_ref, tiles_ref, inverse_ref, sums_ref, raw_ref, to_odd, to_even, left_ref, scales_ref, window):
    scales = scales_of(sums_ref[...], zones)
    for place, scale in enumerate(scales):
        scales_ref[place : place + 1, :] = jnp.broadcast_to(scale, (1, 128))
    rows = (raw_ref[...] * scales[0]) * inverse_ref[...]
    halo_step(rows, False, table_ref, tiles_ref, to_odd, to_even, left_ref, window)


def again_kernel(place, table_ref, tiles_ref, inverse_ref, scales_ref, odd, own, even, to_odd, to_even, left_ref, window):
    raw = 0.85 * (own[...] + odd[...] + even[...]) + 0.15
    rows = (raw * scales_ref[place : place + 1, 0:1]) * inverse_ref[...]
    halo_step(rows, False, table_ref, tiles_ref, to_odd, to_even, left_ref, window)


def transposed_kernel(table_ref, tiles_ref, inverse_ref, scales_ref, odd, own, even, probe_ref, to_odd, to_even, pushed_ref, scaled_ref, root_ref, window):
    blocks, chans, width = pushed_ref.shape
    raw = 0.85 * (own[...] + odd[...] + even[...]) + 0.15
    root = jnp.sqrt(raw * scales_ref[3:4, 0:1])
    root_ref[...] = root
    inverse_root = 1.0 / root
    gain = root * inverse_ref[...]
    for block in range(blocks):
        probe = probe_ref[:, block * width : (block + 1) * width].astype(F32)
        pushed_ref[block] = (probe * gain[block : block + 1]).astype(BF16)
        scaled = (probe * inverse_root[block : block + 1]).astype(BF16)
        scaled_ref[block] = scaled
        to_odd[2 * blocks + block] = scaled
        to_even[2 * blocks + block] = scaled
    window[...] = jnp.zeros_like(window)

    def visit(tile, target):
        window[target] += jnp.dot(pushed_ref[tile >> 3], tiles_ref[tile], preferred_element_type=F32)

    for_tiles(table_ref, False, visit)
    for part, out in ((0, to_odd), (2, to_even)):
        for block in range(blocks):
            high, low = two_parts(window[part * blocks + block])
            out[block] = high.astype(BF16)
            out[blocks + block] = low.astype(BF16)


def own_products_kernel(table_ref, tiles_ref, pushed_ref, scaled_ref, kept, forward_ref, window, forward):
    blocks = pushed_ref.shape[0]
    window[...] = jnp.zeros_like(window)
    forward[...] = jnp.zeros_like(forward)

    def visit(tile, target):
        block = tile >> 3
        dead = target == DEAD
        place = jnp.where(dead, blocks, target - blocks)
        matrix = tiles_ref[tile]
        window[place] += jnp.dot(pushed_ref[block], matrix, preferred_element_type=F32)
        left = scaled_ref[jnp.where(dead, 0, place)]
        forward[jnp.where(dead, blocks, block)] += lax.dot_general(left, matrix, LAST_DIMS, preferred_element_type=F32)

    for_tiles(table_ref, True, visit)
    kept[...] = window[0:blocks]
    forward_ref[...] = forward[0:blocks]


def embed_kernel(table_ref, tiles_ref, inverse_ref, root_ref, kept, forward_ref, odd, even, out_ref, gram_ref, forward):
    blocks, chans, width = forward_ref.shape
    forward[0:blocks] = forward_ref[...]
    forward[blocks] = jnp.zeros((chans, width), F32)

    def visit(tile, target):
        dead = target == DEAD
        from_odd = odd[jnp.where(target < blocks, 2 * blocks + target, 2 * blocks)]
        from_even = even[jnp.where((target >= 2 * blocks) & (target < 3 * blocks), target, 2 * blocks)]
        left = jnp.where(target < blocks, from_odd, from_even)
        place = jnp.where(dead, blocks, tile >> 3)
        forward[place] += lax.dot_general(left, tiles_ref[tile], LAST_DIMS, preferred_element_type=F32)

    for_tiles(table_ref, False, visit)
    root = root_ref[...]
    inverse_root = 1.0 / root
    gain = root * inverse_ref[...]
    gram = jnp.zeros((chans, chans), F32)
    for block in range(blocks):
        landing = kept[block]
        for message in (odd, even):
            landing = landing + (message[block].astype(F32) + message[blocks + block].astype(F32))
        embedded = 0.5 * (forward[block] * gain[block : block + 1] + landing * inverse_root[block : block + 1])
        out_ref[:, block * width : (block + 1) * width] = embedded
        gram += lax.dot_general(embedded, embedded, LAST_DIMS, precision=HIGHEST, preferred_element_type=F32)
    gram_ref[...] = jnp.concatenate([gram[8 * i : 8 * i + 8] for i in range(4)], axis=1)


def basis_kernel(gram_ref, embedded_ref, out_ref):
    size = embedded_ref.shape[0]
    row = lax.broadcasted_iota(jnp.int32, (size, size), 0)
    col = lax.broadcasted_iota(jnp.int32, (size, size), 1)
    identity = jnp.where(row == col, 1.0, 0.0)
    gram = jnp.sum(gram_ref[...], axis=0)
    gram = jnp.concatenate([gram[:, size * i : size * (i + 1)] for i in range(4)], axis=0)
    work = jnp.concatenate([gram, identity, jnp.zeros((size, 128 - 2 * size), F32)], axis=1)
    line = lax.broadcasted_iota(jnp.int32, work.shape, 0)
    for first in range(0, size, 4):
        columns = [jnp.broadcast_to(work[:, first + i : first + i + 1], work.shape) for i in range(4)]
        for i in range(4):
            step = first + i
            factor = jnp.where(line > step, columns[i] * (1.0 / columns[i][step : step + 1, :]), 0.0)
            work = work - factor * work[step : step + 1, :]
            for j in range(i + 1, 4):
                columns[j] = columns[j] - factor * columns[j][step : step + 1, :]
    pivots = jnp.sum(work[:, :size] * identity, axis=1, keepdims=True)
    inverse = work[:, size : 2 * size] * (1.0 / jnp.sqrt(pivots))
    out_ref[...] = jnp.dot(inverse, embedded_ref[...], precision=HIGHEST, preferred_element_type=F32)


def call(kernel, name, outs, operands, specs, scratch, out_specs=None, limit=24, flops=0, moved=0):
    return pl.pallas_call(
        kernel,
        out_shape=outs,
        in_specs=specs,
        out_specs=out_specs or [VMEM] * len(outs),
        scratch_shapes=scratch,
        compiler_params=pltpu.CompilerParams(vmem_limit_bytes=limit << 20),
        cost_estimate=pl.CostEstimate(flops=flops, bytes_accessed=moved, transcendentals=0),
        name=name,
    )(*operands)


def per_device(tile_blocks, tile_cols, tile_count, start_mass, probe_block):
    blocks, slots, width = tile_blocks.shape[:3]
    chans = probe_block.shape[0]
    zones = blocks * lax.axis_size(RING) * width

    def rows(channels=1):
        return jax.ShapeDtypeStruct((channels * blocks, width), F32)

    def window(channels, kind=F32, places=3 * blocks + 1):
        return pltpu.VMEM((places, channels, width), kind)

    tiles, target, inverse, to_odd, own, to_even = call(
        load_kernel, "load",
        [pltpu.VMEM((blocks * slots, width, width), BF16), pltpu.SMEM((blocks * slots,), jnp.int32), rows(), rows(), rows(), rows()],
        [pltpu.with_memory_space_constraint(x, pltpu.HBM) for x in (tile_cols, tile_count, tile_blocks, start_mass)],
        [pl.BlockSpec(memory_space=pltpu.HBM)] * 4,
        [
            window(blocks), pltpu.VMEM((blocks, width), F32), pltpu.SMEM(tile_cols.shape, jnp.int32),
            pltpu.SMEM(tile_count.shape, jnp.int32), pltpu.SemaphoreType.DMA((blocks,)), pltpu.SemaphoreType.DMA((2 + blocks,)),
        ],
        [VMEM, SMEM, VMEM, VMEM, VMEM, VMEM],
    )
    tiles = pltpu.with_memory_space_constraint(tiles, pltpu.VMEM)
    odd, even = ring_pairs(to_odd, to_even)
    (table,) = call(
        table_kernel, "table", [pltpu.SMEM((136,), jnp.int32)], [pltpu.with_memory_space_constraint(target, pltpu.SMEM)], [SMEM], [],
        [SMEM], flops=1 << 25, moved=1 << 22,
    )
    table = pltpu.with_memory_space_constraint(table, pltpu.SMEM)

    def step(kernel, name, channels, split, operands, extra):
        height = max(16, channels * blocks * (2 if split else 1))
        left = jax.ShapeDtypeStruct((blocks, height, width), BF16)
        to_odd, to_even, left, *extra = call(
            kernel, name, [rows(channels)] * 2 + [left] + extra, (table, tiles, inverse, *operands),
            [SMEM] + [VMEM] * (2 + len(operands)), [window(channels * blocks)], flops=1 << 24, moved=1 << 21,
        )
        odd, even = ring_pairs(to_odd, to_even)
        (own,) = call(
            functools.partial(own_kernel, split), name + "_own", [rows(channels)], (table, tiles, left), [SMEM] + [VMEM] * 2,
            [window(channels * blocks)], flops=1 << 25, moved=1 << 22,
        )
        return odd, own, even, *extra

    odd, own, even, raw = step(second_kernel, "second", 2, True, (odd, own, even), [rows()])
    odd, own, even, second = step(functools.partial(chain_kernel, 2), "third", 2, True, (odd, own, even), [rows(2)])
    odd, own, even, third = step(functools.partial(chain_kernel, 1), "fourth", 1, True, (odd, own, even), [rows(2)])
    (sums,) = call(
        sums_kernel, "sums", [jax.ShapeDtypeStruct((1, 128), F32)], (raw, second, third, odd, own, even), [VMEM] * 6, []
    )
    sums = chip_parts(sums[0])
    odd, own, even, scales = step(
        functools.partial(replay_kernel, zones), "replay_2", 1, False, (sums, raw), [jax.ShapeDtypeStruct((8, 128), F32)]
    )
    odd, own, even = step(functools.partial(again_kernel, 1), "replay_3", 1, False, (scales, odd, own, even), [])
    odd, own, even = step(functools.partial(again_kernel, 2), "replay_4", 1, False, (scales, odd, own, even), [])

    message = jax.ShapeDtypeStruct((3 * blocks, chans, width), BF16)
    narrow = jax.ShapeDtypeStruct((blocks, chans, width), BF16)
    wide = jax.ShapeDtypeStruct((blocks, chans, width), F32)
    to_odd, to_even, pushed, scaled, root = call(
        transposed_kernel, "transposed", [message, message, narrow, narrow, rows()],
        (table, tiles, inverse, scales, odd, own, even, probe_block), [SMEM] + [VMEM] * 7, [window(chans)],
    )
    odd, even = ring_pairs(to_odd, to_even)
    kept, forward = call(
        own_products_kernel, "own_products", [wide, wide], (table, tiles, pushed, scaled), [SMEM] + [VMEM] * 3,
        [window(chans, places=blocks + 1)] * 2, flops=1 << 28, moved=1 << 23,
    )
    embedded, gram = call(
        embed_kernel, "embed",
        [jax.ShapeDtypeStruct((chans, blocks * width), F32), jax.ShapeDtypeStruct((8, 128), F32)],
        (table, tiles, inverse, root, kept, forward, odd, even), [SMEM] + [VMEM] * 7, [window(chans, places=blocks + 1)],
    )
    (basis,) = call(
        basis_kernel, "basis", [jax.ShapeDtypeStruct((chans, blocks * width), F32)], (plane_parts(gram), embedded), [VMEM] * 2, []
    )
    return basis


def solution(mesh):
    return jax.shard_map(
        per_device,
        mesh=mesh,
        in_specs=(P(RING, None, None, None), P(RING, None), P(RING), P(RING), P(None, RING)),
        out_specs=P(None, RING),
        check_vma=False,
    )
```

time: 174 us -> 139 us (0.80)
  blocking collectives: 0 us -> 35 us
  waiting for transfers between devices: 47.7 us -> 16.1 us
  starting transfers between devices: 92.6 us -> 62.3 us
  local copies, waits for them, and re-layouts: 4.82 us -> 0.06 us
  Pallas kernels: 26.7 us -> 22.7 us
    all_to_all x0 -> x2, blocking collectives: none -> 35 us  [gathered(): lax.all_to_all(spread, axis, 0, 0, tiled=True, axis_index_groups=groups)]
    ppermute x42 -> x21, waiting for transfers between devices: 47.7 us -> 16.1 us  [swap(): lax.ppermute(shard, axis, [(i, partner(i) % count) for i in range(count)])]
    ppermute x42 -> x21, starting transfers between devices: 92.6 us -> 62.3 us  [swap(): lax.ppermute(shard, axis, [(i, partner(i) % count) for i in range(count)])]
    unnamed x6 -> x2, local copies, waits for them, and re-layouts: 4.04 us -> 0.01 us
    pallas_call x12 -> x19, Pallas kernels: 26.7 us -> 22.7 us  [call(): pl.pallas_call(kernel, out_shape=outs, in_specs=specs, out_specs=out_spec...]
  transfers between devices with their start and end apart: 42 -> 21, of which waited for: 24 -> 12; matrix products, arithmetic and copies ran while one was open for 0% -> 0% of each run, Pallas kernels for 2% -> 5%
where the time goes in v1:
time: 139 us; the launch traced here: 136 us
  starting transfers between devices  62.3 us (45%)
  blocking collectives  35 us (25%)
  Pallas kernels  22.7 us (16%)
  waiting for transfers between devices  16.1 us (12%)
    ppermute x21, starting transfers between devices, swap(): lax.ppermute(shard, axis, [(i, partner(i) % count) for i in range(count)])  62.3 us
    all_to_all x2, blocking collectives, gathered(): lax.all_to_all(spread, axis, 0, 0, tiled=True, axis_index_groups=groups)  35 us
    pallas_call x19, Pallas kernels, call(): pl.pallas_call(kernel, out_shape=outs, in_specs=specs, out_specs=out_spec...  22.7 us
    ppermute x21, waiting for transfers between devices, swap(): lax.ppermute(shard, axis, [(i, partner(i) % count) for i in range(count)])  16.1 us
  transfers between devices with their start and end apart: 21, of which 12 were waited for; matrix products, arithmetic and copies ran while one was open for 0% of the time, Pallas kernels for 5%

profile of v1, /device:TPU:2, one launch (start us, length us, event | category | flops | bytes accessed | tf_op | source)
XLA Modules:
  0.0 136.4 jit_solution(16963940258134031174)
XLA Ops:
  0.0 7.1 %load.1 = (bf16[64,256,256]{2,1,0:T(8,128)(2,1)S(1)}, s32[64]{0:T(128)S(4)}, f32[8,256]{1,0:T(8,128)S(1)}, f32[8,256]{1,0:T(8,128)S(1)}, f32[8,256]{1,0:T(8,128)S(1)}, /*index=5*/f32[8,256]{1,0:T(8,128)S(1)}) custom-call(s32[8,8]{1,0:T(8,128)} %cols_hbm.1, s32[8]{0:T(128)} %count_hbm.1, bf16[8,8,256,256]{3,2,1,0:T(8,128)(2,1)} %tiles_hbm.1, f32[2048]{0:T(1024)} %start_hbm.1), custom_call_target="tpu_custom_call" | custom-call | tf_op jit(solution)/shard_map/load/pallas_call | solution.py:371
  7.1 1.6 %collective-permute-start = (f32[8,256]{1,0:T(8,128)S(1)}, f32[8,256]{1,0:T(8,128)S(1)}, u32[]{:S(2)}, u32[]{:S(2)}) collective-permute-start(f32[8,256]{1,0:T(8,128)S(1)} %get-tuple-element.45), channel_id=1, source_target_pairs={{0,255},{1,2},{2,1},{3,4},{4,3},{5,6},{6,5},{7,8},{8,7},{9,10},{10... | collective-permute-start | bytes 24584 | tf_op jit(solution)/shard_map/ppermute | solution.py:27
  8.6 9.0 %collective-permute-start.1 = (f32[8,256]{1,0:T(8,128)S(1)}, f32[8,256]{1,0:T(8,128)S(1)}, u32[]{:S(2)}, u32[]{:S(2)}) collective-permute-start(f32[8,256]{1,0:T(8,128)S(1)} %get-tuple-element.47), channel_id=1, source_target_pairs={{0,1},{1,0},{2,3},{3,2},{4,5},{5,4},{6,7},{7,6},{8,9},{9,8},{10,11... | collective-permute-start | bytes 24584 | tf_op jit(solution)/shard_map/ppermute | solution.py:27
  17.6 1.6 %collective-permute-done.1.even = f32[8,256]{1,0:T(8,128)S(1)} collective-permute-done((f32[8,256]{1,0:T(8,128)S(1)}, f32[8,256]{1,0:T(8,128)S(1)}, u32[]{:S(2)}, u32[]{:S(2)}) %collective-permute-start.1) | collective-permute-done | bytes 8224 | tf_op jit(solution)/shard_map/ppermute | solution.py:27
  20.0 6.9 %collective-permute-start.3 = (f32[16,256]{1,0:T(8,128)S(1)}, f32[16,256]{1,0:T(8,128)S(1)}, u32[]{:S(2)}, u32[]{:S(2)}) collective-permute-start(f32[16,256]{1,0:T(8,128)S(1)} %get-tuple-element.51), channel_id=1, source_target_pairs={{0,1},{1,0},{2,3},{3,2},{4,5},{5,4},{6,7},{7,6},{8,9},{9,8},{10,11... | collective-permute-start | bytes 49160 | tf_op jit(solution)/shard_map/ppermute | solution.py:27
  26.9 0.9 second_own.1.own
  29.4 6.9 %collective-permute-start.5 = (f32[16,256]{1,0:T(8,128)S(1)}, f32[16,256]{1,0:T(8,128)S(1)}, u32[]{:S(2)}, u32[]{:S(2)}) collective-permute-start(f32[16,256]{1,0:T(8,128)S(1)} %get-tuple-element.55), channel_id=1, source_target_pairs={{0,1},{1,0},{2,3},{3,2},{4,5},{5,4},{6,7},{7,6},{8,9},{9,8},{10,11... | collective-permute-start | bytes 49160 | tf_op jit(solution)/shard_map/ppermute | solution.py:27
  36.3 0.9 third_own.1.own
  38.7 6.9 %collective-permute-start.7 = (f32[8,256]{1,0:T(8,128)S(1)}, f32[8,256]{1,0:T(8,128)S(1)}, u32[]{:S(2)}, u32[]{:S(2)}) collective-permute-start(f32[8,256]{1,0:T(8,128)S(1)} %get-tuple-element.59), channel_id=1, source_target_pairs={{0,1},{1,0},{2,3},{3,2},{4,5},{5,4},{6,7},{7,6},{8,9},{9,8},{10,11... | collective-permute-start | bytes 24584 | tf_op jit(solution)/shard_map/ppermute | solution.py:27
  45.6 0.8 fourth_own.1.own
  46.4 0.8 collective-permute-done.7.even
  47.3 1.1 collective-permute-done.8
  48.5 20.7 %all_to_all.13 = f32[128,1,128]{2,1,0:T(1,128)S(1)} all-to-all(f32[128,1,128]{2,1,0:T(1,128)S(1)} %broadcast_in_dim.4), channel_id=1, replica_groups={{0,1,2,3,8,9,10,11,16,17,18,19,24,25,26,27,32,33,34,35,40,41,42,43,48,4..., dimensions={0} | all-to-all | bytes 131072 | tf_op jit(solution)/shard_map/all_to_all | solution.py:38
  70.1 1.5 %collective-permute-start.10 = (f32[8,256]{1,0:T(8,128)S(1)}, f32[8,256]{1,0:T(8,128)S(1)}, u32[]{:S(2)}, u32[]{:S(2)}) collective-permute-start(f32[8,256]{1,0:T(8,128)S(1)} %get-tuple-element.63), channel_id=1, source_target_pairs={{0,1},{1,0},{2,3},{3,2},{4,5},{5,4},{6,7},{7,6},{8,9},{9,8},{10,11... | collective-permute-start | bytes 24584 | tf_op jit(solution)/shard_map/ppermute | solution.py:27
  71.6 0.8 replay_2_own.1.own
  72.5 1.3 collective-permute-done.9.odd
  74.5 2.0 %collective-permute-start.11 = (f32[8,256]{1,0:T(8,128)S(1)}, f32[8,256]{1,0:T(8,128)S(1)}, u32[]{:S(2)}, u32[]{:S(2)}) collective-permute-start(f32[8,256]{1,0:T(8,128)S(1)} %get-tuple-element.64), channel_id=1, source_target_pairs={{0,255},{1,2},{2,1},{3,4},{4,3},{5,6},{6,5},{7,8},{8,7},{9,10},{10... | collective-permute-start | bytes 24584 | tf_op jit(solution)/shard_map/ppermute | solution.py:27
  76.5 5.5 %collective-permute-start.12 = (f32[8,256]{1,0:T(8,128)S(1)}, f32[8,256]{1,0:T(8,128)S(1)}, u32[]{:S(2)}, u32[]{:S(2)}) collective-permute-start(f32[8,256]{1,0:T(8,128)S(1)} %get-tuple-element.66), channel_id=1, source_target_pairs={{0,1},{1,0},{2,3},{3,2},{4,5},{5,4},{6,7},{7,6},{8,9},{9,8},{10,11... | collective-permute-start | bytes 24584 | tf_op jit(solution)/shard_map/ppermute | solution.py:27
  81.9 0.8 replay_3_own.1.own
  84.3 6.9 %collective-permute-start.14 = (f32[8,256]{1,0:T(8,128)S(1)}, f32[8,256]{1,0:T(8,128)S(1)}, u32[]{:S(2)}, u32[]{:S(2)}) collective-permute-start(f32[8,256]{1,0:T(8,128)S(1)} %get-tuple-element.69), channel_id=1, source_target_pairs={{0,1},{1,0},{2,3},{3,2},{4,5},{5,4},{6,7},{7,6},{8,9},{9,8},{10,11... | collective-permute-start | bytes 24584 | tf_op jit(solution)/shard_map/ppermute | solution.py:27
  91.2 0.8 replay_4_own.1.own
  92.0 0.9 collective-permute-done.14.even
  93.7 7.2 %collective-permute-start.16 = (bf16[24,32,256]{2,1,0:T(8,128)(2,1)S(1)}, bf16[24,32,256]{2,1,0:T(8,128)(2,1)S(1)}, u32[]{:S(2)}, u32[]{:S(2)}) collective-permute-start(bf16[24,32,256]{2,1,0:T(8,128)(2,1)S(1)} %get-tuple-element.76), channel_id=1, source_target_pairs={{0,1},{1,0},{2,3},{3,2},{4,5},{5,4},{6,7},{7,6},{8,9},{9,8},{10,11... | collective-permute-start | bytes 1179656 | tf_op jit(solution)/shard_map/ppermute | solution.py:27
  100.9 1.9 %own_products.1 = (f32[8,32,256]{2,1,0:T(8,128)S(1)}, f32[8,32,256]{2,1,0:T(8,128)S(1)}) custom-call(s32[136]{0:T(256)S(4)} %table.1.table_ref, bf16[64,256,256]{2,1,0:T(8,128)(2,1)S(1)} %get-tuple-element.43.tiles_ref, bf16[8,32,256]{2,1,0:T(8,128)(2,1)S(1)} %get-tuple-element.71.pushed_ref, bf16[8,32,256]{2,1,0:T(8,128)(2,1)S(1)} %get-tuple-element.72.scaled_ref), custom_call_target="tpu_custom_call" | custom-call | flops 268435456 | bytes 8388608 | tf_op jit(solution)/shard_map/own_products/pallas_call | solution.py:371
  102.9 3.8 %collective-permute-done.16.even = bf16[24,32,256]{2,1,0:T(8,128)(2,1)S(1)} collective-permute-done((bf16[24,32,256]{2,1,0:T(8,128)(2,1)S(1)}, bf16[24,32,256]{2,1,0:T(8,128)(2,1)S(1)}, u32[]{:S(2)}, u32[]{:S(2)}) %collective-permute-start.16) | collective-permute-done | bytes 393248 | tf_op jit(solution)/shard_map/ppermute | solution.py:27
  106.7 1.3 embed.1
  108.1 1.2 collective-permute-done.17
  109.2 5.3 %collective-permute-start.19 = (f32[8,128]{1,0:T(8,128)S(1)}, f32[8,128]{1,0:T(8,128)S(1)}, u32[]{:S(2)}, u32[]{:S(2)}) collective-permute-start(f32[8,128]{1,0:T(8,128)S(1)} %add.16), channel_id=1, source_target_pairs={{0,1},{1,0},{2,3},{3,2},{4,5},{5,4},{6,7},{7,6},{8,9},{9,8},{10,11... | collective-permute-start | bytes 12296 | tf_op jit(solution)/shard_map/ppermute | solution.py:27
  114.5 2.1 %collective-permute-start.18 = (f32[8,128]{1,0:T(8,128)S(1)}, f32[8,128]{1,0:T(8,128)S(1)}, u32[]{:S(2)}, u32[]{:S(2)}) collective-permute-start(f32[8,128]{1,0:T(8,128)S(1)} %add.16), channel_id=1, source_target_pairs={{0,2},{1,3},{2,0},{3,1},{4,6},{5,7},{6,4},{7,5},{8,10},{9,11},{10,... | collective-permute-start | bytes 12296 | tf_op jit(solution)/shard_map/ppermute | solution.py:27
  116.6 3.0 %collective-permute-done.18 = f32[8,128]{1,0:T(8,128)S(1)} collective-permute-done((f32[8,128]{1,0:T(8,128)S(1)}, f32[8,128]{1,0:T(8,128)S(1)}, u32[]{:S(2)}, u32[]{:S(2)}) %collective-permute-start.18) | collective-permute-done | bytes 4128 | tf_op jit(solution)/shard_map/ppermute | solution.py:27
  119.7 14.2 %all_to_all.14.gram_ref = f32[32,8,128]{2,1,0:T(8,128)S(1)} all-to-all(f32[32,8,128]{2,1,0:T(8,128)S(1)} %broadcast_in_dim.5), channel_id=1, replica_groups={{0,8,16,24,32,40,48,56,64,72,80,88,96,104,112,120,128,136,144,152,160,1..., dimensions={0} | all-to-all | bytes 262144 | tf_op jit(solution)/shard_map/all_to_all | solution.py:38
  133.9 2.5 %basis.1 = f32[32,2048]{1,0:T(8,128)} custom-call(f32[32,8,128]{2,1,0:T(8,128)S(1)} %all_to_all.14.gram_ref, f32[32,2048]{1,0:T(8,128)S(1)} %get-tuple-element.78.embedded_ref), custom_call_target="tpu_custom_call" | custom-call | tf_op jit(solution)/shard_map/basis/pallas_call | solution.py:371
  (38 shorter events, 8.0 us)
Async XLA Ops:
  7.1 10.6 %collective-permute-start = (f32[8,256]{1,0:T(8,128)S(1)}, f32[8,256]{1,0:T(8,128)S(1)}, u32[]{:S(2)}, u32[]{:S(2)}) collective-permute-start(f32[8,256]{1,0:T(8,128)S(1)} %get-tuple-element.45), channel_id=1, source_target_pairs={{0,255},{1,2},{2,1},{3,4},{4,3},{5,6},{6,5},{7,8},{8,7},{9,10},{10... | collective-permute-start | bytes 24584 | tf_op jit(solution)/shard_map/ppermute | solution.py:27
  8.6 10.6 %collective-permute-start.1 = (f32[8,256]{1,0:T(8,128)S(1)}, f32[8,256]{1,0:T(8,128)S(1)}, u32[]{:S(2)}, u32[]{:S(2)}) collective-permute-start(f32[8,256]{1,0:T(8,128)S(1)} %get-tuple-element.47), channel_id=1, source_target_pairs={{0,1},{1,0},{2,3},{3,2},{4,5},{5,4},{6,7},{7,6},{8,9},{9,8},{10,11... | collective-permute-start | bytes 24584 | tf_op jit(solution)/shard_map/ppermute | solution.py:27
  19.9 7.9 %collective-permute-start.2 = (f32[16,256]{1,0:T(8,128)S(1)}, f32[16,256]{1,0:T(8,128)S(1)}, u32[]{:S(2)}, u32[]{:S(2)}) collective-permute-start(f32[16,256]{1,0:T(8,128)S(1)} %get-tuple-element.49), channel_id=1, source_target_pairs={{0,255},{1,2},{2,1},{3,4},{4,3},{5,6},{6,5},{7,8},{8,7},{9,10},{10... | collective-permute-start | bytes 49160 | tf_op jit(solution)/shard_map/ppermute | solution.py:27
  20.0 8.6 %collective-permute-start.3 = (f32[16,256]{1,0:T(8,128)S(1)}, f32[16,256]{1,0:T(8,128)S(1)}, u32[]{:S(2)}, u32[]{:S(2)}) collective-permute-start(f32[16,256]{1,0:T(8,128)S(1)} %get-tuple-element.51), channel_id=1, source_target_pairs={{0,1},{1,0},{2,3},{3,2},{4,5},{5,4},{6,7},{7,6},{8,9},{9,8},{10,11... | collective-permute-start | bytes 49160 | tf_op jit(solution)/shard_map/ppermute | solution.py:27
  29.3 7.9 %collective-permute-start.4 = (f32[16,256]{1,0:T(8,128)S(1)}, f32[16,256]{1,0:T(8,128)S(1)}, u32[]{:S(2)}, u32[]{:S(2)}) collective-permute-start(f32[16,256]{1,0:T(8,128)S(1)} %get-tuple-element.53), channel_id=1, source_target_pairs={{0,255},{1,2},{2,1},{3,4},{4,3},{5,6},{6,5},{7,8},{8,7},{9,10},{10... | collective-permute-start | bytes 49160 | tf_op jit(solution)/shard_map/ppermute | solution.py:27
  29.4 8.6 %collective-permute-start.5 = (f32[16,256]{1,0:T(8,128)S(1)}, f32[16,256]{1,0:T(8,128)S(1)}, u32[]{:S(2)}, u32[]{:S(2)}) collective-permute-start(f32[16,256]{1,0:T(8,128)S(1)} %get-tuple-element.55), channel_id=1, source_target_pairs={{0,1},{1,0},{2,3},{3,2},{4,5},{5,4},{6,7},{7,6},{8,9},{9,8},{10,11... | collective-permute-start | bytes 49160 | tf_op jit(solution)/shard_map/ppermute | solution.py:27
  38.6 7.8 %collective-permute-start.6 = (f32[8,256]{1,0:T(8,128)S(1)}, f32[8,256]{1,0:T(8,128)S(1)}, u32[]{:S(2)}, u32[]{:S(2)}) collective-permute-start(f32[8,256]{1,0:T(8,128)S(1)} %get-tuple-element.57), channel_id=1, source_target_pairs={{0,255},{1,2},{2,1},{3,4},{4,3},{5,6},{6,5},{7,8},{8,7},{9,10},{10... | collective-permute-start | bytes 24584 | tf_op jit(solution)/shard_map/ppermute | solution.py:27
  38.7 8.5 %collective-permute-start.7 = (f32[8,256]{1,0:T(8,128)S(1)}, f32[8,256]{1,0:T(8,128)S(1)}, u32[]{:S(2)}, u32[]{:S(2)}) collective-permute-start(f32[8,256]{1,0:T(8,128)S(1)} %get-tuple-element.59), channel_id=1, source_target_pairs={{0,1},{1,0},{2,3},{3,2},{4,5},{5,4},{6,7},{7,6},{8,9},{9,8},{10,11... | collective-permute-start | bytes 24584 | tf_op jit(solution)/shard_map/ppermute | solution.py:27
  47.3 1.1 collective-permute-start.8
  70.0 3.7 %collective-permute-start.9 = (f32[8,256]{1,0:T(8,128)S(1)}, f32[8,256]{1,0:T(8,128)S(1)}, u32[]{:S(2)}, u32[]{:S(2)}) collective-permute-start(f32[8,256]{1,0:T(8,128)S(1)} %get-tuple-element.61), channel_id=1, source_target_pairs={{0,255},{1,2},{2,1},{3,4},{4,3},{5,6},{6,5},{7,8},{8,7},{9,10},{10... | collective-permute-start | bytes 24584 | tf_op jit(solution)/shard_map/ppermute | solution.py:27
  70.1 3.7 %collective-permute-start.10 = (f32[8,256]{1,0:T(8,128)S(1)}, f32[8,256]{1,0:T(8,128)S(1)}, u32[]{:S(2)}, u32[]{:S(2)}) collective-permute-start(f32[8,256]{1,0:T(8,128)S(1)} %get-tuple-element.63), channel_id=1, source_target_pairs={{0,1},{1,0},{2,3},{3,2},{4,5},{5,4},{6,7},{7,6},{8,9},{9,8},{10,11... | collective-permute-start | bytes 24584 | tf_op jit(solution)/shard_map/ppermute | solution.py:27
  74.5 8.3 %collective-permute-start.11 = (f32[8,256]{1,0:T(8,128)S(1)}, f32[8,256]{1,0:T(8,128)S(1)}, u32[]{:S(2)}, u32[]{:S(2)}) collective-permute-start(f32[8,256]{1,0:T(8,128)S(1)} %get-tuple-element.64), channel_id=1, source_target_pairs={{0,255},{1,2},{2,1},{3,4},{4,3},{5,6},{6,5},{7,8},{8,7},{9,10},{10... | collective-permute-start | bytes 24584 | tf_op jit(solution)/shard_map/ppermute | solution.py:27
  76.5 7.1 %collective-permute-start.12 = (f32[8,256]{1,0:T(8,128)S(1)}, f32[8,256]{1,0:T(8,128)S(1)}, u32[]{:S(2)}, u32[]{:S(2)}) collective-permute-start(f32[8,256]{1,0:T(8,128)S(1)} %get-tuple-element.66), channel_id=1, source_target_pairs={{0,1},{1,0},{2,3},{3,2},{4,5},{5,4},{6,7},{7,6},{8,9},{9,8},{10,11... | collective-permute-start | bytes 24584 | tf_op jit(solution)/shard_map/ppermute | solution.py:27
  82.7 10.1 %copy-start = (bf16[32,2048]{1,0:T(8,128)(2,1)S(1)}, bf16[32,2048]{1,0:T(8,128)(2,1)}, u32[]{:S(2)}) copy-start(bf16[32,2048]{1,0:T(8,128)(2,1)} %probe_ref.1) | copy-start | bytes 393220
  84.2 7.8 %collective-permute-start.13 = (f32[8,256]{1,0:T(8,128)S(1)}, f32[8,256]{1,0:T(8,128)S(1)}, u32[]{:S(2)}, u32[]{:S(2)}) collective-permute-start(f32[8,256]{1,0:T(8,128)S(1)} %get-tuple-element.67), channel_id=1, source_target_pairs={{0,255},{1,2},{2,1},{3,4},{4,3},{5,6},{6,5},{7,8},{8,7},{9,10},{10... | collective-permute-start | bytes 24584 | tf_op jit(solution)/shard_map/ppermute | solution.py:27
  84.3 8.6 %collective-permute-start.14 = (f32[8,256]{1,0:T(8,128)S(1)}, f32[8,256]{1,0:T(8,128)S(1)}, u32[]{:S(2)}, u32[]{:S(2)}) collective-permute-start(f32[8,256]{1,0:T(8,128)S(1)} %get-tuple-element.69), channel_id=1, source_target_pairs={{0,1},{1,0},{2,3},{3,2},{4,5},{5,4},{6,7},{7,6},{8,9},{9,8},{10,11... | collective-permute-start | bytes 24584 | tf_op jit(solution)/shard_map/ppermute | solution.py:27
  93.6 9.2 %collective-permute-start.15 = (bf16[24,32,256]{2,1,0:T(8,128)(2,1)S(1)}, bf16[24,32,256]{2,1,0:T(8,128)(2,1)S(1)}, u32[]{:S(2)}, u32[]{:S(2)}) collective-permute-start(bf16[24,32,256]{2,1,0:T(8,128)(2,1)S(1)} %get-tuple-element.75), channel_id=1, source_target_pairs={{0,255},{1,2},{2,1},{3,4},{4,3},{5,6},{6,5},{7,8},{8,7},{9,10},{10... | collective-permute-start | bytes 1179656 | tf_op jit(solution)/shard_map/ppermute | solution.py:27
  93.7 12.9 %collective-permute-start.16 = (bf16[24,32,256]{2,1,0:T(8,128)(2,1)S(1)}, bf16[24,32,256]{2,1,0:T(8,128)(2,1)S(1)}, u32[]{:S(2)}, u32[]{:S(2)}) collective-permute-start(bf16[24,32,256]{2,1,0:T(8,128)(2,1)S(1)} %get-tuple-element.76), channel_id=1, source_target_pairs={{0,1},{1,0},{2,3},{3,2},{4,5},{5,4},{6,7},{7,6},{8,9},{9,8},{10,11... | collective-permute-start | bytes 1179656 | tf_op jit(solution)/shard_map/ppermute | solution.py:27
  108.0 1.2 collective-permute-start.17
  109.2 7.4 %collective-permute-start.20 = (f32[8,128]{1,0:T(8,128)S(1)}, f32[8,128]{1,0:T(8,128)S(1)}, u32[]{:S(2)}, u32[]{:S(2)}) collective-permute-start(f32[8,128]{1,0:T(8,128)S(1)} %add.16), channel_id=1, source_target_pairs={{0,3},{1,2},{2,1},{3,0},{4,7},{5,6},{6,5},{7,4},{8,11},{9,10},{10,... | collective-permute-start | bytes 12296 | tf_op jit(solution)/shard_map/ppermute | solution.py:27
  109.2 7.4 %collective-permute-start.19 = (f32[8,128]{1,0:T(8,128)S(1)}, f32[8,128]{1,0:T(8,128)S(1)}, u32[]{:S(2)}, u32[]{:S(2)}) collective-permute-start(f32[8,128]{1,0:T(8,128)S(1)} %add.16), channel_id=1, source_target_pairs={{0,1},{1,0},{2,3},{3,2},{4,5},{5,4},{6,7},{7,6},{8,9},{9,8},{10,11... | collective-permute-start | bytes 12296 | tf_op jit(solution)/shard_map/ppermute | solution.py:27
  114.5 5.1 %collective-permute-start.18 = (f32[8,128]{1,0:T(8,128)S(1)}, f32[8,128]{1,0:T(8,128)S(1)}, u32[]{:S(2)}, u32[]{:S(2)}) collective-permute-start(f32[8,128]{1,0:T(8,128)S(1)} %add.16), channel_id=1, source_target_pairs={{0,2},{1,3},{2,0},{3,1},{4,6},{5,7},{6,4},{7,5},{8,10},{9,11},{10,... | collective-permute-start | bytes 12296 | tf_op jit(solution)/shard_map/ppermute | solution.py:27

commit v2 on v1

--- a/solution.py
+++ b/solution.py
@@ -257,18 +257,31 @@
     return scale_1, scale_2, scale_3, scale_4
 
 
-def replay_kernel(zones, table_ref, tiles_ref, inverse_ref, sums_ref, raw_ref, to_odd, to_even, left_ref, scales_ref, window):
+def replay_kernel(zones, table_ref, tiles_ref, inverse_ref, sums_ref, raw_ref, second_ref, third_ref, to_odd, to_even, left_ref,
+                  scales_ref, window):
     scales = scales_of(sums_ref[...], zones)
     for place, scale in enumerate(scales):
         scales_ref[place : place + 1, :] = jnp.broadcast_to(scale, (1, 128))
-    rows = (raw_ref[...] * scales[0]) * inverse_ref[...]
-    halo_step(rows, False, table_ref, tiles_ref, to_odd, to_even, left_ref, window)
-
-
-def again_kernel(place, table_ref, tiles_ref, inverse_ref, scales_ref, odd, own, even, to_odd, to_even, left_ref, window):
-    raw = 0.85 * (own[...] + odd[...] + even[...]) + 0.15
-    rows = (raw * scales_ref[place : place + 1, 0:1]) * inverse_ref[...]
-    halo_step(rows, False, table_ref, tiles_ref, to_odd, to_even, left_ref, window)
+    inverse = inverse_ref[...]
+    blocks = inverse.shape[0]
+    a2 = 0.85 * scales[0]
+    a3 = 0.85 * scales[1]
+
+    def own_products(rows):
+        spread_blocks(rows, left_ref)
+        push_rows(table_ref, True, tiles_ref, left_ref, window, False)
+        return jnp.sum(window[blocks : 2 * blocks], axis=1)
+
+    def rounded(rows):
+        return rows.astype(BF16).astype(F32)
+
+    plain_2 = (raw_ref[...] * scales[0]) * inverse
+    chain_2 = a2 * second_ref[0:blocks] + 0.15
+    raw_2 = chain_2 + 0.85 * own_products(rounded(plain_2) - plain_2)
+    chain_3 = a3 * (a2 * third_ref[0:blocks] + 0.15 * second_ref[blocks : 2 * blocks]) + 0.15
+    weights_3 = rounded((raw_2 * scales[1]) * inverse)
+    raw_3 = chain_3 + 0.85 * own_products(weights_3 - (chain_2 * scales[1]) * inverse)
+    halo_step((raw_3 * scales[2]) * inverse, False, table_ref, tiles_ref, to_odd, to_even, left_ref, window)
 
 
 def transposed_kernel(table_ref, tiles_ref, inverse_ref, scales_ref, odd, own, even, probe_ref, to_odd, to_even, pushed_ref, scaled_ref, root_ref, window):
@@ -432,10 +445,9 @@
     )
     sums = chip_parts(sums[0])
     odd, own, even, scales = step(
-        functools.partial(replay_kernel, zones), "replay_2", 1, False, (sums, raw), [jax.ShapeDtypeStruct((8, 128), F32)]
-    )
-    odd, own, even = step(functools.partial(again_kernel, 1), "replay_3", 1, False, (scales, odd, own, even), [])
-    odd, own, even = step(functools.partial(again_kernel, 2), "replay_4", 1, False, (scales, odd, own, even), [])
+        functools.partial(replay_kernel, zones), "replay", 1, False, (sums, raw, second, third),
+        [jax.ShapeDtypeStruct((8, 128), F32)],
+    )
 
     message = jax.ShapeDtypeStruct((3 * blocks, chans, width), BF16)
     narrow = jax.ShapeDtypeStruct((blocks, chans, width), BF16)

time: 139 us -> 121 us (0.87)
  starting transfers between devices: 62.3 us -> 48.6 us
  waiting for transfers between devices: 16.1 us -> 12.8 us
    ppermute x21 -> x17, starting transfers between devices: 62.3 us -> 48.6 us  [swap(): lax.ppermute(shard, axis, [(i, partner(i) % count) for i in range(count)])]
    ppermute x21 -> x17, waiting for transfers between devices: 16.1 us -> 12.8 us  [swap(): lax.ppermute(shard, axis, [(i, partner(i) % count) for i in range(count)])]
    pallas_call x19 -> x15, Pallas kernels: 22.7 us -> 23.7 us  [call(): pl.pallas_call(kernel, out_shape=outs, in_specs=specs, out_specs=out_spec...]
  transfers between devices with their start and end apart: 21 -> 17, of which waited for: 12 -> 11; matrix products, arithmetic and copies ran while one was open for 0% -> 0% of each run, Pallas kernels for 5% -> 6%
where the time goes in v2:
time: 121 us; the launch traced here: 119 us
  starting transfers between devices  48.6 us (40%)
  blocking collectives  34.2 us (28%)
  Pallas kernels  23.7 us (20%)
  waiting for transfers between devices  12.8 us (11%)
    ppermute x17, starting transfers between devices, swap(): lax.ppermute(shard, axis, [(i, partner(i) % count) for i in range(count)])  48.6 us
    all_to_all x2, blocking collectives, gathered(): lax.all_to_all(spread, axis, 0, 0, tiled=True, axis_index_groups=groups)  34.2 us
    pallas_call x15, Pallas kernels, call(): pl.pallas_call(kernel, out_shape=outs, in_specs=specs, out_specs=out_spec...  23.7 us
    ppermute x17, waiting for transfers between devices, swap(): lax.ppermute(shard, axis, [(i, partner(i) % count) for i in range(count)])  12.8 us
  transfers between devices with their start and end apart: 17, of which 11 were waited for; matrix products, arithmetic and copies ran while one was open for 0% of the time, Pallas kernels for 6%

profile of v2, /device:TPU:2, one launch (start us, length us, event | category | flops | bytes accessed | tf_op | source)
XLA Modules:
  0.0 119.4 jit_solution(207866122361805304)
XLA Ops:
  0.0 7.1 %load.1 = (bf16[64,256,256]{2,1,0:T(8,128)(2,1)S(1)}, s32[64]{0:T(128)S(4)}, f32[8,256]{1,0:T(8,128)S(1)}, f32[8,256]{1,0:T(8,128)S(1)}, f32[8,256]{1,0:T(8,128)S(1)}, /*index=5*/f32[8,256]{1,0:T(8,128)S(1)}) custom-call(s32[8,8]{1,0:T(8,128)} %cols_hbm.1, s32[8]{0:T(128)} %count_hbm.1, bf16[8,8,256,256]{3,2,1,0:T(8,128)(2,1)} %tiles_hbm.1, f32[2048]{0:T(1024)} %start_hbm.1), custom_call_target="tpu_custom_call" | custom-call | tf_op jit(solution)/shard_map/load/pallas_call | solution.py:384
  7.1 1.6 %collective-permute-start = (f32[8,256]{1,0:T(8,128)S(1)}, f32[8,256]{1,0:T(8,128)S(1)}, u32[]{:S(2)}, u32[]{:S(2)}) collective-permute-start(f32[8,256]{1,0:T(8,128)S(1)} %get-tuple-element.39), channel_id=1, source_target_pairs={{0,255},{1,2},{2,1},{3,4},{4,3},{5,6},{6,5},{7,8},{8,7},{9,10},{10... | collective-permute-start | bytes 24584 | tf_op jit(solution)/shard_map/ppermute | solution.py:27
  8.6 9.0 %collective-permute-start.1 = (f32[8,256]{1,0:T(8,128)S(1)}, f32[8,256]{1,0:T(8,128)S(1)}, u32[]{:S(2)}, u32[]{:S(2)}) collective-permute-start(f32[8,256]{1,0:T(8,128)S(1)} %get-tuple-element.41), channel_id=1, source_target_pairs={{0,1},{1,0},{2,3},{3,2},{4,5},{5,4},{6,7},{7,6},{8,9},{9,8},{10,11... | collective-permute-start | bytes 24584 | tf_op jit(solution)/shard_map/ppermute | solution.py:27
  17.6 1.6 %collective-permute-done.1.even = f32[8,256]{1,0:T(8,128)S(1)} collective-permute-done((f32[8,256]{1,0:T(8,128)S(1)}, f32[8,256]{1,0:T(8,128)S(1)}, u32[]{:S(2)}, u32[]{:S(2)}) %collective-permute-start.1) | collective-permute-done | bytes 8224 | tf_op jit(solution)/shard_map/ppermute | solution.py:27
  19.3 0.7 second.1
  20.0 6.6 %collective-permute-start.3 = (f32[16,256]{1,0:T(8,128)S(1)}, f32[16,256]{1,0:T(8,128)S(1)}, u32[]{:S(2)}, u32[]{:S(2)}) collective-permute-start(f32[16,256]{1,0:T(8,128)S(1)} %get-tuple-element.45), channel_id=1, source_target_pairs={{0,1},{1,0},{2,3},{3,2},{4,5},{5,4},{6,7},{7,6},{8,9},{9,8},{10,11... | collective-permute-start | bytes 49160 | tf_op jit(solution)/shard_map/ppermute | solution.py:27
  26.6 1.2 %second_own.1.own = f32[16,256]{1,0:T(8,128)S(1)} custom-call(s32[136]{0:T(256)S(4)} %table.1.table_ref, bf16[64,256,256]{2,1,0:T(8,128)(2,1)S(1)} %get-tuple-element.37.tiles_ref, bf16[8,32,256]{2,1,0:T(8,128)(2,1)S(1)} %get-tuple-element.44.left_ref), custom_call_target="tpu_custom_call" | custom-call | flops 33554432 | bytes 4194304 | tf_op jit(solution)/shard_map/second_own/pallas_call | solution.py:384
  27.9 0.6 collective-permute-done.3.even
  28.5 0.7 third.1
  29.3 6.4 %collective-permute-start.5 = (f32[16,256]{1,0:T(8,128)S(1)}, f32[16,256]{1,0:T(8,128)S(1)}, u32[]{:S(2)}, u32[]{:S(2)}) collective-permute-start(f32[16,256]{1,0:T(8,128)S(1)} %get-tuple-element.49), channel_id=1, source_target_pairs={{0,1},{1,0},{2,3},{3,2},{4,5},{5,4},{6,7},{7,6},{8,9},{9,8},{10,11... | collective-permute-start | bytes 49160 | tf_op jit(solution)/shard_map/ppermute | solution.py:27
  35.7 1.2 %third_own.1.own = f32[16,256]{1,0:T(8,128)S(1)} custom-call(s32[136]{0:T(256)S(4)} %table.1.table_ref, bf16[64,256,256]{2,1,0:T(8,128)(2,1)S(1)} %get-tuple-element.37.tiles_ref, bf16[8,32,256]{2,1,0:T(8,128)(2,1)S(1)} %get-tuple-element.48.left_ref), custom_call_target="tpu_custom_call" | custom-call | flops 33554432 | bytes 4194304 | tf_op jit(solution)/shard_map/third_own/pallas_call | solution.py:384
  37.5 0.6 fourth.1
  38.2 6.5 %collective-permute-start.7 = (f32[8,256]{1,0:T(8,128)S(1)}, f32[8,256]{1,0:T(8,128)S(1)}, u32[]{:S(2)}, u32[]{:S(2)}) collective-permute-start(f32[8,256]{1,0:T(8,128)S(1)} %get-tuple-element.53), channel_id=1, source_target_pairs={{0,1},{1,0},{2,3},{3,2},{4,5},{5,4},{6,7},{7,6},{8,9},{9,8},{10,11... | collective-permute-start | bytes 24584 | tf_op jit(solution)/shard_map/ppermute | solution.py:27
  44.7 1.1 fourth_own.1.own
  46.5 1.1 collective-permute-done.8
  47.6 20.7 %all_to_all.13 = f32[128,1,128]{2,1,0:T(1,128)S(1)} all-to-all(f32[128,1,128]{2,1,0:T(1,128)S(1)} %broadcast_in_dim.4), channel_id=1, replica_groups={{0,1,2,3,8,9,10,11,16,17,18,19,24,25,26,27,32,33,34,35,40,41,42,43,48,4..., dimensions={0} | all-to-all | bytes 131072 | tf_op jit(solution)/shard_map/all_to_all | solution.py:38
  68.3 2.9 %replay.1 = (f32[8,256]{1,0:T(8,128)S(1)}, f32[8,256]{1,0:T(8,128)S(1)}, bf16[8,16,256]{2,1,0:T(8,128)(2,1)S(1)}, f32[8,128]{1,0:T(8,128)S(1)}) custom-call(s32[136]{0:T(256)S(4)} %table.1.table_ref, bf16[64,256,256]{2,1,0:T(8,128)(2,1)S(1)} %get-tuple-element.37.tiles_ref, f32[8,256]{1,0:T(8,128)S(1)} %get-tuple-element.38.inverse_ref, ...), custom_call_target="tpu_custom_call" | custom-call | flops 16777216 | bytes 2097152 | tf_op jit(solution)/shard_map/replay/pallas_call | solution.py:384
  71.4 1.8 %collective-permute-start.10 = (f32[8,256]{1,0:T(8,128)S(1)}, f32[8,256]{1,0:T(8,128)S(1)}, u32[]{:S(2)}, u32[]{:S(2)}) collective-permute-start(f32[8,256]{1,0:T(8,128)S(1)} %get-tuple-element.57), channel_id=1, source_target_pairs={{0,1},{1,0},{2,3},{3,2},{4,5},{5,4},{6,7},{7,6},{8,9},{9,8},{10,11... | collective-permute-start | bytes 24584 | tf_op jit(solution)/shard_map/ppermute | solution.py:27
  73.2 1.1 replay_own.1.own
  74.3 0.8 collective-permute-done.9.odd
  75.1 0.8 transposed.1
  75.9 2.0 %collective-permute-start.11 = (bf16[24,32,256]{2,1,0:T(8,128)(2,1)S(1)}, bf16[24,32,256]{2,1,0:T(8,128)(2,1)S(1)}, u32[]{:S(2)}, u32[]{:S(2)}) collective-permute-start(bf16[24,32,256]{2,1,0:T(8,128)(2,1)S(1)} %get-tuple-element.63), channel_id=1, source_target_pairs={{0,255},{1,2},{2,1},{3,4},{4,3},{5,6},{6,5},{7,8},{8,7},{9,10},{10... | collective-permute-start | bytes 1179656 | tf_op jit(solution)/shard_map/ppermute | solution.py:27
  77.9 5.4 %collective-permute-start.12 = (bf16[24,32,256]{2,1,0:T(8,128)(2,1)S(1)}, bf16[24,32,256]{2,1,0:T(8,128)(2,1)S(1)}, u32[]{:S(2)}, u32[]{:S(2)}) collective-permute-start(bf16[24,32,256]{2,1,0:T(8,128)(2,1)S(1)} %get-tuple-element.64), channel_id=1, source_target_pairs={{0,1},{1,0},{2,3},{3,2},{4,5},{5,4},{6,7},{7,6},{8,9},{9,8},{10,11... | collective-permute-start | bytes 1179656 | tf_op jit(solution)/shard_map/ppermute | solution.py:27
  83.3 2.5 %own_products.1 = (f32[8,32,256]{2,1,0:T(8,128)S(1)}, f32[8,32,256]{2,1,0:T(8,128)S(1)}) custom-call(s32[136]{0:T(256)S(4)} %table.1.table_ref, bf16[64,256,256]{2,1,0:T(8,128)(2,1)S(1)} %get-tuple-element.37.tiles_ref, bf16[8,32,256]{2,1,0:T(8,128)(2,1)S(1)} %get-tuple-element.59.pushed_ref, bf16[8,32,256]{2,1,0:T(8,128)(2,1)S(1)} %get-tuple-element.60.scaled_ref), custom_call_target="tpu_custom_call" | custom-call | flops 268435456 | bytes 8388608 | tf_op jit(solution)/shard_map/own_products/pallas_call | solution.py:384
  86.3 2.8 %collective-permute-done.12.even = bf16[24,32,256]{2,1,0:T(8,128)(2,1)S(1)} collective-permute-done((bf16[24,32,256]{2,1,0:T(8,128)(2,1)S(1)}, bf16[24,32,256]{2,1,0:T(8,128)(2,1)S(1)}, u32[]{:S(2)}, u32[]{:S(2)}) %collective-permute-start.12) | collective-permute-done | bytes 393248 | tf_op jit(solution)/shard_map/ppermute | solution.py:27
  89.1 1.3 %embed.1 = (f32[32,2048]{1,0:T(8,128)S(1)}, f32[8,128]{1,0:T(8,128)S(1)}) custom-call(s32[136]{0:T(256)S(4)} %table.1.table_ref, bf16[64,256,256]{2,1,0:T(8,128)(2,1)S(1)} %get-tuple-element.37.tiles_ref, f32[8,256]{1,0:T(8,128)S(1)} %get-tuple-element.38.inverse_ref, f32[8,256]{1,0:T(8,128)S(1)} %get-tuple-element.58.root_ref, ...), custom_call_target="tpu_custom_call" | custom-call | tf_op jit(solution)/shard_map/embed/pallas_call | solution.py:384
  90.5 1.2 collective-permute-done.13
  92.2 6.2 %collective-permute-start.15 = (f32[8,128]{1,0:T(8,128)S(1)}, f32[8,128]{1,0:T(8,128)S(1)}, u32[]{:S(2)}, u32[]{:S(2)}) collective-permute-start(f32[8,128]{1,0:T(8,128)S(1)} %add.16), channel_id=1, source_target_pairs={{0,1},{1,0},{2,3},{3,2},{4,5},{5,4},{6,7},{7,6},{8,9},{9,8},{10,11... | collective-permute-start | bytes 12296 | tf_op jit(solution)/shard_map/ppermute | solution.py:27
  98.4 2.1 %collective-permute-start.14 = (f32[8,128]{1,0:T(8,128)S(1)}, f32[8,128]{1,0:T(8,128)S(1)}, u32[]{:S(2)}, u32[]{:S(2)}) collective-permute-start(f32[8,128]{1,0:T(8,128)S(1)} %add.16), channel_id=1, source_target_pairs={{0,2},{1,3},{2,0},{3,1},{4,6},{5,7},{6,4},{7,5},{8,10},{9,11},{10,... | collective-permute-start | bytes 12296 | tf_op jit(solution)/shard_map/ppermute | solution.py:27
  100.4 3.0 %collective-permute-done.14 = f32[8,128]{1,0:T(8,128)S(1)} collective-permute-done((f32[8,128]{1,0:T(8,128)S(1)}, f32[8,128]{1,0:T(8,128)S(1)}, u32[]{:S(2)}, u32[]{:S(2)}) %collective-permute-start.14) | collective-permute-done | bytes 4128 | tf_op jit(solution)/shard_map/ppermute | solution.py:27
  103.5 13.4 %all_to_all.14.gram_ref = f32[32,8,128]{2,1,0:T(8,128)S(1)} all-to-all(f32[32,8,128]{2,1,0:T(8,128)S(1)} %broadcast_in_dim.5), channel_id=1, replica_groups={{0,8,16,24,32,40,48,56,64,72,80,88,96,104,112,120,128,136,144,152,160,1..., dimensions={0} | all-to-all | bytes 262144 | tf_op jit(solution)/shard_map/all_to_all | solution.py:38
  116.9 2.5 %basis.1 = f32[32,2048]{1,0:T(8,128)} custom-call(f32[32,8,128]{2,1,0:T(8,128)S(1)} %all_to_all.14.gram_ref, f32[32,2048]{1,0:T(8,128)S(1)} %get-tuple-element.66.embedded_ref), custom_call_target="tpu_custom_call" | custom-call | tf_op jit(solution)/shard_map/basis/pallas_call | solution.py:384
  (26 shorter events, 2.8 us)
Async XLA Ops:
  7.1 10.6 %collective-permute-start = (f32[8,256]{1,0:T(8,128)S(1)}, f32[8,256]{1,0:T(8,128)S(1)}, u32[]{:S(2)}, u32[]{:S(2)}) collective-permute-start(f32[8,256]{1,0:T(8,128)S(1)} %get-tuple-element.39), channel_id=1, source_target_pairs={{0,255},{1,2},{2,1},{3,4},{4,3},{5,6},{6,5},{7,8},{8,7},{9,10},{10... | collective-permute-start | bytes 24584 | tf_op jit(solution)/shard_map/ppermute | solution.py:27
  8.6 10.6 %collective-permute-start.1 = (f32[8,256]{1,0:T(8,128)S(1)}, f32[8,256]{1,0:T(8,128)S(1)}, u32[]{:S(2)}, u32[]{:S(2)}) collective-permute-start(f32[8,256]{1,0:T(8,128)S(1)} %get-tuple-element.41), channel_id=1, source_target_pairs={{0,1},{1,0},{2,3},{3,2},{4,5},{5,4},{6,7},{7,6},{8,9},{9,8},{10,11... | collective-permute-start | bytes 24584 | tf_op jit(solution)/shard_map/ppermute | solution.py:27
  19.9 7.9 %collective-permute-start.2 = (f32[16,256]{1,0:T(8,128)S(1)}, f32[16,256]{1,0:T(8,128)S(1)}, u32[]{:S(2)}, u32[]{:S(2)}) collective-permute-start(f32[16,256]{1,0:T(8,128)S(1)} %get-tuple-element.43), channel_id=1, source_target_pairs={{0,255},{1,2},{2,1},{3,4},{4,3},{5,6},{6,5},{7,8},{8,7},{9,10},{10... | collective-permute-start | bytes 49160 | tf_op jit(solution)/shard_map/ppermute | solution.py:27
  20.0 8.5 %collective-permute-start.3 = (f32[16,256]{1,0:T(8,128)S(1)}, f32[16,256]{1,0:T(8,128)S(1)}, u32[]{:S(2)}, u32[]{:S(2)}) collective-permute-start(f32[16,256]{1,0:T(8,128)S(1)} %get-tuple-element.45), channel_id=1, source_target_pairs={{0,1},{1,0},{2,3},{3,2},{4,5},{5,4},{6,7},{7,6},{8,9},{9,8},{10,11... | collective-permute-start | bytes 49160 | tf_op jit(solution)/shard_map/ppermute | solution.py:27
  29.2 7.8 %collective-permute-start.4 = (f32[16,256]{1,0:T(8,128)S(1)}, f32[16,256]{1,0:T(8,128)S(1)}, u32[]{:S(2)}, u32[]{:S(2)}) collective-permute-start(f32[16,256]{1,0:T(8,128)S(1)} %get-tuple-element.47), channel_id=1, source_target_pairs={{0,255},{1,2},{2,1},{3,4},{4,3},{5,6},{6,5},{7,8},{8,7},{9,10},{10... | collective-permute-start | bytes 49160 | tf_op jit(solution)/shard_map/ppermute | solution.py:27
  29.3 8.2 %collective-permute-start.5 = (f32[16,256]{1,0:T(8,128)S(1)}, f32[16,256]{1,0:T(8,128)S(1)}, u32[]{:S(2)}, u32[]{:S(2)}) collective-permute-start(f32[16,256]{1,0:T(8,128)S(1)} %get-tuple-element.49), channel_id=1, source_target_pairs={{0,1},{1,0},{2,3},{3,2},{4,5},{5,4},{6,7},{7,6},{8,9},{9,8},{10,11... | collective-permute-start | bytes 49160 | tf_op jit(solution)/shard_map/ppermute | solution.py:27
  38.1 7.7 %collective-permute-start.6 = (f32[8,256]{1,0:T(8,128)S(1)}, f32[8,256]{1,0:T(8,128)S(1)}, u32[]{:S(2)}, u32[]{:S(2)}) collective-permute-start(f32[8,256]{1,0:T(8,128)S(1)} %get-tuple-element.51), channel_id=1, source_target_pairs={{0,255},{1,2},{2,1},{3,4},{4,3},{5,6},{6,5},{7,8},{8,7},{9,10},{10... | collective-permute-start | bytes 24584 | tf_op jit(solution)/shard_map/ppermute | solution.py:27
  38.2 8.1 %collective-permute-start.7 = (f32[8,256]{1,0:T(8,128)S(1)}, f32[8,256]{1,0:T(8,128)S(1)}, u32[]{:S(2)}, u32[]{:S(2)}) collective-permute-start(f32[8,256]{1,0:T(8,128)S(1)} %get-tuple-element.53), channel_id=1, source_target_pairs={{0,1},{1,0},{2,3},{3,2},{4,5},{5,4},{6,7},{7,6},{8,9},{9,8},{10,11... | collective-permute-start | bytes 24584 | tf_op jit(solution)/shard_map/ppermute | solution.py:27
  46.4 1.1 collective-permute-start.8
  68.3 6.8 %copy-start = (bf16[32,2048]{1,0:T(8,128)(2,1)S(1)}, bf16[32,2048]{1,0:T(8,128)(2,1)}, u32[]{:S(2)}) copy-start(bf16[32,2048]{1,0:T(8,128)(2,1)} %probe_ref.1) | copy-start | bytes 393220
  71.3 3.7 %collective-permute-start.9 = (f32[8,256]{1,0:T(8,128)S(1)}, f32[8,256]{1,0:T(8,128)S(1)}, u32[]{:S(2)}, u32[]{:S(2)}) collective-permute-start(f32[8,256]{1,0:T(8,128)S(1)} %get-tuple-element.55), channel_id=1, source_target_pairs={{0,255},{1,2},{2,1},{3,4},{4,3},{5,6},{6,5},{7,8},{8,7},{9,10},{10... | collective-permute-start | bytes 24584 | tf_op jit(solution)/shard_map/ppermute | solution.py:27
  71.4 3.7 %collective-permute-start.10 = (f32[8,256]{1,0:T(8,128)S(1)}, f32[8,256]{1,0:T(8,128)S(1)}, u32[]{:S(2)}, u32[]{:S(2)}) collective-permute-start(f32[8,256]{1,0:T(8,128)S(1)} %get-tuple-element.57), channel_id=1, source_target_pairs={{0,1},{1,0},{2,3},{3,2},{4,5},{5,4},{6,7},{7,6},{8,9},{9,8},{10,11... | collective-permute-start | bytes 24584 | tf_op jit(solution)/shard_map/ppermute | solution.py:27
  75.9 10.4 %collective-permute-start.11 = (bf16[24,32,256]{2,1,0:T(8,128)(2,1)S(1)}, bf16[24,32,256]{2,1,0:T(8,128)(2,1)S(1)}, u32[]{:S(2)}, u32[]{:S(2)}) collective-permute-start(bf16[24,32,256]{2,1,0:T(8,128)(2,1)S(1)} %get-tuple-element.63), channel_id=1, source_target_pairs={{0,255},{1,2},{2,1},{3,4},{4,3},{5,6},{6,5},{7,8},{8,7},{9,10},{10... | collective-permute-start | bytes 1179656 | tf_op jit(solution)/shard_map/ppermute | solution.py:27
  77.9 11.2 %collective-permute-start.12 = (bf16[24,32,256]{2,1,0:T(8,128)(2,1)S(1)}, bf16[24,32,256]{2,1,0:T(8,128)(2,1)S(1)}, u32[]{:S(2)}, u32[]{:S(2)}) collective-permute-start(bf16[24,32,256]{2,1,0:T(8,128)(2,1)S(1)} %get-tuple-element.64), channel_id=1, source_target_pairs={{0,1},{1,0},{2,3},{3,2},{4,5},{5,4},{6,7},{7,6},{8,9},{9,8},{10,11... | collective-permute-start | bytes 1179656 | tf_op jit(solution)/shard_map/ppermute | solution.py:27
  90.4 1.2 %collective-permute-start.13 = (f32[8,128]{1,0:T(8,128)S(1)}, f32[8,128]{1,0:T(8,128)S(1)}, u32[]{:S(2)}, u32[]{:S(2)}) collective-permute-start(f32[8,128]{1,0:T(8,128)S(1)} %get-tuple-element.65), channel_id=1, source_target_pairs={{0,4},{4,0},{8,12},{12,8},{16,20},{20,16},{24,28},{28,24},{32,36},... | collective-permute-start | bytes 12296 | tf_op jit(solution)/shard_map/ppermute | solution.py:27
  91.6 8.8 %collective-permute-start.16 = (f32[8,128]{1,0:T(8,128)S(1)}, f32[8,128]{1,0:T(8,128)S(1)}, u32[]{:S(2)}, u32[]{:S(2)}) collective-permute-start(f32[8,128]{1,0:T(8,128)S(1)} %add.16), channel_id=1, source_target_pairs={{0,3},{1,2},{2,1},{3,0},{4,7},{5,6},{6,5},{7,4},{8,11},{9,10},{10,... | collective-permute-start | bytes 12296 | tf_op jit(solution)/shard_map/ppermute | solution.py:27
  92.2 8.2 %collective-permute-start.15 = (f32[8,128]{1,0:T(8,128)S(1)}, f32[8,128]{1,0:T(8,128)S(1)}, u32[]{:S(2)}, u32[]{:S(2)}) collective-permute-start(f32[8,128]{1,0:T(8,128)S(1)} %add.16), channel_id=1, source_target_pairs={{0,1},{1,0},{2,3},{3,2},{4,5},{5,4},{6,7},{7,6},{8,9},{9,8},{10,11... | collective-permute-start | bytes 12296 | tf_op jit(solution)/shard_map/ppermute | solution.py:27
  98.4 5.1 %collective-permute-start.14 = (f32[8,128]{1,0:T(8,128)S(1)}, f32[8,128]{1,0:T(8,128)S(1)}, u32[]{:S(2)}, u32[]{:S(2)}) collective-permute-start(f32[8,128]{1,0:T(8,128)S(1)} %add.16), channel_id=1, source_target_pairs={{0,2},{1,3},{2,0},{3,1},{4,6},{5,7},{6,4},{7,5},{8,10},{9,11},{10,... | collective-permute-start | bytes 12296 | tf_op jit(solution)/shard_map/ppermute | solution.py:27

commit v3 on v2

--- a/solution.py
+++ b/solution.py
@@ -48,7 +48,7 @@
 
 def plane_parts(part):
     part = part + swap(part, "rows", lambda i: i ^ 1)
-    part = part + sum(swap(part, "cols", lambda i, d=d: i ^ d) for d in (2, 1, 3))
+    part = part + sum(swap(part, "cols", lambda i, d=d: i ^ d) for d in (1, 2, 3))
     groups = [list(range(core, lax.axis_size("rows"), 2)) for core in (0, 1)]
     return gathered(part, "rows", groups)
 
@@ -98,7 +98,7 @@
         out[rows, :] = jnp.sum(window[part * 8 : (part + 1) * 8, rows, :], axis=1)
 
 
-def load_kernel(cols_hbm, count_hbm, tiles_hbm, start_hbm, tiles_ref, target_ref, inverse_ref, odd_ref, own_ref, even_ref,
+def load_kernel(cols_hbm, count_hbm, tiles_hbm, start_hbm, tiles_ref, table_ref, inverse_ref, to_odd, to_even, left_ref,
                 window, start_ref, cols_ref, count_ref, sems, small_sems):
     blocks, slots, width = tiles_hbm.shape[:3]
     small = [
@@ -113,72 +113,61 @@
     ]
     for copy in small + copies:
         copy.start()
-    ones = jnp.ones((16, 128), BF16)
-    window[...] = jnp.zeros_like(window)
-    line = lax.broadcasted_iota(jnp.int32, (16, width), 0)
     total_blocks = blocks * lax.axis_size("rows") * lax.axis_size("cols")
     place = lax.axis_index("rows") * lax.axis_size("cols") + lax.axis_index("cols")
     swapped = place % 2 == 1
+    for entry in range(128):
+        table_ref[entry] = DEAD
     for copy in small:
         copy.wait()
-
-    def row_sums(block):
+    halo_count, own_count = jnp.int32(0), jnp.int32(0)
+    for block in range(blocks):
+        for slot in range(slots):
+            target = cols_ref[block, slot] - place * blocks + blocks
+            target = jnp.where(target < 0, target + total_blocks, target)
+            target = jnp.where(target >= total_blocks, target - total_blocks, target)
+            own = (target >= blocks) & (target < 2 * blocks)
+            flipped = jnp.where(target < blocks, target + 2 * blocks, target - 2 * blocks)
+            target = jnp.where(swapped & jnp.logical_not(own), flipped, target)
+            live = slot < count_ref[block]
+            to_own = live & own
+            to_halo = live & jnp.logical_not(own)
+            entry = target + (block * slots + slot) * 32
+            table_ref[jnp.where(to_halo, halo_count, jnp.where(to_own, 64 + own_count, SPARE))] = entry
+            halo_count += jnp.where(to_halo, 1, 0)
+            own_count += jnp.where(to_own, 1, 0)
+    table_ref[HALO_CHUNKS] = (halo_count + CHUNK - 1) >> 3
+    table_ref[OWN_CHUNKS] = (own_count + CHUNK - 1) >> 3
+
+    ones = jnp.ones((16, 128), BF16)
+
+    def folded_tiles(block):
         folded = jnp.zeros((width, 128), F32)
         for slot in range(slots):
             tile = tiles_ref[block * slots + slot].astype(F32)
             folded = folded + (tile[:, :128] + tile[:, 128:]) * jnp.where(slot < count_ref[block], 1.0, 0.0)
+        return folded
+
+    def row_sums(folded):
         total = jnp.zeros((16, width), F32)
         for _ in range(3):
             part = folded.astype(BF16)
             folded = folded - part.astype(F32)
             total = total + lax.dot_general(ones, part, LAST_DIMS, preferred_element_type=F32)
-        return total
-
-    def target_of(block, slot):
-        target = cols_ref[block, slot] - place * blocks + blocks
-        target = jnp.where(target < 0, target + total_blocks, target)
-        target = jnp.where(target >= total_blocks, target - total_blocks, target)
-        flipped = jnp.where(target >= 2 * blocks, target - 2 * blocks, jnp.where(target < blocks, target + 2 * blocks, target))
-        target = jnp.where(swapped, flipped, target)
-        return jnp.where(slot < count_ref[block], target, DEAD)
-
-    def push_block(block, total):
-        inverse = 1.0 / total
-        inverse_ref[block : block + 1, :] = inverse[0:1]
-        left = jnp.where(line == block, start_ref[block : block + 1, :] * inverse, 0.0).astype(BF16)
-        for slot in range(slots):
-            tile = block * slots + slot
-            target = target_of(block, slot)
-            target_ref[tile] = target
-            window[target] += jnp.dot(left, tiles_ref[tile], preferred_element_type=F32)[0:8]
-
+        return total[0:1]
+
+    sums = []
     before = None
     for block in range(blocks):
         copies[block].wait()
-        total = row_sums(block)
+        folded = folded_tiles(block)
         if before is not None:
-            push_block(block - 1, before)
-        before = total
-    push_block(blocks - 1, before)
-    landed(window, 0, odd_ref)
-    landed(window, 1, own_ref)
-    landed(window, 2, even_ref)
-
-
-def table_kernel(target_ref, table_ref):
-    for entry in range(128):
-        table_ref[entry] = DEAD
-    halo_count, own_count = jnp.int32(0), jnp.int32(0)
-    for tile in range(target_ref.shape[0]):
-        target = target_ref[tile]
-        to_own = (target >= 8) & (target < 16)
-        to_halo = (target < 8) | ((target >= 16) & (target < DEAD))
-        entry = target + tile * 32
-        table_ref[jnp.where(to_halo, halo_count, jnp.where(to_own, 64 + own_count, SPARE))] = entry
-        halo_count += jnp.where(to_halo, 1, 0)
-        own_count += jnp.where(to_own, 1, 0)
-    table_ref[HALO_CHUNKS] = (halo_count + CHUNK - 1) >> 3
-    table_ref[OWN_CHUNKS] = (own_count + CHUNK - 1) >> 3
+            sums.append(row_sums(before))
+        before = folded
+    sums.append(row_sums(before))
+    inverse = 1.0 / jnp.concatenate(sums, axis=0)
+    inverse_ref[...] = inverse
+    halo_step(start_ref[...] * inverse, False, table_ref, tiles_ref, to_odd, to_even, left_ref, window)
 
 
 def halo_step(rows, split, table_ref, tiles_ref, to_odd, to_even, left_ref, window):
@@ -358,7 +347,7 @@
     gram_ref[...] = jnp.concatenate([gram[8 * i : 8 * i + 8] for i in range(4)], axis=1)
 
 
-def basis_kernel(gram_ref, embedded_ref, out_ref):
+def basis_kernel(gram_ref, embedded_ref, out_hbm, out_ref, sems):
     size = embedded_ref.shape[0]
     row = lax.broadcasted_iota(jnp.int32, (size, size), 0)
     col = lax.broadcasted_iota(jnp.int32, (size, size), 1)
@@ -367,17 +356,26 @@
     gram = jnp.concatenate([gram[:, size * i : size * (i + 1)] for i in range(4)], axis=0)
     work = jnp.concatenate([gram, identity, jnp.zeros((size, 128 - 2 * size), F32)], axis=1)
     line = lax.broadcasted_iota(jnp.int32, work.shape, 0)
-    for first in range(0, size, 4):
-        columns = [jnp.broadcast_to(work[:, first + i : first + i + 1], work.shape) for i in range(4)]
-        for i in range(4):
+    for first in range(0, size, 16):
+        columns = [jnp.broadcast_to(work[:, first + i : first + i + 1], work.shape) for i in range(16)]
+        for i in range(16):
             step = first + i
             factor = jnp.where(line > step, columns[i] * (1.0 / columns[i][step : step + 1, :]), 0.0)
             work = work - factor * work[step : step + 1, :]
-            for j in range(i + 1, 4):
+            for j in range(i + 1, 16):
                 columns[j] = columns[j] - factor * columns[j][step : step + 1, :]
     pivots = jnp.sum(work[:, :size] * identity, axis=1, keepdims=True)
     inverse = work[:, size : 2 * size] * (1.0 / jnp.sqrt(pivots))
-    out_ref[...] = jnp.dot(inverse, embedded_ref[...], precision=HIGHEST, preferred_element_type=F32)
+    parts = sems.shape[0]
+    width = embedded_ref.shape[1] // parts
+    copies = []
+    for part in range(parts):
+        span = pl.ds(part * width, width)
+        out_ref[:, span] = jnp.dot(inverse, embedded_ref[:, span], precision=HIGHEST, preferred_element_type=F32)
+        copies.append(pltpu.make_async_copy(out_ref.at[:, span], out_hbm.at[:, span], sems.at[part]))
+        copies[-1].start()
+    for copy in copies:
+        copy.wait()
 
 
 def call(kernel, name, outs, operands, specs, scratch, out_specs=None, limit=24, flops=0, moved=0):
@@ -404,9 +402,12 @@
     def window(channels, kind=F32, places=3 * blocks + 1):
         return pltpu.VMEM((places, channels, width), kind)
 
-    tiles, target, inverse, to_odd, own, to_even = call(
+    tiles, table, inverse, to_odd, to_even, left = call(
         load_kernel, "load",
-        [pltpu.VMEM((blocks * slots, width, width), BF16), pltpu.SMEM((blocks * slots,), jnp.int32), rows(), rows(), rows(), rows()],
+        [
+            pltpu.VMEM((blocks * slots, width, width), BF16), pltpu.SMEM((136,), jnp.int32), rows(), rows(), rows(),
+            jax.ShapeDtypeStruct((blocks, 16, width), BF16),
+        ],
         [pltpu.with_memory_space_constraint(x, pltpu.HBM) for x in (tile_cols, tile_count, tile_blocks, start_mass)],
         [pl.BlockSpec(memory_space=pltpu.HBM)] * 4,
         [
@@ -416,12 +417,17 @@
         [VMEM, SMEM, VMEM, VMEM, VMEM, VMEM],
     )
     tiles = pltpu.with_memory_space_constraint(tiles, pltpu.VMEM)
-    odd, even = ring_pairs(to_odd, to_even)
-    (table,) = call(
-        table_kernel, "table", [pltpu.SMEM((136,), jnp.int32)], [pltpu.with_memory_space_constraint(target, pltpu.SMEM)], [SMEM], [],
-        [SMEM], flops=1 << 25, moved=1 << 22,
-    )
     table = pltpu.with_memory_space_constraint(table, pltpu.SMEM)
+
+    def exchange(to_odd, to_even, left, name, channels, split):
+        odd, even = ring_pairs(to_odd, to_even)
+        (own,) = call(
+            functools.partial(own_kernel, split), name + "_own", [rows(channels)], (table, tiles, left), [SMEM] + [VMEM] * 2,
+            [window(channels * blocks)], flops=1 << 25, moved=1 << 22,
+        )
+        return odd, own, even
+
+    odd, own, even = exchange(to_odd, to_even, left, "first", 1, False)
 
     def step(kernel, name, channels, split, operands, extra):
         height = max(16, channels * blocks * (2 if split else 1))
@@ -430,12 +436,7 @@
             kernel, name, [rows(channels)] * 2 + [left] + extra, (table, tiles, inverse, *operands),
             [SMEM] + [VMEM] * (2 + len(operands)), [window(channels * blocks)], flops=1 << 24, moved=1 << 21,
         )
-        odd, even = ring_pairs(to_odd, to_even)
-        (own,) = call(
-            functools.partial(own_kernel, split), name + "_own", [rows(channels)], (table, tiles, left), [SMEM] + [VMEM] * 2,
-            [window(channels * blocks)], flops=1 << 25, moved=1 << 22,
-        )
-        return odd, own, even, *extra
+        return *exchange(to_odd, to_even, left, name, channels, split), *extra
 
     odd, own, even, raw = step(second_kernel, "second", 2, True, (odd, own, even), [rows()])
     odd, own, even, second = step(functools.partial(chain_kernel, 2), "third", 2, True, (odd, own, even), [rows(2)])
@@ -467,7 +468,8 @@
         (table, tiles, inverse, root, kept, forward, odd, even), [SMEM] + [VMEM] * 7, [window(chans, places=blocks + 1)],
     )
     (basis,) = call(
-        basis_kernel, "basis", [jax.ShapeDtypeStruct((chans, blocks * width), F32)], (plane_parts(gram), embedded), [VMEM] * 2, []
+        basis_kernel, "basis", [pltpu.HBM((chans, blocks * width), F32)], (plane_parts(gram), embedded), [VMEM] * 2,
+        [pltpu.VMEM((chans, blocks * width), F32), pltpu.SemaphoreType.DMA((4,))], [pl.BlockSpec(memory_space=pltpu.HBM)],
     )
     return basis
 

time: 121 us -> 119 us (0.983)
  Pallas kernels: 23.7 us -> 20.4 us
  waiting for transfers between devices: 12.8 us -> 14.2 us
    pallas_call x15, Pallas kernels: 23.7 us -> 20.4 us  [call(): pl.pallas_call(kernel, out_shape=outs, in_specs=specs, out_specs=out_spec...]
    ppermute x17, waiting for transfers between devices: 12.8 us -> 14.2 us  [swap(): lax.ppermute(shard, axis, [(i, partner(i) % count) for i in range(count)])]
  transfers between devices with their start and end apart: 17 -> 17, of which waited for: 11 -> 12; matrix products, arithmetic and copies ran while one was open for 0% -> 0% of each run, Pallas kernels for 6% -> 5%
where the time goes in v3:
time: 119 us; the launch traced here: 118 us
  starting transfers between devices  47.9 us (40%)
  blocking collectives  35.3 us (30%)
  Pallas kernels  20.4 us (17%)
  waiting for transfers between devices  14.2 us (12%)
    ppermute x17, starting transfers between devices, swap(): lax.ppermute(shard, axis, [(i, partner(i) % count) for i in range(count)])  47.9 us
    all_to_all x2, blocking collectives, gathered(): lax.all_to_all(spread, axis, 0, 0, tiled=True, axis_index_groups=groups)  35.3 us
    pallas_call x15, Pallas kernels, call(): pl.pallas_call(kernel, out_shape=outs, in_specs=specs, out_specs=out_spec...  20.4 us
    ppermute x17, waiting for transfers between devices, swap(): lax.ppermute(shard, axis, [(i, partner(i) % count) for i in range(count)])  14.2 us
  transfers between devices with their start and end apart: 17, of which 12 were waited for; matrix products, arithmetic and copies ran while one was open for 0% of the time, Pallas kernels for 5%

profile of v3, /device:TPU:2, one launch (start us, length us, event | category | flops | bytes accessed | tf_op | source)
XLA Modules:
  0.0 118.2 jit_solution(13773792645324775312)
XLA Ops:
  0.0 5.7 %load.1 = (bf16[64,256,256]{2,1,0:T(8,128)(2,1)S(1)}, s32[136]{0:T(256)S(4)}, f32[8,256]{1,0:T(8,128)S(1)}, f32[8,256]{1,0:T(8,128)S(1)}, f32[8,256]{1,0:T(8,128)S(1)}, /*index=5*/bf16[8,16,256]{2,1,0:T(8,128)(2,1)S(1)}) custom-call(s32[8,8]{1,0:T(8,128)} %cols_hbm.1, s32[8]{0:T(128)} %count_hbm.1, bf16[8,8,256,256]{3,2,1,0:T(8,128)(2,1)} %tiles_hbm.1, ...), custom_call_target="tpu_custom_call" | custom-call | tf_op jit(solution)/shard_map/load/pallas_call | solution.py:382
  5.7 1.6 %collective-permute-start = (f32[8,256]{1,0:T(8,128)S(1)}, f32[8,256]{1,0:T(8,128)S(1)}, u32[]{:S(2)}, u32[]{:S(2)}) collective-permute-start(f32[8,256]{1,0:T(8,128)S(1)} %get-tuple-element.39), channel_id=1, source_target_pairs={{0,255},{1,2},{2,1},{3,4},{4,3},{5,6},{6,5},{7,8},{8,7},{9,10},{10... | collective-permute-start | bytes 24584 | tf_op jit(solution)/shard_map/ppermute | solution.py:27
  7.3 8.7 %collective-permute-start.1 = (f32[8,256]{1,0:T(8,128)S(1)}, f32[8,256]{1,0:T(8,128)S(1)}, u32[]{:S(2)}, u32[]{:S(2)}) collective-permute-start(f32[8,256]{1,0:T(8,128)S(1)} %get-tuple-element.41), channel_id=1, source_target_pairs={{0,1},{1,0},{2,3},{3,2},{4,5},{5,4},{6,7},{7,6},{8,9},{9,8},{10,11... | collective-permute-start | bytes 24584 | tf_op jit(solution)/shard_map/ppermute | solution.py:27
  16.0 0.8 first_own.1.own
  16.8 0.8 collective-permute-done.1.even
  18.4 6.6 %collective-permute-start.3 = (f32[16,256]{1,0:T(8,128)S(1)}, f32[16,256]{1,0:T(8,128)S(1)}, u32[]{:S(2)}, u32[]{:S(2)}) collective-permute-start(f32[16,256]{1,0:T(8,128)S(1)} %get-tuple-element.45), channel_id=1, source_target_pairs={{0,1},{1,0},{2,3},{3,2},{4,5},{5,4},{6,7},{7,6},{8,9},{9,8},{10,11... | collective-permute-start | bytes 49160 | tf_op jit(solution)/shard_map/ppermute | solution.py:27
  25.0 0.9 second_own.1.own
  27.5 6.6 %collective-permute-start.5 = (f32[16,256]{1,0:T(8,128)S(1)}, f32[16,256]{1,0:T(8,128)S(1)}, u32[]{:S(2)}, u32[]{:S(2)}) collective-permute-start(f32[16,256]{1,0:T(8,128)S(1)} %get-tuple-element.49), channel_id=1, source_target_pairs={{0,1},{1,0},{2,3},{3,2},{4,5},{5,4},{6,7},{7,6},{8,9},{9,8},{10,11... | collective-permute-start | bytes 49160 | tf_op jit(solution)/shard_map/ppermute | solution.py:27
  34.1 0.9 third_own.1.own
  35.0 0.8 collective-permute-done.5.even
  36.5 6.6 %collective-permute-start.7 = (f32[8,256]{1,0:T(8,128)S(1)}, f32[8,256]{1,0:T(8,128)S(1)}, u32[]{:S(2)}, u32[]{:S(2)}) collective-permute-start(f32[8,256]{1,0:T(8,128)S(1)} %get-tuple-element.53), channel_id=1, source_target_pairs={{0,1},{1,0},{2,3},{3,2},{4,5},{5,4},{6,7},{7,6},{8,9},{9,8},{10,11... | collective-permute-start | bytes 24584 | tf_op jit(solution)/shard_map/ppermute | solution.py:27
  43.1 0.8 fourth_own.1.own
  43.9 0.8 collective-permute-done.7.even
  44.8 1.1 collective-permute-done.8
  46.0 21.7 %all_to_all.13 = f32[128,1,128]{2,1,0:T(1,128)S(1)} all-to-all(f32[128,1,128]{2,1,0:T(1,128)S(1)} %broadcast_in_dim.4), channel_id=1, replica_groups={{0,1,2,3,8,9,10,11,16,17,18,19,24,25,26,27,32,33,34,35,40,41,42,43,48,4..., dimensions={0} | all-to-all | bytes 131072 | tf_op jit(solution)/shard_map/all_to_all | solution.py:38
  67.7 2.6 %replay.1 = (f32[8,256]{1,0:T(8,128)S(1)}, f32[8,256]{1,0:T(8,128)S(1)}, bf16[8,16,256]{2,1,0:T(8,128)(2,1)S(1)}, f32[8,128]{1,0:T(8,128)S(1)}) custom-call(s32[136]{0:T(256)S(4)} %get-tuple-element.36.table_ref, bf16[64,256,256]{2,1,0:T(8,128)(2,1)S(1)} %get-tuple-element.37.tiles_ref, f32[8,256]{1,0:T(8,128)S(1)} %get-tuple-element.38.inverse_ref, ...), custom_call_target="tpu_custom_call" | custom-call | flops 16777216 | bytes 2097152 | tf_op jit(solution)/shard_map/replay/pallas_call | solution.py:382
  70.9 1.5 %collective-permute-start.10 = (f32[8,256]{1,0:T(8,128)S(1)}, f32[8,256]{1,0:T(8,128)S(1)}, u32[]{:S(2)}, u32[]{:S(2)}) collective-permute-start(f32[8,256]{1,0:T(8,128)S(1)} %get-tuple-element.57), channel_id=1, source_target_pairs={{0,1},{1,0},{2,3},{3,2},{4,5},{5,4},{6,7},{7,6},{8,9},{9,8},{10,11... | collective-permute-start | bytes 24584 | tf_op jit(solution)/shard_map/ppermute | solution.py:27
  72.4 0.8 replay_own.1.own
  73.3 0.8 collective-permute-done.9.odd
  75.4 1.5 %collective-permute-start.11 = (bf16[24,32,256]{2,1,0:T(8,128)(2,1)S(1)}, bf16[24,32,256]{2,1,0:T(8,128)(2,1)S(1)}, u32[]{:S(2)}, u32[]{:S(2)}) collective-permute-start(bf16[24,32,256]{2,1,0:T(8,128)(2,1)S(1)} %get-tuple-element.63), channel_id=1, source_target_pairs={{0,255},{1,2},{2,1},{3,4},{4,3},{5,6},{6,5},{7,8},{8,7},{9,10},{10... | collective-permute-start | bytes 1179656 | tf_op jit(solution)/shard_map/ppermute | solution.py:27
  76.9 5.7 %collective-permute-start.12 = (bf16[24,32,256]{2,1,0:T(8,128)(2,1)S(1)}, bf16[24,32,256]{2,1,0:T(8,128)(2,1)S(1)}, u32[]{:S(2)}, u32[]{:S(2)}) collective-permute-start(bf16[24,32,256]{2,1,0:T(8,128)(2,1)S(1)} %get-tuple-element.64), channel_id=1, source_target_pairs={{0,1},{1,0},{2,3},{3,2},{4,5},{5,4},{6,7},{7,6},{8,9},{9,8},{10,11... | collective-permute-start | bytes 1179656 | tf_op jit(solution)/shard_map/ppermute | solution.py:27
  82.6 1.9 %own_products.1 = (f32[8,32,256]{2,1,0:T(8,128)S(1)}, f32[8,32,256]{2,1,0:T(8,128)S(1)}) custom-call(s32[136]{0:T(256)S(4)} %get-tuple-element.36.table_ref, bf16[64,256,256]{2,1,0:T(8,128)(2,1)S(1)} %get-tuple-element.37.tiles_ref, bf16[8,32,256]{2,1,0:T(8,128)(2,1)S(1)} %get-tuple-element.59.pushed_ref, bf16[8,32,256]{2,1,0:T(8,128)(2,1)S(1)} %get-tuple-element.60.scaled_ref), custom_call_target="tpu_custom_call" | custom-call | flops 268435456 | bytes 8388608 | tf_op jit(solution)/shard_map/own_products/pallas_call | solution.py:382
  84.5 1.0 collective-permute-done.11.odd
  85.5 2.8 %collective-permute-done.12.even = bf16[24,32,256]{2,1,0:T(8,128)(2,1)S(1)} collective-permute-done((bf16[24,32,256]{2,1,0:T(8,128)(2,1)S(1)}, bf16[24,32,256]{2,1,0:T(8,128)(2,1)S(1)}, u32[]{:S(2)}, u32[]{:S(2)}) %collective-permute-start.12) | collective-permute-done | bytes 393248 | tf_op jit(solution)/shard_map/ppermute | solution.py:27
  88.3 1.3 %embed.1 = (f32[32,2048]{1,0:T(8,128)S(1)}, f32[8,128]{1,0:T(8,128)S(1)}) custom-call(s32[136]{0:T(256)S(4)} %get-tuple-element.36.table_ref, bf16[64,256,256]{2,1,0:T(8,128)(2,1)S(1)} %get-tuple-element.37.tiles_ref, f32[8,256]{1,0:T(8,128)S(1)} %get-tuple-element.38.inverse_ref, f32[8,256]{1,0:T(8,128)S(1)} %get-tuple-element.58.root_ref, ...), custom_call_target="tpu_custom_call" | custom-call | tf_op jit(solution)/shard_map/embed/pallas_call | solution.py:382
  89.7 1.2 collective-permute-done.13
  90.9 0.8 collective-permute-start.16
  91.6 7.3 %collective-permute-start.15 = (f32[8,128]{1,0:T(8,128)S(1)}, f32[8,128]{1,0:T(8,128)S(1)}, u32[]{:S(2)}, u32[]{:S(2)}) collective-permute-start(f32[8,128]{1,0:T(8,128)S(1)} %add.16), channel_id=1, source_target_pairs={{0,2},{1,3},{2,0},{3,1},{4,6},{5,7},{6,4},{7,5},{8,10},{9,11},{10,... | collective-permute-start | bytes 12296 | tf_op jit(solution)/shard_map/ppermute | solution.py:27
  99.0 1.6 %collective-permute-done.15 = f32[8,128]{1,0:T(8,128)S(1)} collective-permute-done((f32[8,128]{1,0:T(8,128)S(1)}, f32[8,128]{1,0:T(8,128)S(1)}, u32[]{:S(2)}, u32[]{:S(2)}) %collective-permute-start.15) | collective-permute-done | bytes 4128 | tf_op jit(solution)/shard_map/ppermute | solution.py:27
  100.5 2.0 %collective-permute-done.14 = f32[8,128]{1,0:T(8,128)S(1)} collective-permute-done((f32[8,128]{1,0:T(8,128)S(1)}, f32[8,128]{1,0:T(8,128)S(1)}, u32[]{:S(2)}, u32[]{:S(2)}) %collective-permute-start.14) | collective-permute-done | bytes 4128 | tf_op jit(solution)/shard_map/ppermute | solution.py:27
  102.6 13.6 %all_to_all.14.gram_ref = f32[32,8,128]{2,1,0:T(8,128)S(1)} all-to-all(f32[32,8,128]{2,1,0:T(8,128)S(1)} %broadcast_in_dim.5), channel_id=1, replica_groups={{0,8,16,24,32,40,48,56,64,72,80,88,96,104,112,120,128,136,144,152,160,1..., dimensions={0} | all-to-all | bytes 262144 | tf_op jit(solution)/shard_map/all_to_all | solution.py:38
  116.2 1.9 %basis.1 = f32[32,2048]{1,0:T(8,128)} custom-call(f32[32,8,128]{2,1,0:T(8,128)S(1)} %all_to_all.14.gram_ref, f32[32,2048]{1,0:T(8,128)S(1)} %get-tuple-element.66.embedded_ref), custom_call_target="tpu_custom_call" | custom-call | tf_op jit(solution)/shard_map/basis/pallas_call | solution.py:382
  (26 shorter events, 5.2 us)
Async XLA Ops:
  5.7 11.1 %collective-permute-start = (f32[8,256]{1,0:T(8,128)S(1)}, f32[8,256]{1,0:T(8,128)S(1)}, u32[]{:S(2)}, u32[]{:S(2)}) collective-permute-start(f32[8,256]{1,0:T(8,128)S(1)} %get-tuple-element.39), channel_id=1, source_target_pairs={{0,255},{1,2},{2,1},{3,4},{4,3},{5,6},{6,5},{7,8},{8,7},{9,10},{10... | collective-permute-start | bytes 24584 | tf_op jit(solution)/shard_map/ppermute | solution.py:27
  7.3 10.4 %collective-permute-start.1 = (f32[8,256]{1,0:T(8,128)S(1)}, f32[8,256]{1,0:T(8,128)S(1)}, u32[]{:S(2)}, u32[]{:S(2)}) collective-permute-start(f32[8,256]{1,0:T(8,128)S(1)} %get-tuple-element.41), channel_id=1, source_target_pairs={{0,1},{1,0},{2,3},{3,2},{4,5},{5,4},{6,7},{7,6},{8,9},{9,8},{10,11... | collective-permute-start | bytes 24584 | tf_op jit(solution)/shard_map/ppermute | solution.py:27
  18.3 7.6 %collective-permute-start.2 = (f32[16,256]{1,0:T(8,128)S(1)}, f32[16,256]{1,0:T(8,128)S(1)}, u32[]{:S(2)}, u32[]{:S(2)}) collective-permute-start(f32[16,256]{1,0:T(8,128)S(1)} %get-tuple-element.43), channel_id=1, source_target_pairs={{0,255},{1,2},{2,1},{3,4},{4,3},{5,6},{6,5},{7,8},{8,7},{9,10},{10... | collective-permute-start | bytes 49160 | tf_op jit(solution)/shard_map/ppermute | solution.py:27
  18.4 8.3 %collective-permute-start.3 = (f32[16,256]{1,0:T(8,128)S(1)}, f32[16,256]{1,0:T(8,128)S(1)}, u32[]{:S(2)}, u32[]{:S(2)}) collective-permute-start(f32[16,256]{1,0:T(8,128)S(1)} %get-tuple-element.45), channel_id=1, source_target_pairs={{0,1},{1,0},{2,3},{3,2},{4,5},{5,4},{6,7},{7,6},{8,9},{9,8},{10,11... | collective-permute-start | bytes 49160 | tf_op jit(solution)/shard_map/ppermute | solution.py:27
  27.4 7.6 %collective-permute-start.4 = (f32[16,256]{1,0:T(8,128)S(1)}, f32[16,256]{1,0:T(8,128)S(1)}, u32[]{:S(2)}, u32[]{:S(2)}) collective-permute-start(f32[16,256]{1,0:T(8,128)S(1)} %get-tuple-element.47), channel_id=1, source_target_pairs={{0,255},{1,2},{2,1},{3,4},{4,3},{5,6},{6,5},{7,8},{8,7},{9,10},{10... | collective-permute-start | bytes 49160 | tf_op jit(solution)/shard_map/ppermute | solution.py:27
  27.5 8.3 %collective-permute-start.5 = (f32[16,256]{1,0:T(8,128)S(1)}, f32[16,256]{1,0:T(8,128)S(1)}, u32[]{:S(2)}, u32[]{:S(2)}) collective-permute-start(f32[16,256]{1,0:T(8,128)S(1)} %get-tuple-element.49), channel_id=1, source_target_pairs={{0,1},{1,0},{2,3},{3,2},{4,5},{5,4},{6,7},{7,6},{8,9},{9,8},{10,11... | collective-permute-start | bytes 49160 | tf_op jit(solution)/shard_map/ppermute | solution.py:27
  36.4 7.5 %collective-permute-start.6 = (f32[8,256]{1,0:T(8,128)S(1)}, f32[8,256]{1,0:T(8,128)S(1)}, u32[]{:S(2)}, u32[]{:S(2)}) collective-permute-start(f32[8,256]{1,0:T(8,128)S(1)} %get-tuple-element.51), channel_id=1, source_target_pairs={{0,255},{1,2},{2,1},{3,4},{4,3},{5,6},{6,5},{7,8},{8,7},{9,10},{10... | collective-permute-start | bytes 24584 | tf_op jit(solution)/shard_map/ppermute | solution.py:27
  36.5 8.2 %collective-permute-start.7 = (f32[8,256]{1,0:T(8,128)S(1)}, f32[8,256]{1,0:T(8,128)S(1)}, u32[]{:S(2)}, u32[]{:S(2)}) collective-permute-start(f32[8,256]{1,0:T(8,128)S(1)} %get-tuple-element.53), channel_id=1, source_target_pairs={{0,1},{1,0},{2,3},{3,2},{4,5},{5,4},{6,7},{7,6},{8,9},{9,8},{10,11... | collective-permute-start | bytes 24584 | tf_op jit(solution)/shard_map/ppermute | solution.py:27
  44.8 1.1 collective-permute-start.8
  67.7 6.9 %copy-start = (bf16[32,2048]{1,0:T(8,128)(2,1)S(1)}, bf16[32,2048]{1,0:T(8,128)(2,1)}, u32[]{:S(2)}) copy-start(bf16[32,2048]{1,0:T(8,128)(2,1)} %probe_ref.1) | copy-start | bytes 393220
  70.3 3.7 %collective-permute-start.9 = (f32[8,256]{1,0:T(8,128)S(1)}, f32[8,256]{1,0:T(8,128)S(1)}, u32[]{:S(2)}, u32[]{:S(2)}) collective-permute-start(f32[8,256]{1,0:T(8,128)S(1)} %get-tuple-element.55), channel_id=1, source_target_pairs={{0,255},{1,2},{2,1},{3,4},{4,3},{5,6},{6,5},{7,8},{8,7},{9,10},{10... | collective-permute-start | bytes 24584 | tf_op jit(solution)/shard_map/ppermute | solution.py:27
  70.9 3.7 %collective-permute-start.10 = (f32[8,256]{1,0:T(8,128)S(1)}, f32[8,256]{1,0:T(8,128)S(1)}, u32[]{:S(2)}, u32[]{:S(2)}) collective-permute-start(f32[8,256]{1,0:T(8,128)S(1)} %get-tuple-element.57), channel_id=1, source_target_pairs={{0,1},{1,0},{2,3},{3,2},{4,5},{5,4},{6,7},{7,6},{8,9},{9,8},{10,11... | collective-permute-start | bytes 24584 | tf_op jit(solution)/shard_map/ppermute | solution.py:27
  75.4 10.1 %collective-permute-start.11 = (bf16[24,32,256]{2,1,0:T(8,128)(2,1)S(1)}, bf16[24,32,256]{2,1,0:T(8,128)(2,1)S(1)}, u32[]{:S(2)}, u32[]{:S(2)}) collective-permute-start(bf16[24,32,256]{2,1,0:T(8,128)(2,1)S(1)} %get-tuple-element.63), channel_id=1, source_target_pairs={{0,255},{1,2},{2,1},{3,4},{4,3},{5,6},{6,5},{7,8},{8,7},{9,10},{10... | collective-permute-start | bytes 1179656 | tf_op jit(solution)/shard_map/ppermute | solution.py:27
  76.9 11.4 %collective-permute-start.12 = (bf16[24,32,256]{2,1,0:T(8,128)(2,1)S(1)}, bf16[24,32,256]{2,1,0:T(8,128)(2,1)S(1)}, u32[]{:S(2)}, u32[]{:S(2)}) collective-permute-start(bf16[24,32,256]{2,1,0:T(8,128)(2,1)S(1)} %get-tuple-element.64), channel_id=1, source_target_pairs={{0,1},{1,0},{2,3},{3,2},{4,5},{5,4},{6,7},{7,6},{8,9},{9,8},{10,11... | collective-permute-start | bytes 1179656 | tf_op jit(solution)/shard_map/ppermute | solution.py:27
  89.7 1.2 %collective-permute-start.13 = (f32[8,128]{1,0:T(8,128)S(1)}, f32[8,128]{1,0:T(8,128)S(1)}, u32[]{:S(2)}, u32[]{:S(2)}) collective-permute-start(f32[8,128]{1,0:T(8,128)S(1)} %get-tuple-element.65), channel_id=1, source_target_pairs={{0,4},{4,0},{8,12},{12,8},{16,20},{20,16},{24,28},{28,24},{32,36},... | collective-permute-start | bytes 12296 | tf_op jit(solution)/shard_map/ppermute | solution.py:27
  90.9 8.1 %collective-permute-start.16 = (f32[8,128]{1,0:T(8,128)S(1)}, f32[8,128]{1,0:T(8,128)S(1)}, u32[]{:S(2)}, u32[]{:S(2)}) collective-permute-start(f32[8,128]{1,0:T(8,128)S(1)} %add.16), channel_id=1, source_target_pairs={{0,3},{1,2},{2,1},{3,0},{4,7},{5,6},{6,5},{7,4},{8,11},{9,10},{10,... | collective-permute-start | bytes 12296 | tf_op jit(solution)/shard_map/ppermute | solution.py:27
  91.6 8.9 %collective-permute-start.15 = (f32[8,128]{1,0:T(8,128)S(1)}, f32[8,128]{1,0:T(8,128)S(1)}, u32[]{:S(2)}, u32[]{:S(2)}) collective-permute-start(f32[8,128]{1,0:T(8,128)S(1)} %add.16), channel_id=1, source_target_pairs={{0,2},{1,3},{2,0},{3,1},{4,6},{5,7},{6,4},{7,5},{8,10},{9,11},{10,... | collective-permute-start | bytes 12296 | tf_op jit(solution)/shard_map/ppermute | solution.py:27
  98.9 3.6 %collective-permute-start.14 = (f32[8,128]{1,0:T(8,128)S(1)}, f32[8,128]{1,0:T(8,128)S(1)}, u32[]{:S(2)}, u32[]{:S(2)}) collective-permute-start(f32[8,128]{1,0:T(8,128)S(1)} %add.16), channel_id=1, source_target_pairs={{0,1},{1,0},{2,3},{3,2},{4,5},{5,4},{6,7},{7,6},{8,9},{9,8},{10,11... | collective-permute-start | bytes 12296 | tf_op jit(solution)/shard_map/ppermute | solution.py:27

commit v4 on v3

--- a/solution.py
+++ b/solution.py
@@ -17,9 +17,11 @@
 VMEM = pl.BlockSpec(memory_space=pltpu.VMEM)
 CHUNK = 8
 DEAD = 24
-HALO_CHUNKS = 128
-OWN_CHUNKS = 129
-SPARE = 130
+ODD, EVEN, OWN = 0, 1, 2
+ROOM = 64
+CHUNKS = 3 * ROOM
+SPARE = CHUNKS + 3
+TABLE = CHUNKS + 8
 
 
 def swap(shard, axis, partner):
@@ -27,10 +29,12 @@
     return lax.ppermute(shard, axis, [(i, partner(i) % count) for i in range(count)])
 
 
-def ring_pairs(shard_odd, shard_even):
-    got_odd = swap(shard_odd, RING, lambda i: i + 1 if i % 2 else i - 1)
-    got_even = swap(shard_even, RING, lambda i: i - 1 if i % 2 else i + 1)
-    return got_odd, got_even
+def swap_odd(shard):
+    return swap(shard, RING, lambda i: i + 1 if i % 2 else i - 1)
+
+
+def swap_even(shard):
+    return swap(shard, RING, lambda i: i - 1 if i % 2 else i + 1)
 
 
 def gathered(part, axis, groups):
@@ -67,19 +71,19 @@
         left_ref[block] = jnp.where(owner == block, rows, 0.0).astype(BF16)
 
 
-def for_tiles(table_ref, own, visit):
-    first = 64 if own else 0
-
-    def chunk(number, carry):
-        for place in range(CHUNK):
-            entry = table_ref[first + number * CHUNK + place]
-            visit(entry >> 5, entry & 31)
-        return carry
-
-    lax.fori_loop(0, table_ref[OWN_CHUNKS if own else HALO_CHUNKS], chunk, 0)
-
-
-def push_rows(table_ref, own, tiles_ref, left_ref, window, split):
+def for_tiles(table_ref, lists, visit):
+    for number in lists:
+
+        def chunk(place, carry, first=number * ROOM):
+            for offset in range(CHUNK):
+                entry = table_ref[first + place * CHUNK + offset]
+                visit(entry >> 5, entry & 31)
+            return carry
+
+        lax.fori_loop(0, table_ref[CHUNKS + number], chunk, 0)
+
+
+def push_rows(table_ref, lists, tiles_ref, left_ref, window, split):
     height = window.shape[1]
     window[...] = jnp.zeros_like(window)
 
@@ -89,7 +93,7 @@
             product = product[:height] + product[height : 2 * height]
         window[target] += product[:height]
 
-    for_tiles(table_ref, own, visit)
+    for_tiles(table_ref, lists, visit)
 
 
 def landed(window, part, out):
@@ -98,7 +102,7 @@
         out[rows, :] = jnp.sum(window[part * 8 : (part + 1) * 8, rows, :], axis=1)
 
 
-def load_kernel(cols_hbm, count_hbm, tiles_hbm, start_hbm, tiles_ref, table_ref, inverse_ref, to_odd, to_even, left_ref,
+def load_kernel(cols_hbm, count_hbm, tiles_hbm, start_hbm, tiles_ref, table_ref, inverse_ref, to_odd, left_ref, to_even,
                 window, start_ref, cols_ref, count_ref, sems, small_sems):
     blocks, slots, width = tiles_hbm.shape[:3]
     small = [
@@ -116,11 +120,11 @@
     total_blocks = blocks * lax.axis_size("rows") * lax.axis_size("cols")
     place = lax.axis_index("rows") * lax.axis_size("cols") + lax.axis_index("cols")
     swapped = place % 2 == 1
-    for entry in range(128):
+    for entry in range(CHUNKS):
         table_ref[entry] = DEAD
     for copy in small:
         copy.wait()
-    halo_count, own_count = jnp.int32(0), jnp.int32(0)
+    counts = [jnp.int32(0)] * 3
     for block in range(blocks):
         for slot in range(slots):
             target = cols_ref[block, slot] - place * blocks + blocks
@@ -130,14 +134,15 @@
             flipped = jnp.where(target < blocks, target + 2 * blocks, target - 2 * blocks)
             target = jnp.where(swapped & jnp.logical_not(own), flipped, target)
             live = slot < count_ref[block]
-            to_own = live & own
-            to_halo = live & jnp.logical_not(own)
             entry = target + (block * slots + slot) * 32
-            table_ref[jnp.where(to_halo, halo_count, jnp.where(to_own, 64 + own_count, SPARE))] = entry
-            halo_count += jnp.where(to_halo, 1, 0)
-            own_count += jnp.where(to_own, 1, 0)
-    table_ref[HALO_CHUNKS] = (halo_count + CHUNK - 1) >> 3
-    table_ref[OWN_CHUNKS] = (own_count + CHUNK - 1) >> 3
+            chosen = [live & (target < blocks), live & (target >= 2 * blocks), live & own]
+            place_of = SPARE
+            for number in (ODD, EVEN, OWN):
+                place_of = jnp.where(chosen[number], number * ROOM + counts[number], place_of)
+                counts[number] += jnp.where(chosen[number], 1, 0)
+            table_ref[place_of] = entry
+    for number in (ODD, EVEN, OWN):
+        table_ref[CHUNKS + number] = (counts[number] + CHUNK - 1) >> 3
 
     ones = jnp.ones((16, 128), BF16)
 
@@ -167,36 +172,41 @@
     sums.append(row_sums(before))
     inverse = 1.0 / jnp.concatenate(sums, axis=0)
     inverse_ref[...] = inverse
-    halo_step(start_ref[...] * inverse, False, table_ref, tiles_ref, to_odd, to_even, left_ref, window)
-
-
-def halo_step(rows, split, table_ref, tiles_ref, to_odd, to_even, left_ref, window):
+    halo_step(start_ref[...] * inverse, False, table_ref, tiles_ref, to_odd, left_ref, to_even, window)
+
+
+def halo_step(rows, split, table_ref, tiles_ref, to_odd, left_ref, *rest):
+    window = rest[-1]
     spread_blocks(jnp.concatenate(two_parts(rows), axis=0) if split else rows, left_ref)
-    push_rows(table_ref, False, tiles_ref, left_ref, window, split)
+    push_rows(table_ref, (ODD,) if len(rest) == 1 else (ODD, EVEN), tiles_ref, left_ref, window, split)
     landed(window, 0, to_odd)
-    landed(window, 2, to_even)
-
-
-def second_kernel(table_ref, tiles_ref, inverse_ref, odd, own, even, to_odd, to_even, left_ref, value_ref, window):
+    if len(rest) > 1:
+        landed(window, 2, rest[0])
+
+
+def second_kernel(table_ref, tiles_ref, inverse_ref, odd, own, even, to_odd, left_ref, value_ref, *rest):
     raw = 0.85 * (own[...] + odd[...] + even[...]) + 0.15
     value_ref[...] = raw
     inverse = inverse_ref[...]
     rows = jnp.concatenate([raw * inverse, inverse], axis=0)
-    halo_step(rows, True, table_ref, tiles_ref, to_odd, to_even, left_ref, window)
-
-
-def chain_kernel(channels, table_ref, tiles_ref, inverse_ref, odd, own, even, to_odd, to_even, left_ref, value_ref, window):
+    halo_step(rows, True, table_ref, tiles_ref, to_odd, left_ref, *rest)
+
+
+def chain_kernel(channels, table_ref, tiles_ref, inverse_ref, odd, own, even, to_odd, left_ref, value_ref, *rest):
     value = own[...] + odd[...] + even[...]
     value_ref[...] = value
     inverse = inverse_ref[...]
     rows = [value[8 * c : 8 * c + 8] * inverse for c in range(channels)]
     rows = jnp.concatenate(rows, axis=0) if channels > 1 else rows[0]
-    halo_step(rows, True, table_ref, tiles_ref, to_odd, to_even, left_ref, window)
-
-
-def own_kernel(split, table_ref, tiles_ref, left_ref, kept, window):
-    push_rows(table_ref, True, tiles_ref, left_ref, window, split)
+    halo_step(rows, True, table_ref, tiles_ref, to_odd, left_ref, *rest)
+
+
+def own_kernel(split, table_ref, tiles_ref, left_ref, kept, *rest):
+    window = rest[-1]
+    push_rows(table_ref, (OWN,) if len(rest) == 1 else (EVEN, OWN), tiles_ref, left_ref, window, split)
     landed(window, 1, kept)
+    if len(rest) > 1:
+        landed(window, 2, rest[0])
 
 
 def sums_kernel(raw_ref, second_ref, third_ref, odd, own, even, out_ref):
@@ -246,8 +256,8 @@
     return scale_1, scale_2, scale_3, scale_4
 
 
-def replay_kernel(zones, table_ref, tiles_ref, inverse_ref, sums_ref, raw_ref, second_ref, third_ref, to_odd, to_even, left_ref,
-                  scales_ref, window):
+def replay_kernel(zones, table_ref, tiles_ref, inverse_ref, sums_ref, raw_ref, second_ref, third_ref, to_odd, left_ref,
+                  scales_ref, to_even, window):
     scales = scales_of(sums_ref[...], zones)
     for place, scale in enumerate(scales):
         scales_ref[place : place + 1, :] = jnp.broadcast_to(scale, (1, 128))
@@ -258,7 +268,7 @@
 
     def own_products(rows):
         spread_blocks(rows, left_ref)
-        push_rows(table_ref, True, tiles_ref, left_ref, window, False)
+        push_rows(table_ref, (OWN,), tiles_ref, left_ref, window, False)
         return jnp.sum(window[blocks : 2 * blocks], axis=1)
 
     def rounded(rows):
@@ -270,7 +280,7 @@
     chain_3 = a3 * (a2 * third_ref[0:blocks] + 0.15 * second_ref[blocks : 2 * blocks]) + 0.15
     weights_3 = rounded((raw_2 * scales[1]) * inverse)
     raw_3 = chain_3 + 0.85 * own_products(weights_3 - (chain_2 * scales[1]) * inverse)
-    halo_step((raw_3 * scales[2]) * inverse, False, table_ref, tiles_ref, to_odd, to_even, left_ref, window)
+    halo_step((raw_3 * scales[2]) * inverse, False, table_ref, tiles_ref, to_odd, left_ref, to_even, window)
 
 
 def transposed_kernel(table_ref, tiles_ref, inverse_ref, scales_ref, odd, own, even, probe_ref, to_odd, to_even, pushed_ref, scaled_ref, root_ref, window):
@@ -292,7 +302,7 @@
     def visit(tile, target):
         window[target] += jnp.dot(pushed_ref[tile >> 3], tiles_ref[tile], preferred_element_type=F32)
 
-    for_tiles(table_ref, False, visit)
+    for_tiles(table_ref, (ODD, EVEN), visit)
     for part, out in ((0, to_odd), (2, to_even)):
         for block in range(blocks):
             high, low = two_parts(window[part * blocks + block])
@@ -314,7 +324,7 @@
         left = scaled_ref[jnp.where(dead, 0, place)]
         forward[jnp.where(dead, blocks, block)] += lax.dot_general(left, matrix, LAST_DIMS, preferred_element_type=F32)
 
-    for_tiles(table_ref, True, visit)
+    for_tiles(table_ref, (OWN,), visit)
     kept[...] = window[0:blocks]
     forward_ref[...] = forward[0:blocks]
 
@@ -332,7 +342,7 @@
         place = jnp.where(dead, blocks, tile >> 3)
         forward[place] += lax.dot_general(left, tiles_ref[tile], LAST_DIMS, preferred_element_type=F32)
 
-    for_tiles(table_ref, False, visit)
+    for_tiles(table_ref, (ODD, EVEN), visit)
     root = root_ref[...]
     inverse_root = 1.0 / root
     gain = root * inverse_ref[...]
@@ -402,11 +412,11 @@
     def window(channels, kind=F32, places=3 * blocks + 1):
         return pltpu.VMEM((places, channels, width), kind)
 
-    tiles, table, inverse, to_odd, to_even, left = call(
+    tiles, table, inverse, to_odd, left, to_even = call(
         load_kernel, "load",
         [
-            pltpu.VMEM((blocks * slots, width, width), BF16), pltpu.SMEM((136,), jnp.int32), rows(), rows(), rows(),
-            jax.ShapeDtypeStruct((blocks, 16, width), BF16),
+            pltpu.VMEM((blocks * slots, width, width), BF16), pltpu.SMEM((TABLE,), jnp.int32), rows(), rows(),
+            jax.ShapeDtypeStruct((blocks, 16, width), BF16), rows(),
         ],
         [pltpu.with_memory_space_constraint(x, pltpu.HBM) for x in (tile_cols, tile_count, tile_blocks, start_mass)],
         [pl.BlockSpec(memory_space=pltpu.HBM)] * 4,
@@ -419,35 +429,37 @@
     tiles = pltpu.with_memory_space_constraint(tiles, pltpu.VMEM)
     table = pltpu.with_memory_space_constraint(table, pltpu.SMEM)
 
-    def exchange(to_odd, to_even, left, name, channels, split):
-        odd, even = ring_pairs(to_odd, to_even)
-        (own,) = call(
-            functools.partial(own_kernel, split), name + "_own", [rows(channels)], (table, tiles, left), [SMEM] + [VMEM] * 2,
+    def exchange(to_odd, left, name, channels, split, to_even=None):
+        odd = swap_odd(to_odd)
+        outs = [rows(channels)] * (1 if to_even is not None else 2)
+        own, *made = call(
+            functools.partial(own_kernel, split), name + "_own", outs, (table, tiles, left), [SMEM] + [VMEM] * 2,
             [window(channels * blocks)], flops=1 << 25, moved=1 << 22,
         )
-        return odd, own, even
-
-    odd, own, even = exchange(to_odd, to_even, left, "first", 1, False)
-
-    def step(kernel, name, channels, split, operands, extra):
+        return odd, own, swap_even(made[0] if made else to_even)
+
+    odd, own, even = exchange(to_odd, left, "first", 1, False, to_even)
+
+    def step(kernel, name, channels, split, operands, extra, both):
         height = max(16, channels * blocks * (2 if split else 1))
         left = jax.ShapeDtypeStruct((blocks, height, width), BF16)
-        to_odd, to_even, left, *extra = call(
-            kernel, name, [rows(channels)] * 2 + [left] + extra, (table, tiles, inverse, *operands),
+        to_odd, left, *extra = call(
+            kernel, name, [rows(channels), left] + extra + [rows(channels)] * both, (table, tiles, inverse, *operands),
             [SMEM] + [VMEM] * (2 + len(operands)), [window(channels * blocks)], flops=1 << 24, moved=1 << 21,
         )
-        return *exchange(to_odd, to_even, left, name, channels, split), *extra
-
-    odd, own, even, raw = step(second_kernel, "second", 2, True, (odd, own, even), [rows()])
-    odd, own, even, second = step(functools.partial(chain_kernel, 2), "third", 2, True, (odd, own, even), [rows(2)])
-    odd, own, even, third = step(functools.partial(chain_kernel, 1), "fourth", 1, True, (odd, own, even), [rows(2)])
+        to_even = extra.pop() if both else None
+        return *exchange(to_odd, left, name, channels, split, to_even), *extra
+
+    odd, own, even, raw = step(second_kernel, "second", 2, True, (odd, own, even), [rows()], False)
+    odd, own, even, second = step(functools.partial(chain_kernel, 2), "third", 2, True, (odd, own, even), [rows(2)], False)
+    odd, own, even, third = step(functools.partial(chain_kernel, 1), "fourth", 1, True, (odd, own, even), [rows(2)], True)
     (sums,) = call(
         sums_kernel, "sums", [jax.ShapeDtypeStruct((1, 128), F32)], (raw, second, third, odd, own, even), [VMEM] * 6, []
     )
     sums = chip_parts(sums[0])
     odd, own, even, scales = step(
         functools.partial(replay_kernel, zones), "replay", 1, False, (sums, raw, second, third),
-        [jax.ShapeDtypeStruct((8, 128), F32)],
+        [jax.ShapeDtypeStruct((8, 128), F32)], True,
     )
 
     message = jax.ShapeDtypeStruct((3 * blocks, chans, width), BF16)
@@ -457,7 +469,7 @@
         transposed_kernel, "transposed", [message, message, narrow, narrow, rows()],
         (table, tiles, inverse, scales, odd, own, even, probe_block), [SMEM] + [VMEM] * 7, [window(chans)],
     )
-    odd, even = ring_pairs(to_odd, to_even)
+    odd, even = swap_odd(to_odd), swap_even(to_even)
     kept, forward = call(
         own_products_kernel, "own_products", [wide, wide], (table, tiles, pushed, scaled), [SMEM] + [VMEM] * 3,
         [window(chans, places=blocks + 1)] * 2, flops=1 << 28, moved=1 << 23,

time: 119 us -> 118 us (level)
  starting transfers between devices: 47.9 us -> 41.6 us
  Pallas kernels: 20.4 us -> 24.9 us
  waiting for transfers between devices: 14.2 us -> 15.8 us
    ppermute x17, starting transfers between devices: 47.9 us -> 41.6 us  [swap(): lax.ppermute(shard, axis, [(i, partner(i) % count) for i in range(count)])]
    pallas_call x15, Pallas kernels: 20.4 us -> 24.9 us  [call(): pl.pallas_call(kernel, out_shape=outs, in_specs=specs, out_specs=out_spec...]
    ppermute x17, waiting for transfers between devices: 14.2 us -> 15.8 us  [swap(): lax.ppermute(shard, axis, [(i, partner(i) % count) for i in range(count)])]
  transfers between devices with their start and end apart: 17 -> 17, of which waited for: 12 -> 12; matrix products, arithmetic and copies ran while one was open for 0% -> 0% of each run, Pallas kernels for 5% -> 8%
where the time goes in v4:
time: 118 us; the launch traced here: 117 us
  starting transfers between devices  41.6 us (35%)
  blocking collectives  34.4 us (29%)
  Pallas kernels  24.9 us (21%)
  waiting for transfers between devices  15.8 us (13%)
    ppermute x17, starting transfers between devices, swap(): lax.ppermute(shard, axis, [(i, partner(i) % count) for i in range(count)])  41.6 us
    all_to_all x2, blocking collectives, gathered(): lax.all_to_all(spread, axis, 0, 0, tiled=True, axis_index_groups=groups)  34.4 us
    pallas_call x15, Pallas kernels, call(): pl.pallas_call(kernel, out_shape=outs, in_specs=specs, out_specs=out_spec...  24.9 us
    ppermute x17, waiting for transfers between devices, swap(): lax.ppermute(shard, axis, [(i, partner(i) % count) for i in range(count)])  15.8 us
  transfers between devices with their start and end apart: 17, of which 12 were waited for; matrix products, arithmetic and copies ran while one was open for 0% of the time, Pallas kernels for 8%

profile of v4, /device:TPU:2, one launch (start us, length us, event | category | flops | bytes accessed | tf_op | source)
XLA Modules:
  0.0 117.2 jit_solution(4563949455894136664)
XLA Ops:
  0.0 5.9 %load.1 = (bf16[64,256,256]{2,1,0:T(8,128)(2,1)S(1)}, s32[200]{0:T(256)S(4)}, f32[8,256]{1,0:T(8,128)S(1)}, f32[8,256]{1,0:T(8,128)S(1)}, bf16[8,16,256]{2,1,0:T(8,128)(2,1)S(1)}, /*index=5*/f32[8,256]{1,0:T(8,128)S(1)}) custom-call(s32[8,8]{1,0:T(8,128)} %cols_hbm.1, s32[8]{0:T(128)} %count_hbm.1, bf16[8,8,256,256]{3,2,1,0:T(8,128)(2,1)} %tiles_hbm.1, ...), custom_call_target="tpu_custom_call" | custom-call | tf_op jit(solution)/shard_map/load/pallas_call | solution.py:392
  6.0 1.8 %collective-permute-start = (f32[8,256]{1,0:T(8,128)S(1)}, f32[8,256]{1,0:T(8,128)S(1)}, u32[]{:S(2)}, u32[]{:S(2)}) collective-permute-start(f32[8,256]{1,0:T(8,128)S(1)} %get-tuple-element.41), channel_id=1, source_target_pairs={{0,255},{1,2},{2,1},{3,4},{4,3},{5,6},{6,5},{7,8},{8,7},{9,10},{10... | collective-permute-start | bytes 24584 | tf_op jit(solution)/shard_map/ppermute | solution.py:29
  7.8 8.7 %collective-permute-start.1 = (f32[8,256]{1,0:T(8,128)S(1)}, f32[8,256]{1,0:T(8,128)S(1)}, u32[]{:S(2)}, u32[]{:S(2)}) collective-permute-start(f32[8,256]{1,0:T(8,128)S(1)} %get-tuple-element.43), channel_id=1, source_target_pairs={{0,1},{1,0},{2,3},{3,2},{4,5},{5,4},{6,7},{7,6},{8,9},{9,8},{10,11... | collective-permute-start | bytes 24584 | tf_op jit(solution)/shard_map/ppermute | solution.py:29
  16.5 1.0 first_own.1.own
  18.6 1.8 %second_own.1 = (f32[16,256]{1,0:T(8,128)S(1)}, f32[16,256]{1,0:T(8,128)S(1)}) custom-call(s32[200]{0:T(256)S(4)} %get-tuple-element.38.table_ref, bf16[64,256,256]{2,1,0:T(8,128)(2,1)S(1)} %get-tuple-element.39.tiles_ref, bf16[8,32,256]{2,1,0:T(8,128)(2,1)S(1)} %get-tuple-element.46.left_ref), custom_call_target="tpu_custom_call" | custom-call | flops 33554432 | bytes 4194304 | tf_op jit(solution)/shard_map/second_own/pallas_call | solution.py:392
  20.5 6.1 %collective-permute-start.3 = (f32[16,256]{1,0:T(8,128)S(1)}, f32[16,256]{1,0:T(8,128)S(1)}, u32[]{:S(2)}, u32[]{:S(2)}) collective-permute-start(f32[16,256]{1,0:T(8,128)S(1)} %get-tuple-element.48), channel_id=1, source_target_pairs={{0,1},{1,0},{2,3},{3,2},{4,5},{5,4},{6,7},{7,6},{8,9},{9,8},{10,11... | collective-permute-start | bytes 49160 | tf_op jit(solution)/shard_map/ppermute | solution.py:29
  26.5 1.7 %collective-permute-done.3.even = f32[16,256]{1,0:T(8,128)S(1)} collective-permute-done((f32[16,256]{1,0:T(8,128)S(1)}, f32[16,256]{1,0:T(8,128)S(1)}, u32[]{:S(2)}, u32[]{:S(2)}) %collective-permute-start.3) | collective-permute-done | bytes 16416 | tf_op jit(solution)/shard_map/ppermute | solution.py:29
  28.7 1.8 %third_own.1 = (f32[16,256]{1,0:T(8,128)S(1)}, f32[16,256]{1,0:T(8,128)S(1)}) custom-call(s32[200]{0:T(256)S(4)} %get-tuple-element.38.table_ref, bf16[64,256,256]{2,1,0:T(8,128)(2,1)S(1)} %get-tuple-element.39.tiles_ref, bf16[8,32,256]{2,1,0:T(8,128)(2,1)S(1)} %get-tuple-element.51.left_ref), custom_call_target="tpu_custom_call" | custom-call | flops 33554432 | bytes 4194304 | tf_op jit(solution)/shard_map/third_own/pallas_call | solution.py:392
  30.6 5.0 %collective-permute-start.5 = (f32[16,256]{1,0:T(8,128)S(1)}, f32[16,256]{1,0:T(8,128)S(1)}, u32[]{:S(2)}, u32[]{:S(2)}) collective-permute-start(f32[16,256]{1,0:T(8,128)S(1)} %get-tuple-element.53), channel_id=1, source_target_pairs={{0,1},{1,0},{2,3},{3,2},{4,5},{5,4},{6,7},{7,6},{8,9},{9,8},{10,11... | collective-permute-start | bytes 49160 | tf_op jit(solution)/shard_map/ppermute | solution.py:29
  35.6 1.7 %collective-permute-done.5.even = f32[16,256]{1,0:T(8,128)S(1)} collective-permute-done((f32[16,256]{1,0:T(8,128)S(1)}, f32[16,256]{1,0:T(8,128)S(1)}, u32[]{:S(2)}, u32[]{:S(2)}) %collective-permute-start.5) | collective-permute-done | bytes 16416 | tf_op jit(solution)/shard_map/ppermute | solution.py:29
  37.3 0.8 fourth.1
  38.2 5.8 %collective-permute-start.7 = (f32[8,256]{1,0:T(8,128)S(1)}, f32[8,256]{1,0:T(8,128)S(1)}, u32[]{:S(2)}, u32[]{:S(2)}) collective-permute-start(f32[8,256]{1,0:T(8,128)S(1)} %get-tuple-element.57), channel_id=1, source_target_pairs={{0,1},{1,0},{2,3},{3,2},{4,5},{5,4},{6,7},{7,6},{8,9},{9,8},{10,11... | collective-permute-start | bytes 24584 | tf_op jit(solution)/shard_map/ppermute | solution.py:29
  44.0 1.1 fourth_own.1.own
  45.8 1.1 collective-permute-done.8
  47.0 20.7 %all_to_all.13 = f32[128,1,128]{2,1,0:T(1,128)S(1)} all-to-all(f32[128,1,128]{2,1,0:T(1,128)S(1)} %broadcast_in_dim.4), channel_id=1, replica_groups={{0,1,2,3,8,9,10,11,16,17,18,19,24,25,26,27,32,33,34,35,40,41,42,43,48,4..., dimensions={0} | all-to-all | bytes 131072 | tf_op jit(solution)/shard_map/all_to_all | solution.py:42
  67.7 3.2 %replay.1 = (f32[8,256]{1,0:T(8,128)S(1)}, bf16[8,16,256]{2,1,0:T(8,128)(2,1)S(1)}, f32[8,128]{1,0:T(8,128)S(1)}, f32[8,256]{1,0:T(8,128)S(1)}) custom-call(s32[200]{0:T(256)S(4)} %get-tuple-element.38.table_ref, bf16[64,256,256]{2,1,0:T(8,128)(2,1)S(1)} %get-tuple-element.39.tiles_ref, f32[8,256]{1,0:T(8,128)S(1)} %get-tuple-element.40.inverse_ref, ...), custom_call_target="tpu_custom_call" | custom-call | flops 16777216 | bytes 2097152 | tf_op jit(solution)/shard_map/replay/pallas_call | solution.py:392
  71.6 1.1 replay_own.1.own
  72.7 2.0 %collective-permute-done.9.odd = f32[8,256]{1,0:T(8,128)S(1)} collective-permute-done((f32[8,256]{1,0:T(8,128)S(1)}, f32[8,256]{1,0:T(8,128)S(1)}, u32[]{:S(2)}, u32[]{:S(2)}) %collective-permute-start.9) | collective-permute-done | bytes 8224 | tf_op jit(solution)/shard_map/ppermute | solution.py:29
  74.7 1.1 transposed.1
  75.8 2.3 %collective-permute-start.11 = (bf16[24,32,256]{2,1,0:T(8,128)(2,1)S(1)}, bf16[24,32,256]{2,1,0:T(8,128)(2,1)S(1)}, u32[]{:S(2)}, u32[]{:S(2)}) collective-permute-start(bf16[24,32,256]{2,1,0:T(8,128)(2,1)S(1)} %get-tuple-element.67), channel_id=1, source_target_pairs={{0,255},{1,2},{2,1},{3,4},{4,3},{5,6},{6,5},{7,8},{8,7},{9,10},{10... | collective-permute-start | bytes 1179656 | tf_op jit(solution)/shard_map/ppermute | solution.py:29
  78.1 3.9 %collective-permute-start.12 = (bf16[24,32,256]{2,1,0:T(8,128)(2,1)S(1)}, bf16[24,32,256]{2,1,0:T(8,128)(2,1)S(1)}, u32[]{:S(2)}, u32[]{:S(2)}) collective-permute-start(bf16[24,32,256]{2,1,0:T(8,128)(2,1)S(1)} %get-tuple-element.68), channel_id=1, source_target_pairs={{0,1},{1,0},{2,3},{3,2},{4,5},{5,4},{6,7},{7,6},{8,9},{9,8},{10,11... | collective-permute-start | bytes 1179656 | tf_op jit(solution)/shard_map/ppermute | solution.py:29
  82.0 2.5 %own_products.1 = (f32[8,32,256]{2,1,0:T(8,128)S(1)}, f32[8,32,256]{2,1,0:T(8,128)S(1)}) custom-call(s32[200]{0:T(256)S(4)} %get-tuple-element.38.table_ref, bf16[64,256,256]{2,1,0:T(8,128)(2,1)S(1)} %get-tuple-element.39.tiles_ref, bf16[8,32,256]{2,1,0:T(8,128)(2,1)S(1)} %get-tuple-element.63.pushed_ref, bf16[8,32,256]{2,1,0:T(8,128)(2,1)S(1)} %get-tuple-element.64.scaled_ref), custom_call_target="tpu_custom_call" | custom-call | flops 268435456 | bytes 8388608 | tf_op jit(solution)/shard_map/own_products/pallas_call | solution.py:392
  84.5 1.5 %collective-permute-done.11.odd = bf16[24,32,256]{2,1,0:T(8,128)(2,1)S(1)} collective-permute-done((bf16[24,32,256]{2,1,0:T(8,128)(2,1)S(1)}, bf16[24,32,256]{2,1,0:T(8,128)(2,1)S(1)}, u32[]{:S(2)}, u32[]{:S(2)}) %collective-permute-start.11) | collective-permute-done | bytes 393248 | tf_op jit(solution)/shard_map/ppermute | solution.py:29
  86.0 1.8 %collective-permute-done.12.even = bf16[24,32,256]{2,1,0:T(8,128)(2,1)S(1)} collective-permute-done((bf16[24,32,256]{2,1,0:T(8,128)(2,1)S(1)}, bf16[24,32,256]{2,1,0:T(8,128)(2,1)S(1)}, u32[]{:S(2)}, u32[]{:S(2)}) %collective-permute-start.12) | collective-permute-done | bytes 393248 | tf_op jit(solution)/shard_map/ppermute | solution.py:29
  87.8 1.8 %embed.1 = (f32[32,2048]{1,0:T(8,128)S(1)}, f32[8,128]{1,0:T(8,128)S(1)}) custom-call(s32[200]{0:T(256)S(4)} %get-tuple-element.38.table_ref, bf16[64,256,256]{2,1,0:T(8,128)(2,1)S(1)} %get-tuple-element.39.tiles_ref, f32[8,256]{1,0:T(8,128)S(1)} %get-tuple-element.40.inverse_ref, f32[8,256]{1,0:T(8,128)S(1)} %get-tuple-element.62.root_ref, ...), custom_call_target="tpu_custom_call" | custom-call | tf_op jit(solution)/shard_map/embed/pallas_call | solution.py:392
  89.6 1.2 collective-permute-done.13
  90.8 2.4 %collective-permute-start.16 = (f32[8,128]{1,0:T(8,128)S(1)}, f32[8,128]{1,0:T(8,128)S(1)}, u32[]{:S(2)}, u32[]{:S(2)}) collective-permute-start(f32[8,128]{1,0:T(8,128)S(1)} %add.16), channel_id=1, source_target_pairs={{0,3},{1,2},{2,1},{3,0},{4,7},{5,6},{6,5},{7,4},{8,11},{9,10},{10,... | collective-permute-start | bytes 12296 | tf_op jit(solution)/shard_map/ppermute | solution.py:29
  93.2 4.6 %collective-permute-start.15 = (f32[8,128]{1,0:T(8,128)S(1)}, f32[8,128]{1,0:T(8,128)S(1)}, u32[]{:S(2)}, u32[]{:S(2)}) collective-permute-start(f32[8,128]{1,0:T(8,128)S(1)} %add.16), channel_id=1, source_target_pairs={{0,2},{1,3},{2,0},{3,1},{4,6},{5,7},{6,4},{7,5},{8,10},{9,11},{10,... | collective-permute-start | bytes 12296 | tf_op jit(solution)/shard_map/ppermute | solution.py:29
  97.8 1.6 %collective-permute-done.15 = f32[8,128]{1,0:T(8,128)S(1)} collective-permute-done((f32[8,128]{1,0:T(8,128)S(1)}, f32[8,128]{1,0:T(8,128)S(1)}, u32[]{:S(2)}, u32[]{:S(2)}) %collective-permute-start.15) | collective-permute-done | bytes 4128 | tf_op jit(solution)/shard_map/ppermute | solution.py:29
  99.3 2.0 %collective-permute-done.14 = f32[8,128]{1,0:T(8,128)S(1)} collective-permute-done((f32[8,128]{1,0:T(8,128)S(1)}, f32[8,128]{1,0:T(8,128)S(1)}, u32[]{:S(2)}, u32[]{:S(2)}) %collective-permute-start.14) | collective-permute-done | bytes 4128 | tf_op jit(solution)/shard_map/ppermute | solution.py:29
  101.4 13.7 %all_to_all.14.gram_ref = f32[32,8,128]{2,1,0:T(8,128)S(1)} all-to-all(f32[32,8,128]{2,1,0:T(8,128)S(1)} %broadcast_in_dim.5), channel_id=1, replica_groups={{0,8,16,24,32,40,48,56,64,72,80,88,96,104,112,120,128,136,144,152,160,1..., dimensions={0} | all-to-all | bytes 262144 | tf_op jit(solution)/shard_map/all_to_all | solution.py:42
  115.1 1.9 %basis.1 = f32[32,2048]{1,0:T(8,128)} custom-call(f32[32,8,128]{2,1,0:T(8,128)S(1)} %all_to_all.14.gram_ref, f32[32,2048]{1,0:T(8,128)S(1)} %get-tuple-element.70.embedded_ref), custom_call_target="tpu_custom_call" | custom-call | tf_op jit(solution)/shard_map/basis/pallas_call | solution.py:392
  (26 shorter events, 3.2 us)
Async XLA Ops:
  6.0 11.6 %collective-permute-start = (f32[8,256]{1,0:T(8,128)S(1)}, f32[8,256]{1,0:T(8,128)S(1)}, u32[]{:S(2)}, u32[]{:S(2)}) collective-permute-start(f32[8,256]{1,0:T(8,128)S(1)} %get-tuple-element.41), channel_id=1, source_target_pairs={{0,255},{1,2},{2,1},{3,4},{4,3},{5,6},{6,5},{7,8},{8,7},{9,10},{10... | collective-permute-start | bytes 24584 | tf_op jit(solution)/shard_map/ppermute | solution.py:29
  7.8 10.4 %collective-permute-start.1 = (f32[8,256]{1,0:T(8,128)S(1)}, f32[8,256]{1,0:T(8,128)S(1)}, u32[]{:S(2)}, u32[]{:S(2)}) collective-permute-start(f32[8,256]{1,0:T(8,128)S(1)} %get-tuple-element.43), channel_id=1, source_target_pairs={{0,1},{1,0},{2,3},{3,2},{4,5},{5,4},{6,7},{7,6},{8,9},{9,8},{10,11... | collective-permute-start | bytes 24584 | tf_op jit(solution)/shard_map/ppermute | solution.py:29
  18.5 8.0 %collective-permute-start.2 = (f32[16,256]{1,0:T(8,128)S(1)}, f32[16,256]{1,0:T(8,128)S(1)}, u32[]{:S(2)}, u32[]{:S(2)}) collective-permute-start(f32[16,256]{1,0:T(8,128)S(1)} %get-tuple-element.45), channel_id=1, source_target_pairs={{0,255},{1,2},{2,1},{3,4},{4,3},{5,6},{6,5},{7,8},{8,7},{9,10},{10... | collective-permute-start | bytes 49160 | tf_op jit(solution)/shard_map/ppermute | solution.py:29
  20.5 7.8 %collective-permute-start.3 = (f32[16,256]{1,0:T(8,128)S(1)}, f32[16,256]{1,0:T(8,128)S(1)}, u32[]{:S(2)}, u32[]{:S(2)}) collective-permute-start(f32[16,256]{1,0:T(8,128)S(1)} %get-tuple-element.48), channel_id=1, source_target_pairs={{0,1},{1,0},{2,3},{3,2},{4,5},{5,4},{6,7},{7,6},{8,9},{9,8},{10,11... | collective-permute-start | bytes 49160 | tf_op jit(solution)/shard_map/ppermute | solution.py:29
  28.6 7.0 %collective-permute-start.4 = (f32[16,256]{1,0:T(8,128)S(1)}, f32[16,256]{1,0:T(8,128)S(1)}, u32[]{:S(2)}, u32[]{:S(2)}) collective-permute-start(f32[16,256]{1,0:T(8,128)S(1)} %get-tuple-element.50), channel_id=1, source_target_pairs={{0,255},{1,2},{2,1},{3,4},{4,3},{5,6},{6,5},{7,8},{8,7},{9,10},{10... | collective-permute-start | bytes 49160 | tf_op jit(solution)/shard_map/ppermute | solution.py:29
  30.6 6.7 %collective-permute-start.5 = (f32[16,256]{1,0:T(8,128)S(1)}, f32[16,256]{1,0:T(8,128)S(1)}, u32[]{:S(2)}, u32[]{:S(2)}) collective-permute-start(f32[16,256]{1,0:T(8,128)S(1)} %get-tuple-element.53), channel_id=1, source_target_pairs={{0,1},{1,0},{2,3},{3,2},{4,5},{5,4},{6,7},{7,6},{8,9},{9,8},{10,11... | collective-permute-start | bytes 49160 | tf_op jit(solution)/shard_map/ppermute | solution.py:29
  38.1 7.0 %collective-permute-start.6 = (f32[8,256]{1,0:T(8,128)S(1)}, f32[8,256]{1,0:T(8,128)S(1)}, u32[]{:S(2)}, u32[]{:S(2)}) collective-permute-start(f32[8,256]{1,0:T(8,128)S(1)} %get-tuple-element.55), channel_id=1, source_target_pairs={{0,255},{1,2},{2,1},{3,4},{4,3},{5,6},{6,5},{7,8},{8,7},{9,10},{10... | collective-permute-start | bytes 24584 | tf_op jit(solution)/shard_map/ppermute | solution.py:29
  38.2 7.4 %collective-permute-start.7 = (f32[8,256]{1,0:T(8,128)S(1)}, f32[8,256]{1,0:T(8,128)S(1)}, u32[]{:S(2)}, u32[]{:S(2)}) collective-permute-start(f32[8,256]{1,0:T(8,128)S(1)} %get-tuple-element.57), channel_id=1, source_target_pairs={{0,1},{1,0},{2,3},{3,2},{4,5},{5,4},{6,7},{7,6},{8,9},{9,8},{10,11... | collective-permute-start | bytes 24584 | tf_op jit(solution)/shard_map/ppermute | solution.py:29
  45.8 1.1 collective-permute-start.8
  67.7 7.1 %copy-start = (bf16[32,2048]{1,0:T(8,128)(2,1)S(1)}, bf16[32,2048]{1,0:T(8,128)(2,1)}, u32[]{:S(2)}) copy-start(bf16[32,2048]{1,0:T(8,128)(2,1)} %probe_ref.1) | copy-start | bytes 393220
  70.9 3.7 %collective-permute-start.9 = (f32[8,256]{1,0:T(8,128)S(1)}, f32[8,256]{1,0:T(8,128)S(1)}, u32[]{:S(2)}, u32[]{:S(2)}) collective-permute-start(f32[8,256]{1,0:T(8,128)S(1)} %get-tuple-element.59), channel_id=1, source_target_pairs={{0,255},{1,2},{2,1},{3,4},{4,3},{5,6},{6,5},{7,8},{8,7},{9,10},{10... | collective-permute-start | bytes 24584 | tf_op jit(solution)/shard_map/ppermute | solution.py:29
  71.0 3.7 %collective-permute-start.10 = (f32[8,256]{1,0:T(8,128)S(1)}, f32[8,256]{1,0:T(8,128)S(1)}, u32[]{:S(2)}, u32[]{:S(2)}) collective-permute-start(f32[8,256]{1,0:T(8,128)S(1)} %get-tuple-element.61), channel_id=1, source_target_pairs={{0,1},{1,0},{2,3},{3,2},{4,5},{5,4},{6,7},{7,6},{8,9},{9,8},{10,11... | collective-permute-start | bytes 24584 | tf_op jit(solution)/shard_map/ppermute | solution.py:29
  75.8 10.2 %collective-permute-start.11 = (bf16[24,32,256]{2,1,0:T(8,128)(2,1)S(1)}, bf16[24,32,256]{2,1,0:T(8,128)(2,1)S(1)}, u32[]{:S(2)}, u32[]{:S(2)}) collective-permute-start(bf16[24,32,256]{2,1,0:T(8,128)(2,1)S(1)} %get-tuple-element.67), channel_id=1, source_target_pairs={{0,255},{1,2},{2,1},{3,4},{4,3},{5,6},{6,5},{7,8},{8,7},{9,10},{10... | collective-permute-start | bytes 1179656 | tf_op jit(solution)/shard_map/ppermute | solution.py:29
  78.1 9.7 %collective-permute-start.12 = (bf16[24,32,256]{2,1,0:T(8,128)(2,1)S(1)}, bf16[24,32,256]{2,1,0:T(8,128)(2,1)S(1)}, u32[]{:S(2)}, u32[]{:S(2)}) collective-permute-start(bf16[24,32,256]{2,1,0:T(8,128)(2,1)S(1)} %get-tuple-element.68), channel_id=1, source_target_pairs={{0,1},{1,0},{2,3},{3,2},{4,5},{5,4},{6,7},{7,6},{8,9},{9,8},{10,11... | collective-permute-start | bytes 1179656 | tf_op jit(solution)/shard_map/ppermute | solution.py:29
  89.6 1.2 %collective-permute-start.13 = (f32[8,128]{1,0:T(8,128)S(1)}, f32[8,128]{1,0:T(8,128)S(1)}, u32[]{:S(2)}, u32[]{:S(2)}) collective-permute-start(f32[8,128]{1,0:T(8,128)S(1)} %get-tuple-element.69), channel_id=1, source_target_pairs={{0,4},{4,0},{8,12},{12,8},{16,20},{20,16},{24,28},{28,24},{32,36},... | collective-permute-start | bytes 12296 | tf_op jit(solution)/shard_map/ppermute | solution.py:29
  90.8 7.0 %collective-permute-start.16 = (f32[8,128]{1,0:T(8,128)S(1)}, f32[8,128]{1,0:T(8,128)S(1)}, u32[]{:S(2)}, u32[]{:S(2)}) collective-permute-start(f32[8,128]{1,0:T(8,128)S(1)} %add.16), channel_id=1, source_target_pairs={{0,3},{1,2},{2,1},{3,0},{4,7},{5,6},{6,5},{7,4},{8,11},{9,10},{10,... | collective-permute-start | bytes 12296 | tf_op jit(solution)/shard_map/ppermute | solution.py:29
  93.2 6.2 %collective-permute-start.15 = (f32[8,128]{1,0:T(8,128)S(1)}, f32[8,128]{1,0:T(8,128)S(1)}, u32[]{:S(2)}, u32[]{:S(2)}) collective-permute-start(f32[8,128]{1,0:T(8,128)S(1)} %add.16), channel_id=1, source_target_pairs={{0,2},{1,3},{2,0},{3,1},{4,6},{5,7},{6,4},{7,5},{8,10},{9,11},{10,... | collective-permute-start | bytes 12296 | tf_op jit(solution)/shard_map/ppermute | solution.py:29
  97.8 3.6 %collective-permute-start.14 = (f32[8,128]{1,0:T(8,128)S(1)}, f32[8,128]{1,0:T(8,128)S(1)}, u32[]{:S(2)}, u32[]{:S(2)}) collective-permute-start(f32[8,128]{1,0:T(8,128)S(1)} %add.16), channel_id=1, source_target_pairs={{0,1},{1,0},{2,3},{3,2},{4,5},{5,4},{6,7},{7,6},{8,9},{9,8},{10,11... | collective-permute-start | bytes 12296 | tf_op jit(solution)/shard_map/ppermute | solution.py:29

commit v5 on v3

--- a/solution.py
+++ b/solution.py
@@ -300,7 +300,7 @@
             out[blocks + block] = low.astype(BF16)
 
 
-def own_products_kernel(table_ref, tiles_ref, pushed_ref, scaled_ref, kept, forward_ref, window, forward):
+def own_products_kernel(table_ref, tiles_ref, inverse_ref, root_ref, pushed_ref, scaled_ref, base_ref, window, forward):
     blocks = pushed_ref.shape[0]
     window[...] = jnp.zeros_like(window)
     forward[...] = jnp.zeros_like(forward)
@@ -315,14 +315,17 @@
         forward[jnp.where(dead, blocks, block)] += lax.dot_general(left, matrix, LAST_DIMS, preferred_element_type=F32)
 
     for_tiles(table_ref, True, visit)
-    kept[...] = window[0:blocks]
-    forward_ref[...] = forward[0:blocks]
-
-
-def embed_kernel(table_ref, tiles_ref, inverse_ref, root_ref, kept, forward_ref, odd, even, out_ref, gram_ref, forward):
-    blocks, chans, width = forward_ref.shape
-    forward[0:blocks] = forward_ref[...]
-    forward[blocks] = jnp.zeros((chans, width), F32)
+    root = root_ref[...]
+    inverse_root = 1.0 / root
+    gain = root * inverse_ref[...]
+    for block in range(blocks):
+        line = slice(block, block + 1)
+        base_ref[block] = 0.5 * (forward[block] * gain[line] + window[block] * inverse_root[line])
+
+
+def embed_kernel(table_ref, tiles_ref, inverse_ref, root_ref, base_ref, odd, even, out_ref, gram_ref, forward):
+    blocks, chans, width = base_ref.shape
+    forward[...] = jnp.zeros_like(forward)
 
     def visit(tile, target):
         dead = target == DEAD
@@ -338,10 +341,10 @@
     gain = root * inverse_ref[...]
     gram = jnp.zeros((chans, chans), F32)
     for block in range(blocks):
-        landing = kept[block]
-        for message in (odd, even):
-            landing = landing + (message[block].astype(F32) + message[blocks + block].astype(F32))
-        embedded = 0.5 * (forward[block] * gain[block : block + 1] + landing * inverse_root[block : block + 1])
+        landing = odd[block].astype(F32) + odd[blocks + block].astype(F32)
+        landing = landing + (even[block].astype(F32) + even[blocks + block].astype(F32))
+        arrived = forward[block] * gain[block : block + 1] + landing * inverse_root[block : block + 1]
+        embedded = base_ref[block] + 0.5 * arrived
         out_ref[:, block * width : (block + 1) * width] = embedded
         gram += lax.dot_general(embedded, embedded, LAST_DIMS, precision=HIGHEST, preferred_element_type=F32)
     gram_ref[...] = jnp.concatenate([gram[8 * i : 8 * i + 8] for i in range(4)], axis=1)
@@ -458,14 +461,14 @@
         (table, tiles, inverse, scales, odd, own, even, probe_block), [SMEM] + [VMEM] * 7, [window(chans)],
     )
     odd, even = ring_pairs(to_odd, to_even)
-    kept, forward = call(
-        own_products_kernel, "own_products", [wide, wide], (table, tiles, pushed, scaled), [SMEM] + [VMEM] * 3,
+    (base,) = call(
+        own_products_kernel, "own_products", [wide], (table, tiles, inverse, root, pushed, scaled), [SMEM] + [VMEM] * 5,
         [window(chans, places=blocks + 1)] * 2, flops=1 << 28, moved=1 << 23,
     )
     embedded, gram = call(
         embed_kernel, "embed",
         [jax.ShapeDtypeStruct((chans, blocks * width), F32), jax.ShapeDtypeStruct((8, 128), F32)],
-        (table, tiles, inverse, root, kept, forward, odd, even), [SMEM] + [VMEM] * 7, [window(chans, places=blocks + 1)],
+        (table, tiles, inverse, root, base, odd, even), [SMEM] + [VMEM] * 6, [window(chans, places=blocks + 1)],
     )
     (basis,) = call(
         basis_kernel, "basis", [pltpu.HBM((chans, blocks * width), F32)], (plane_parts(gram), embedded), [VMEM] * 2,

time: 119 us -> 119 us (level)
  Pallas kernels: 20.4 us -> 23 us
  waiting for transfers between devices: 14.2 us -> 12.2 us
  starting transfers between devices: 47.9 us -> 49.5 us
    pallas_call x15, Pallas kernels: 20.4 us -> 23 us  [call(): pl.pallas_call(kernel, out_shape=outs, in_specs=specs, out_specs=out_spec...]
    ppermute x17, waiting for transfers between devices: 14.2 us -> 12.2 us  [swap(): lax.ppermute(shard, axis, [(i, partner(i) % count) for i in range(count)])]
    ppermute x17, starting transfers between devices: 47.9 us -> 49.5 us  [swap(): lax.ppermute(shard, axis, [(i, partner(i) % count) for i in range(count)])]
  transfers between devices with their start and end apart: 17 -> 17, of which waited for: 12 -> 12; matrix products, arithmetic and copies ran while one was open for 0% -> 0% of each run, Pallas kernels for 5% -> 7%
where the time goes in v5:
time: 119 us
  starting transfers between devices  49.5 us (42%)
  blocking collectives  34.2 us (29%)
  Pallas kernels  23 us (19%)
  waiting for transfers between devices  12.2 us (10%)
    ppermute x17, starting transfers between devices, swap(): lax.ppermute(shard, axis, [(i, partner(i) % count) for i in range(count)])  49.5 us
    all_to_all x2, blocking collectives, gathered(): lax.all_to_all(spread, axis, 0, 0, tiled=True, axis_index_groups=groups)  34.2 us
    pallas_call x15, Pallas kernels, call(): pl.pallas_call(kernel, out_shape=outs, in_specs=specs, out_specs=out_spec...  23 us
    ppermute x17, waiting for transfers between devices, swap(): lax.ppermute(shard, axis, [(i, partner(i) % count) for i in range(count)])  12.2 us
  transfers between devices with their start and end apart: 17, of which 12 were waited for; matrix products, arithmetic and copies ran while one was open for 0% of the time, Pallas kernels for 7%

profile of v5, /device:TPU:2, one launch (start us, length us, event | category | flops | bytes accessed | tf_op | source)
XLA Modules:
  0.0 119.4 jit_solution(11779604132668598372)
XLA Ops:
  0.0 5.7 %load.1 = (bf16[64,256,256]{2,1,0:T(8,128)(2,1)S(1)}, s32[136]{0:T(256)S(4)}, f32[8,256]{1,0:T(8,128)S(1)}, f32[8,256]{1,0:T(8,128)S(1)}, f32[8,256]{1,0:T(8,128)S(1)}, /*index=5*/bf16[8,16,256]{2,1,0:T(8,128)(2,1)S(1)}) custom-call(s32[8,8]{1,0:T(8,128)} %cols_hbm.1, s32[8]{0:T(128)} %count_hbm.1, bf16[8,8,256,256]{3,2,1,0:T(8,128)(2,1)} %tiles_hbm.1, ...), custom_call_target="tpu_custom_call" | custom-call | tf_op jit(solution)/shard_map/load/pallas_call | solution.py:385
  5.7 1.6 %collective-permute-start = (f32[8,256]{1,0:T(8,128)S(1)}, f32[8,256]{1,0:T(8,128)S(1)}, u32[]{:S(2)}, u32[]{:S(2)}) collective-permute-start(f32[8,256]{1,0:T(8,128)S(1)} %get-tuple-element.37), channel_id=1, source_target_pairs={{0,255},{1,2},{2,1},{3,4},{4,3},{5,6},{6,5},{7,8},{8,7},{9,10},{10... | collective-permute-start | bytes 24584 | tf_op jit(solution)/shard_map/ppermute | solution.py:27
  7.3 9.2 %collective-permute-start.1 = (f32[8,256]{1,0:T(8,128)S(1)}, f32[8,256]{1,0:T(8,128)S(1)}, u32[]{:S(2)}, u32[]{:S(2)}) collective-permute-start(f32[8,256]{1,0:T(8,128)S(1)} %get-tuple-element.39), channel_id=1, source_target_pairs={{0,1},{1,0},{2,3},{3,2},{4,5},{5,4},{6,7},{7,6},{8,9},{9,8},{10,11... | collective-permute-start | bytes 24584 | tf_op jit(solution)/shard_map/ppermute | solution.py:27
  16.5 1.1 first_own.1.own
  18.1 0.7 second.1
  18.9 7.2 %collective-permute-start.3 = (f32[16,256]{1,0:T(8,128)S(1)}, f32[16,256]{1,0:T(8,128)S(1)}, u32[]{:S(2)}, u32[]{:S(2)}) collective-permute-start(f32[16,256]{1,0:T(8,128)S(1)} %get-tuple-element.43), channel_id=1, source_target_pairs={{0,1},{1,0},{2,3},{3,2},{4,5},{5,4},{6,7},{7,6},{8,9},{9,8},{10,11... | collective-permute-start | bytes 49160 | tf_op jit(solution)/shard_map/ppermute | solution.py:27
  26.1 1.2 %second_own.1.own = f32[16,256]{1,0:T(8,128)S(1)} custom-call(s32[136]{0:T(256)S(4)} %get-tuple-element.34.table_ref, bf16[64,256,256]{2,1,0:T(8,128)(2,1)S(1)} %get-tuple-element.35.tiles_ref, bf16[8,32,256]{2,1,0:T(8,128)(2,1)S(1)} %get-tuple-element.42.left_ref), custom_call_target="tpu_custom_call" | custom-call | flops 33554432 | bytes 4194304 | tf_op jit(solution)/shard_map/second_own/pallas_call | solution.py:385
  27.8 0.7 third.1
  28.6 7.2 %collective-permute-start.5 = (f32[16,256]{1,0:T(8,128)S(1)}, f32[16,256]{1,0:T(8,128)S(1)}, u32[]{:S(2)}, u32[]{:S(2)}) collective-permute-start(f32[16,256]{1,0:T(8,128)S(1)} %get-tuple-element.47), channel_id=1, source_target_pairs={{0,1},{1,0},{2,3},{3,2},{4,5},{5,4},{6,7},{7,6},{8,9},{9,8},{10,11... | collective-permute-start | bytes 49160 | tf_op jit(solution)/shard_map/ppermute | solution.py:27
  35.8 1.2 %third_own.1.own = f32[16,256]{1,0:T(8,128)S(1)} custom-call(s32[136]{0:T(256)S(4)} %get-tuple-element.34.table_ref, bf16[64,256,256]{2,1,0:T(8,128)(2,1)S(1)} %get-tuple-element.35.tiles_ref, bf16[8,32,256]{2,1,0:T(8,128)(2,1)S(1)} %get-tuple-element.46.left_ref), custom_call_target="tpu_custom_call" | custom-call | flops 33554432 | bytes 4194304 | tf_op jit(solution)/shard_map/third_own/pallas_call | solution.py:385
  37.5 0.6 fourth.1
  38.2 7.1 %collective-permute-start.7 = (f32[8,256]{1,0:T(8,128)S(1)}, f32[8,256]{1,0:T(8,128)S(1)}, u32[]{:S(2)}, u32[]{:S(2)}) collective-permute-start(f32[8,256]{1,0:T(8,128)S(1)} %get-tuple-element.51), channel_id=1, source_target_pairs={{0,1},{1,0},{2,3},{3,2},{4,5},{5,4},{6,7},{7,6},{8,9},{9,8},{10,11... | collective-permute-start | bytes 24584 | tf_op jit(solution)/shard_map/ppermute | solution.py:27
  45.3 1.1 fourth_own.1.own
  47.0 1.1 collective-permute-done.8
  48.2 20.7 %all_to_all.13 = f32[128,1,128]{2,1,0:T(1,128)S(1)} all-to-all(f32[128,1,128]{2,1,0:T(1,128)S(1)} %broadcast_in_dim.4), channel_id=1, replica_groups={{0,1,2,3,8,9,10,11,16,17,18,19,24,25,26,27,32,33,34,35,40,41,42,43,48,4..., dimensions={0} | all-to-all | bytes 131072 | tf_op jit(solution)/shard_map/all_to_all | solution.py:38
  68.9 3.1 %replay.1 = (f32[8,256]{1,0:T(8,128)S(1)}, f32[8,256]{1,0:T(8,128)S(1)}, bf16[8,16,256]{2,1,0:T(8,128)(2,1)S(1)}, f32[8,128]{1,0:T(8,128)S(1)}) custom-call(s32[136]{0:T(256)S(4)} %get-tuple-element.34.table_ref, bf16[64,256,256]{2,1,0:T(8,128)(2,1)S(1)} %get-tuple-element.35.tiles_ref, f32[8,256]{1,0:T(8,128)S(1)} %get-tuple-element.36.inverse_ref, ...), custom_call_target="tpu_custom_call" | custom-call | flops 16777216 | bytes 2097152 | tf_op jit(solution)/shard_map/replay/pallas_call | solution.py:385
  72.1 1.5 %collective-permute-start.10 = (f32[8,256]{1,0:T(8,128)S(1)}, f32[8,256]{1,0:T(8,128)S(1)}, u32[]{:S(2)}, u32[]{:S(2)}) collective-permute-start(f32[8,256]{1,0:T(8,128)S(1)} %get-tuple-element.55), channel_id=1, source_target_pairs={{0,1},{1,0},{2,3},{3,2},{4,5},{5,4},{6,7},{7,6},{8,9},{9,8},{10,11... | collective-permute-start | bytes 24584 | tf_op jit(solution)/shard_map/ppermute | solution.py:27
  73.7 1.1 replay_own.1.own
  74.8 1.0 collective-permute-done.9.odd
  75.9 0.8 transposed.1
  76.7 2.0 %collective-permute-start.11 = (bf16[24,32,256]{2,1,0:T(8,128)(2,1)S(1)}, bf16[24,32,256]{2,1,0:T(8,128)(2,1)S(1)}, u32[]{:S(2)}, u32[]{:S(2)}) collective-permute-start(bf16[24,32,256]{2,1,0:T(8,128)(2,1)S(1)} %get-tuple-element.59), channel_id=1, source_target_pairs={{0,255},{1,2},{2,1},{3,4},{4,3},{5,6},{6,5},{7,8},{8,7},{9,10},{10... | collective-permute-start | bytes 1179656 | tf_op jit(solution)/shard_map/ppermute | solution.py:27
  78.7 5.7 %collective-permute-start.12 = (bf16[24,32,256]{2,1,0:T(8,128)(2,1)S(1)}, bf16[24,32,256]{2,1,0:T(8,128)(2,1)S(1)}, u32[]{:S(2)}, u32[]{:S(2)}) collective-permute-start(bf16[24,32,256]{2,1,0:T(8,128)(2,1)S(1)} %get-tuple-element.60), channel_id=1, source_target_pairs={{0,1},{1,0},{2,3},{3,2},{4,5},{5,4},{6,7},{7,6},{8,9},{9,8},{10,11... | collective-permute-start | bytes 1179656 | tf_op jit(solution)/shard_map/ppermute | solution.py:27
  84.4 2.5 %own_products.1.base_ref = f32[8,32,256]{2,1,0:T(8,128)S(1)} custom-call(s32[136]{0:T(256)S(4)} %get-tuple-element.34.table_ref, bf16[64,256,256]{2,1,0:T(8,128)(2,1)S(1)} %get-tuple-element.35.tiles_ref, f32[8,256]{1,0:T(8,128)S(1)} %get-tuple-element.36.inverse_ref, f32[8,256]{1,0:T(8,128)S(1)} %get-tuple-element.56.root_ref, ...), custom_call_target="tpu_custom_call" | custom-call | flops 268435456 | bytes 8388608 | tf_op jit(solution)/shard_map/own_products/pallas_call | solution.py:385
  87.0 0.8 collective-permute-done.11.odd
  87.8 2.4 %collective-permute-done.12.even = bf16[24,32,256]{2,1,0:T(8,128)(2,1)S(1)} collective-permute-done((bf16[24,32,256]{2,1,0:T(8,128)(2,1)S(1)}, bf16[24,32,256]{2,1,0:T(8,128)(2,1)S(1)}, u32[]{:S(2)}, u32[]{:S(2)}) %collective-permute-start.12) | collective-permute-done | bytes 393248 | tf_op jit(solution)/shard_map/ppermute | solution.py:27
  90.2 1.3 %embed.1 = (f32[32,2048]{1,0:T(8,128)S(1)}, f32[8,128]{1,0:T(8,128)S(1)}) custom-call(s32[136]{0:T(256)S(4)} %get-tuple-element.34.table_ref, bf16[64,256,256]{2,1,0:T(8,128)(2,1)S(1)} %get-tuple-element.35.tiles_ref, f32[8,256]{1,0:T(8,128)S(1)} %get-tuple-element.36.inverse_ref, f32[8,256]{1,0:T(8,128)S(1)} %get-tuple-element.56.root_ref, ...), custom_call_target="tpu_custom_call" | custom-call | tf_op jit(solution)/shard_map/embed/pallas_call | solution.py:385
  91.5 1.2 collective-permute-done.13
  93.3 6.9 %collective-permute-start.15 = (f32[8,128]{1,0:T(8,128)S(1)}, f32[8,128]{1,0:T(8,128)S(1)}, u32[]{:S(2)}, u32[]{:S(2)}) collective-permute-start(f32[8,128]{1,0:T(8,128)S(1)} %add.16), channel_id=1, source_target_pairs={{0,2},{1,3},{2,0},{3,1},{4,6},{5,7},{6,4},{7,5},{8,10},{9,11},{10,... | collective-permute-start | bytes 12296 | tf_op jit(solution)/shard_map/ppermute | solution.py:27
  100.2 1.6 %collective-permute-done.15 = f32[8,128]{1,0:T(8,128)S(1)} collective-permute-done((f32[8,128]{1,0:T(8,128)S(1)}, f32[8,128]{1,0:T(8,128)S(1)}, u32[]{:S(2)}, u32[]{:S(2)}) %collective-permute-start.15) | collective-permute-done | bytes 4128 | tf_op jit(solution)/shard_map/ppermute | solution.py:27
  101.8 2.0 %collective-permute-done.14 = f32[8,128]{1,0:T(8,128)S(1)} collective-permute-done((f32[8,128]{1,0:T(8,128)S(1)}, f32[8,128]{1,0:T(8,128)S(1)}, u32[]{:S(2)}, u32[]{:S(2)}) %collective-permute-start.14) | collective-permute-done | bytes 4128 | tf_op jit(solution)/shard_map/ppermute | solution.py:27
  103.8 13.5 %all_to_all.14.gram_ref = f32[32,8,128]{2,1,0:T(8,128)S(1)} all-to-all(f32[32,8,128]{2,1,0:T(8,128)S(1)} %broadcast_in_dim.5), channel_id=1, replica_groups={{0,8,16,24,32,40,48,56,64,72,80,88,96,104,112,120,128,136,144,152,160,1..., dimensions={0} | all-to-all | bytes 262144 | tf_op jit(solution)/shard_map/all_to_all | solution.py:38
  117.3 1.9 %basis.1 = f32[32,2048]{1,0:T(8,128)} custom-call(f32[32,8,128]{2,1,0:T(8,128)S(1)} %all_to_all.14.gram_ref, f32[32,2048]{1,0:T(8,128)S(1)} %get-tuple-element.62.embedded_ref), custom_call_target="tpu_custom_call" | custom-call | tf_op jit(solution)/shard_map/basis/pallas_call | solution.py:385
  (26 shorter events, 3.3 us)
Async XLA Ops:
  5.7 11.9 %collective-permute-start = (f32[8,256]{1,0:T(8,128)S(1)}, f32[8,256]{1,0:T(8,128)S(1)}, u32[]{:S(2)}, u32[]{:S(2)}) collective-permute-start(f32[8,256]{1,0:T(8,128)S(1)} %get-tuple-element.37), channel_id=1, source_target_pairs={{0,255},{1,2},{2,1},{3,4},{4,3},{5,6},{6,5},{7,8},{8,7},{9,10},{10... | collective-permute-start | bytes 24584 | tf_op jit(solution)/shard_map/ppermute | solution.py:27
  7.3 10.9 %collective-permute-start.1 = (f32[8,256]{1,0:T(8,128)S(1)}, f32[8,256]{1,0:T(8,128)S(1)}, u32[]{:S(2)}, u32[]{:S(2)}) collective-permute-start(f32[8,256]{1,0:T(8,128)S(1)} %get-tuple-element.39), channel_id=1, source_target_pairs={{0,1},{1,0},{2,3},{3,2},{4,5},{5,4},{6,7},{7,6},{8,9},{9,8},{10,11... | collective-permute-start | bytes 24584 | tf_op jit(solution)/shard_map/ppermute | solution.py:27
  18.8 8.5 %collective-permute-start.2 = (f32[16,256]{1,0:T(8,128)S(1)}, f32[16,256]{1,0:T(8,128)S(1)}, u32[]{:S(2)}, u32[]{:S(2)}) collective-permute-start(f32[16,256]{1,0:T(8,128)S(1)} %get-tuple-element.41), channel_id=1, source_target_pairs={{0,255},{1,2},{2,1},{3,4},{4,3},{5,6},{6,5},{7,8},{8,7},{9,10},{10... | collective-permute-start | bytes 49160 | tf_op jit(solution)/shard_map/ppermute | solution.py:27
  18.9 8.9 %collective-permute-start.3 = (f32[16,256]{1,0:T(8,128)S(1)}, f32[16,256]{1,0:T(8,128)S(1)}, u32[]{:S(2)}, u32[]{:S(2)}) collective-permute-start(f32[16,256]{1,0:T(8,128)S(1)} %get-tuple-element.43), channel_id=1, source_target_pairs={{0,1},{1,0},{2,3},{3,2},{4,5},{5,4},{6,7},{7,6},{8,9},{9,8},{10,11... | collective-permute-start | bytes 49160 | tf_op jit(solution)/shard_map/ppermute | solution.py:27
  28.5 8.5 %collective-permute-start.4 = (f32[16,256]{1,0:T(8,128)S(1)}, f32[16,256]{1,0:T(8,128)S(1)}, u32[]{:S(2)}, u32[]{:S(2)}) collective-permute-start(f32[16,256]{1,0:T(8,128)S(1)} %get-tuple-element.45), channel_id=1, source_target_pairs={{0,255},{1,2},{2,1},{3,4},{4,3},{5,6},{6,5},{7,8},{8,7},{9,10},{10... | collective-permute-start | bytes 49160 | tf_op jit(solution)/shard_map/ppermute | solution.py:27
  28.6 8.9 %collective-permute-start.5 = (f32[16,256]{1,0:T(8,128)S(1)}, f32[16,256]{1,0:T(8,128)S(1)}, u32[]{:S(2)}, u32[]{:S(2)}) collective-permute-start(f32[16,256]{1,0:T(8,128)S(1)} %get-tuple-element.47), channel_id=1, source_target_pairs={{0,1},{1,0},{2,3},{3,2},{4,5},{5,4},{6,7},{7,6},{8,9},{9,8},{10,11... | collective-permute-start | bytes 49160 | tf_op jit(solution)/shard_map/ppermute | solution.py:27
  38.1 8.3 %collective-permute-start.6 = (f32[8,256]{1,0:T(8,128)S(1)}, f32[8,256]{1,0:T(8,128)S(1)}, u32[]{:S(2)}, u32[]{:S(2)}) collective-permute-start(f32[8,256]{1,0:T(8,128)S(1)} %get-tuple-element.49), channel_id=1, source_target_pairs={{0,255},{1,2},{2,1},{3,4},{4,3},{5,6},{6,5},{7,8},{8,7},{9,10},{10... | collective-permute-start | bytes 24584 | tf_op jit(solution)/shard_map/ppermute | solution.py:27
  38.2 8.8 %collective-permute-start.7 = (f32[8,256]{1,0:T(8,128)S(1)}, f32[8,256]{1,0:T(8,128)S(1)}, u32[]{:S(2)}, u32[]{:S(2)}) collective-permute-start(f32[8,256]{1,0:T(8,128)S(1)} %get-tuple-element.51), channel_id=1, source_target_pairs={{0,1},{1,0},{2,3},{3,2},{4,5},{5,4},{6,7},{7,6},{8,9},{9,8},{10,11... | collective-permute-start | bytes 24584 | tf_op jit(solution)/shard_map/ppermute | solution.py:27
  47.0 1.1 collective-permute-start.8
  68.9 7.0 %copy-start = (bf16[32,2048]{1,0:T(8,128)(2,1)S(1)}, bf16[32,2048]{1,0:T(8,128)(2,1)}, u32[]{:S(2)}) copy-start(bf16[32,2048]{1,0:T(8,128)(2,1)} %probe_ref.1) | copy-start | bytes 393220
  72.0 3.7 %collective-permute-start.9 = (f32[8,256]{1,0:T(8,128)S(1)}, f32[8,256]{1,0:T(8,128)S(1)}, u32[]{:S(2)}, u32[]{:S(2)}) collective-permute-start(f32[8,256]{1,0:T(8,128)S(1)} %get-tuple-element.53), channel_id=1, source_target_pairs={{0,255},{1,2},{2,1},{3,4},{4,3},{5,6},{6,5},{7,8},{8,7},{9,10},{10... | collective-permute-start | bytes 24584 | tf_op jit(solution)/shard_map/ppermute | solution.py:27
  72.1 3.7 %collective-permute-start.10 = (f32[8,256]{1,0:T(8,128)S(1)}, f32[8,256]{1,0:T(8,128)S(1)}, u32[]{:S(2)}, u32[]{:S(2)}) collective-permute-start(f32[8,256]{1,0:T(8,128)S(1)} %get-tuple-element.55), channel_id=1, source_target_pairs={{0,1},{1,0},{2,3},{3,2},{4,5},{5,4},{6,7},{7,6},{8,9},{9,8},{10,11... | collective-permute-start | bytes 24584 | tf_op jit(solution)/shard_map/ppermute | solution.py:27
  76.7 11.1 %collective-permute-start.11 = (bf16[24,32,256]{2,1,0:T(8,128)(2,1)S(1)}, bf16[24,32,256]{2,1,0:T(8,128)(2,1)S(1)}, u32[]{:S(2)}, u32[]{:S(2)}) collective-permute-start(bf16[24,32,256]{2,1,0:T(8,128)(2,1)S(1)} %get-tuple-element.59), channel_id=1, source_target_pairs={{0,255},{1,2},{2,1},{3,4},{4,3},{5,6},{6,5},{7,8},{8,7},{9,10},{10... | collective-permute-start | bytes 1179656 | tf_op jit(solution)/shard_map/ppermute | solution.py:27
  78.7 11.5 %collective-permute-start.12 = (bf16[24,32,256]{2,1,0:T(8,128)(2,1)S(1)}, bf16[24,32,256]{2,1,0:T(8,128)(2,1)S(1)}, u32[]{:S(2)}, u32[]{:S(2)}) collective-permute-start(bf16[24,32,256]{2,1,0:T(8,128)(2,1)S(1)} %get-tuple-element.60), channel_id=1, source_target_pairs={{0,1},{1,0},{2,3},{3,2},{4,5},{5,4},{6,7},{7,6},{8,9},{9,8},{10,11... | collective-permute-start | bytes 1179656 | tf_op jit(solution)/shard_map/ppermute | solution.py:27
  91.5 1.2 %collective-permute-start.13 = (f32[8,128]{1,0:T(8,128)S(1)}, f32[8,128]{1,0:T(8,128)S(1)}, u32[]{:S(2)}, u32[]{:S(2)}) collective-permute-start(f32[8,128]{1,0:T(8,128)S(1)} %get-tuple-element.61), channel_id=1, source_target_pairs={{0,4},{4,0},{8,12},{12,8},{16,20},{20,16},{24,28},{28,24},{32,36},... | collective-permute-start | bytes 12296 | tf_op jit(solution)/shard_map/ppermute | solution.py:27
  92.7 7.5 %collective-permute-start.16 = (f32[8,128]{1,0:T(8,128)S(1)}, f32[8,128]{1,0:T(8,128)S(1)}, u32[]{:S(2)}, u32[]{:S(2)}) collective-permute-start(f32[8,128]{1,0:T(8,128)S(1)} %add.16), channel_id=1, source_target_pairs={{0,3},{1,2},{2,1},{3,0},{4,7},{5,6},{6,5},{7,4},{8,11},{9,10},{10,... | collective-permute-start | bytes 12296 | tf_op jit(solution)/shard_map/ppermute | solution.py:27
  93.3 8.5 %collective-permute-start.15 = (f32[8,128]{1,0:T(8,128)S(1)}, f32[8,128]{1,0:T(8,128)S(1)}, u32[]{:S(2)}, u32[]{:S(2)}) collective-permute-start(f32[8,128]{1,0:T(8,128)S(1)} %add.16), channel_id=1, source_target_pairs={{0,2},{1,3},{2,0},{3,1},{4,6},{5,7},{6,4},{7,5},{8,10},{9,11},{10,... | collective-permute-start | bytes 12296 | tf_op jit(solution)/shard_map/ppermute | solution.py:27
  100.2 3.6 %collective-permute-start.14 = (f32[8,128]{1,0:T(8,128)S(1)}, f32[8,128]{1,0:T(8,128)S(1)}, u32[]{:S(2)}, u32[]{:S(2)}) collective-permute-start(f32[8,128]{1,0:T(8,128)S(1)} %add.16), channel_id=1, source_target_pairs={{0,1},{1,0},{2,3},{3,2},{4,5},{5,4},{6,7},{7,6},{8,9},{9,8},{10,11... | collective-permute-start | bytes 12296 | tf_op jit(solution)/shard_map/ppermute | solution.py:27
